TPU v7x, 256 devices: a whole 4x4x8 slice. The times are simulated.
256 devices in a mesh: gx: 8 (over x, core), gy: 4 (over z_hi), gz: 8 (over z_lo, y).
Axes of the slice: x: 4, y: 4, z: 8 (z_hi: 4, z_lo: 2; z = z_hi * 2 + z_lo), core: 2. Of those that a mesh axis runs over, the one named last changes fastest.
Arguments:
- features: bfloat16 [16, 8, 16, 2, 49, 128], P('gx', 'gy', 'gz'), may hold values from -6 to 6
- cotangent: bfloat16 [16, 8, 16, 2, 49, 128], P('gx', 'gy', 'gz'), may hold values from -1.5 to 1.5
- counts: int32 [16, 8, 16], P('gx', 'gy', 'gz'), may hold values from 1 to 2, as said below
- sources: int32 [16, 8, 16, 2, 12], P('gx', 'gy', 'gz'), may hold values from 0 to 53, as said below
- wigner: bfloat16 [235, 16, 8, 16, 2, 12], P(None, 'gx', 'gy', 'gz'), may hold values from -2.5 to 2.5
- distance: float32 [16, 8, 16, 2, 12], P('gx', 'gy', 'gz'), may hold values from 1 to 5.5
- direction: float32 [3, 16, 8, 16, 2, 12], P(None, 'gx', 'gy', 'gz'), may hold values from -3 to 3
- weight_zero: bfloat16 [896, 896], replicated, may hold values from -0.1875 to 0.1875
- weight_one: bfloat16 [2, 768, 768], replicated, may hold values from -0.15625 to 0.15625
- weight_two: bfloat16 [2, 640, 640], replicated, may hold values from -0.15625 to 0.15625
- radial_in: float32 [256, 128], replicated, may hold values from -1 to 1
- radial_out: float32 [128, 896], replicated, may hold values from -0.5 to 0.5
Outputs:
- updated: bfloat16 [16, 8, 16, 2, 49, 128], P('gx', 'gy', 'gz')
- grad_features: float32 [16, 8, 16, 2, 49, 128], P('gx', 'gy', 'gz')
- forces: float32 [3, 16, 8, 16, 2], P(None, 'gx', 'gy', 'gz')
Inputs may be any that keep to these rules, and one draw needn't show every extreme that they name: Each cell's atoms fill its first counts slots; some cell holds exactly 2 atoms in every draw. sources = o * 2 + s names slot s, below that cell's count, of the cell displaced by (o // 9 - 1, (o // 3) % 3 - 1, o % 3 - 1) with periodic wrap; the 12 displacements of one slot are distinct; where the displacement is (0, 0, 0), s is another slot of the target's own cell.
All inputs are finite; a program needn't handle non-finite values.
Results may differ from a plain program's by a relative error of at most 0.0075.
Values may be sent and summed in bfloat16 or wider, within the bound.
No kernel may reach another device: no remote copies, remote signals or barrier semaphores. Data moves between devices by JAX's collectives and lax.ppermute only.
A program may use at most 128 MiB of HBM per device.

v0:
```python
import math

import jax
import jax.numpy as jnp
import numpy as np
from jax import lax
from jax.experimental import pallas as pl
from jax.experimental.pallas import tpu as pltpu
from jax.sharding import PartitionSpec as P

LMAX = 6
NB = 256
E = 192
G = 24
CR = 104
cutoff = 6.0
sigma_width = 0.5
bf16 = jnp.bfloat16
f32 = jnp.float32
SCALE = 1.0 / math.sqrt(12.0)

PAIRS = (
    [((0, 2 * q), (0, 2 * q + 1)) for q in range(4)]
    + [((1, l), (-1, l)) for l in range(1, 7)]
    + [((2, l), (-2, l)) for l in range(2, 7)]
)


def rotation_table():
    starts = []
    total = 0
    for degree in range(LMAX + 1):
        starts.append(total)
        total += min(2 * degree + 1, 5) * (2 * degree + 1)
    table = np.zeros((256, 30 * 128), np.float32)
    for q, pair in enumerate(PAIRS):
        for half, (m, degree) in enumerate(pair):
            if degree > LMAX:
                continue
            breadth = 2 * degree + 1
            row = m + min(degree, 2)
            for col in range(breadth):
                for copy in range(2):
                    at = (2 * q + half) * 128 + copy * 64 + degree * degree + col
                    table[starts[degree] + row * breadth + col, at] = 1.0
    return table


def base_table():
    out = np.zeros((64,), np.int32)
    for px in range(4):
        for py in range(4):
            for pz in range(4):
                if px in (0, 3):
                    at = 784 + 392 * 2 + 784 * 2 + (px == 3) * 1568 + (py * 4 + pz) * 98
                elif pz in (0, 3):
                    at = 784 + 392 * 2 + (pz == 3) * 784 + ((px - 1) * 4 + py) * 98
                elif py in (0, 3):
                    at = 784 + (py == 3) * 392 + ((px - 1) * 2 + pz - 1) * 98
                else:
                    at = (((px - 1) * 2 + py - 1) * 2 + pz - 1) * 98
                out[(px * 4 + py) * 4 + pz] = at
    return out


def iota(shape, dim):
    return lax.broadcasted_iota(jnp.int32, shape, dim)


def dot(a, b):
    return lax.dot_general(a, b, (((1,), (0,)), ((), ())), preferred_element_type=f32)


def dot_nt(a, b):
    return lax.dot_general(a, b, (((1,), (1,)), ((), ())), preferred_element_type=f32)


def split2(a):
    hi = a.astype(bf16)
    return hi, (a - hi.astype(f32)).astype(bf16)


def dot3(a, b, op=dot):
    ah, al = split2(a)
    bh, bl = split2(b)
    return op(ah, bh) + (op(ah, bl) + op(al, bh))


def edge_ids():
    e = iota((E, 128), 0)
    cell = (e * 2731) >> 16
    rest = e - 24 * cell
    return cell, rest & 1, rest >> 1


def column(block):
    e = iota((E, 16), 0)
    cell = (e * 2731) >> 16
    rest = e - 24 * cell
    pick = (iota((E, 16), 1) == 2 * cell + (rest & 1)).astype(f32)
    rows = lax.dot_general(
        pick, block, (((1,), (0,)), ((), ())), precision=lax.Precision.HIGHEST, preferred_element_type=f32
    )
    e = iota((E, 12), 0)
    rest = e - 24 * ((e * 2731) >> 16)
    return jnp.sum(jnp.where(iota((E, 12), 1) == (rest >> 1), rows, 0.0), axis=1, keepdims=True)


def occupied_edges(counts_ref):
    cell, slot, _ = edge_ids()
    out = jnp.zeros((E, 128), f32)
    for c in range(8):
        out = jnp.where((cell == c) & (slot < counts_ref[c]), 1.0, out)
    return out


def basis_of(dist):
    centers = iota((E, NB), 1).astype(f32) * (cutoff / (NB - 1))
    offset = dist - centers
    return jnp.exp(-0.5 * (offset / sigma_width) ** 2), offset


def row_masks():
    r = iota((16, 128), 0) & 7
    h = iota((16, 128), 1) >> 6
    return [jnp.where(r == 2 * t + h, 1.0, 0.0).astype(bf16) for t in range(4)]


def lane_masks():
    lane = iota((16, 256), 1) & 7
    return [jnp.where(lane == e, 1.0, 0.0).astype(bf16) for e in range(8)]


def masked(block, mask):
    n, w = block.shape
    return (block.reshape(n // 16, 16, w) * mask[None]).reshape(n, w)


def padded_cell(q, cell):
    o = q >> 1
    dx = (o * 57) >> 9
    r = o - 9 * dx
    dy = (r * 11) >> 5
    dz = r - 3 * dy
    px = (cell >> 2) + dx
    py = ((cell >> 1) & 1) + dy
    pz = (cell & 1) + dz
    return (px * 4 + py) * 4 + pz


def pair_block(a, b):
    return jnp.concatenate([a.reshape(G, 8, 128), b.reshape(G, 8, 128)], axis=1).astype(bf16)


def z_place(m, degree):
    if m == 0:
        return 0, 0, degree * 128
    return abs(m), (0 if m > 0 else E), (degree - abs(m)) * 128


def kernel_a(
    wt_ref, tab_ref, cot_ref, dist_ref, counts_ref, src_ref, rin_ref, rout_ref, w0_ref, w1_ref, w2_ref,
    u_ref, v_ref, z0_ref, z1_ref, z2_ref, gi0_ref, rad_ref, inner_ref, xlo_ref, xhi_ref, mid_ref,
    w0v, w1v, w2v, gr_ref, acc_ref, cs_ref, env_ref, sems,
):
    copies = [
        pltpu.make_async_copy(src, dst, sems.at[i])
        for i, (src, dst) in enumerate(((w0_ref, w0v), (w1_ref, w1v), (w2_ref, w2v)))
    ]
    for c in copies:
        c.start()
    zs = (z0_ref, z1_ref, z2_ref)
    dist = column(dist_ref[...])
    basis, _ = basis_of(dist)
    inner = dot3(basis, rin_ref[...])
    inner_ref[...] = inner
    rad_ref[...] = dot3(inner * jax.nn.sigmoid(inner), rout_ref[...])
    env = 0.5 * (jnp.cos(jnp.broadcast_to(dist, (E, 128)) * (math.pi / cutoff)) + 1.0)
    env_ref[...] = env * (occupied_edges(counts_ref) * SCALE)
    wt = wt_ref[...]
    for q in range(15):
        res = dot(wt, tab_ref[:, 256 * q : 256 * q + 256])
        u_ref[:, 16 * q : 16 * q + 16, :] = pair_block(res[:, :128], res[:, 128:])
    u_ref[:, 240:256, :] = jnp.zeros((G, 16, 128), bf16)

    def turn(g, carry):
        v_ref[g] = u_ref[g].T[:64]
        return carry

    lax.fori_loop(0, G, turn, 0)
    cs_ref[0:784, :] = cot_ref[...].astype(f32)
    cs_ref[784:800, :] = jnp.zeros((16, 128), f32)
    m_rot = jnp.where((iota((16, 128), 0) & 1) == (iota((16, 128), 1) >> 6), 1.0, 0.0).astype(bf16)
    zero8 = jnp.zeros((8, 128), f32)

    def rotate(cp, carry):
        parts = []
        for half in range(2):
            cell = 2 * cp + half
            rhs = jnp.concatenate(
                [
                    cs_ref[pl.ds(98 * cell, 56, 2), :],
                    zero8,
                    cs_ref[pl.ds(98 * cell + 1, 56, 2), :],
                    zero8,
                ],
                axis=0,
            ).astype(bf16)
            for i in range(3):
                g = 3 * cell + i
                res = dot(masked(u_ref[g, 0:240, :], m_rot), rhs)
                scale = env_ref[pl.ds(pl.multiple_of(8 * g, 8), 8), :]
                parts.append(res.reshape(30, 8, 128) * scale[None])
        for j in range(3):
            both = jnp.concatenate([parts[2 * j], parts[2 * j + 1]], axis=1).astype(bf16)
            row = pl.multiple_of(48 * cp + 16 * j, 16)
            for q, pair in enumerate(PAIRS):
                for h, (m, degree) in enumerate(pair):
                    if degree <= LMAX:
                        z, up, col = z_place(m, degree)
                        zs[z][pl.ds(row + up, 16), col : col + 128] = both[2 * q + h]
        return carry

    lax.fori_loop(0, 4, rotate, 0)
    for c in copies:
        c.wait()
    gr_ref[:, 240:256, :] = jnp.zeros((G, 16, 128), bf16)
    z0 = z0_ref[...]
    for q in range(4):
        width = 256 if q < 3 else 128
        at = 256 * q
        gi = dot_nt(z0, w0v[at : at + width, :])
        gi0_ref[:, at : at + width] = gi
        gr = gi * rad_ref[:, at : at + width]
        second = gr[:, 128:] if q < 3 else jnp.zeros((E, 128), f32)
        gr_ref[:, 16 * q : 16 * q + 16, :] = pair_block(gr[:, :128], second)
    for m, wv, first in ((1, w1v, 4), (2, w2v, 10)):
        z = zs[m][...]
        count = 7 - m
        for l0 in range(0, count, 2):
            n = min(2, count - l0)
            a = dot_nt(z, wv[0, 128 * l0 : 128 * (l0 + n), :])
            b = dot_nt(z, wv[1, 128 * l0 : 128 * (l0 + n), :])
            gp = a[:E] + b[E:]
            gn = a[E:] - b[:E]
            for i in range(n):
                q = first + l0 + i
                gr_ref[:, 16 * q : 16 * q + 16, :] = pair_block(
                    gp[:, 128 * i : 128 * i + 128], gn[:, 128 * i : 128 * i + 128]
                )
    acc_ref[...] = jnp.zeros(acc_ref.shape, f32)
    row_ok = iota((56, 128), 0) < 49
    for cell in range(8):
        p = (((cell >> 2) + 1) * 4 + ((cell >> 1) & 1) + 1) * 4 + (cell & 1) + 1
        for s in range(2):
            occ = jnp.where(s < counts_ref[cell], 1.0, 0.0).astype(f32)
            acc_ref[pl.ds(p * CR + s, 56, 2), :] = jnp.where(
                row_ok, cs_ref[pl.ds(98 * cell + s, 56, 2), :] * occ, 0.0
            )
    masks = lane_masks()

    def back(cell, carry):
        for i in range(3):
            g = 3 * cell + i
            v = v_ref[g]
            lhs = jnp.concatenate([masked(v, m) for m in masks], axis=0)
            res = dot(lhs, gr_ref[g])
            for e in range(8):
                q = src_ref[2 * cell + (e & 1), 4 * i + (e >> 1)]
                row = padded_cell(q, cell) * CR + (q & 1)
                acc_ref[pl.ds(row, 56, 2), :] += res[64 * e : 64 * e + 56]
        return carry

    lax.fori_loop(0, 8, back, 0)
    xlo_ref[...] = acc_ref[0 : 16 * CR, :].astype(bf16)
    xhi_ref[...] = acc_ref[48 * CR : 64 * CR, :].astype(bf16)
    mid_ref[...] = acc_ref[16 * CR : 48 * CR, :]


def kernel_b(
    own_ref, ylo_ref, yhi_ref, zlo_ref, zhi_ref, xlo_ref, xhi_ref,
    base_ref, src_ref, counts_ref, srcv_ref, dist_ref, dir_ref,
    u_ref, v_ref, g0_ref, g1_ref, g2_ref, gi0_ref, rad_ref, inner_ref, rin_ref, rout_ref, w0_ref, w1_ref, w2_ref,
    upd_ref, force_ref,
    w0v, w1v, w2v, fs_ref, x0_ref, x1_ref, x2_ref, p0_ref, h_ref, env_ref, us_ref, sems,
):
    copies = [
        pltpu.make_async_copy(src, dst, sems.at[i])
        for i, (src, dst) in enumerate(((w0_ref, w0v), (w1_ref, w1v), (w2_ref, w2v)))
    ]
    for c in copies:
        c.start()
    at = 0
    for piece in (own_ref, ylo_ref, yhi_ref, zlo_ref, zhi_ref, xlo_ref, xhi_ref):
        n = piece.shape[0]
        fs_ref[at : at + n, :] = piece[...].astype(f32)
        at += n
    fs_ref[at : at + 16, :] = jnp.zeros((16, 128), f32)
    xs = (x0_ref, x1_ref, x2_ref)
    gs = (g0_ref, g1_ref, g2_ref)
    masks_r = row_masks()
    zero8 = jnp.zeros((8, 128), f32)

    def rotate(cp, carry):
        parts = []
        for half in range(2):
            cell = 2 * cp + half
            for i in range(3):
                g = 3 * cell + i
                rows = []
                for e in range(8):
                    q = src_ref[2 * cell + (e & 1), 4 * i + (e >> 1)]
                    base = base_ref[padded_cell(q, cell)] + (q & 1)
                    rows += [fs_ref[pl.ds(base, 56, 2), :], zero8]
                rhs = jnp.concatenate(rows, axis=0).astype(bf16)
                u = u_ref[g, 0:240, :]
                lhs = jnp.concatenate([masked(u, m) for m in masks_r], axis=1)
                parts.append(dot(lhs, rhs).reshape(30, 8, 128))
        for j in range(3):
            both = jnp.concatenate([parts[2 * j], parts[2 * j + 1]], axis=1)
            row = pl.multiple_of(48 * cp + 16 * j, 16)
            for q, pair in enumerate(PAIRS):
                for h, (m, degree) in enumerate(pair):
                    if degree > LMAX:
                        continue
                    z, up, col = z_place(m, degree)
                    value = both[2 * q + h]
                    if m == 0:
                        p0_ref[pl.ds(row, 16), col : col + 128] = value
                        value = value * rad_ref[pl.ds(row, 16), col : col + 128]
                    xs[z][pl.ds(row + up, 16), col : col + 128] = value.astype(bf16)
        return carry

    lax.fori_loop(0, 4, rotate, 0)
    for c in copies:
        c.wait()
    h_ref[:, 240:256, :] = jnp.zeros((G, 16, 128), bf16)
    along = jnp.zeros((E, 128), f32)

    def rounded(x):
        return x.astype(bf16).astype(f32)

    x0 = x0_ref[...]
    for q in range(4):
        width = 256 if q < 3 else 128
        at = 256 * q
        hid = rounded(dot(x0, w0v[:, at : at + width]))
        prod = hid * g0_ref[:, at : at + width].astype(f32)
        along = along + prod[:, :128]
        if q < 3:
            along = along + prod[:, 128:]
        second = hid[:, 128:] if q < 3 else jnp.zeros((E, 128), f32)
        h_ref[:, 16 * q : 16 * q + 16, :] = pair_block(hid[:, :128], second)
    for m, wv, first in ((1, w1v, 4), (2, w2v, 10)):
        x = xs[m][...]
        count = 7 - m
        for l0 in range(0, count, 2):
            n = min(2, count - l0)
            a = dot(x, wv[0, :, 128 * l0 : 128 * (l0 + n)])
            b = dot(x, wv[1, :, 128 * l0 : 128 * (l0 + n)])
            hp = rounded(a[:E] - b[E:])
            hn = rounded(b[:E] + a[E:])
            gp = gs[m][0:E, 128 * l0 : 128 * (l0 + n)].astype(f32)
            gn = gs[m][E : 2 * E, 128 * l0 : 128 * (l0 + n)].astype(f32)
            prod = hp * gp + hn * gn
            for i in range(n):
                cut = slice(128 * i, 128 * i + 128)
                along = along + prod[:, cut]
                q = first + l0 + i
                h_ref[:, 16 * q : 16 * q + 16, :] = pair_block(hp[:, cut], hn[:, cut])
    dist = column(dist_ref[...])
    angle = jnp.broadcast_to(dist, (E, 128)) * (math.pi / cutoff)
    env = 0.5 * (jnp.cos(angle) + 1.0)
    env_ref[...] = env
    slope = (-0.5 * math.pi / cutoff) * jnp.sin(angle)
    grad_env = jnp.sum(along, axis=1, keepdims=True) / env
    inner = inner_ref[...]
    grad_act = dot3(gi0_ref[...] * p0_ref[...], rout_ref[...], dot_nt)
    sig = jax.nn.sigmoid(inner)
    grad_inner = grad_act * sig * (1.0 + inner * (1.0 - sig))
    grad_basis = dot3(grad_inner, rin_ref[...], dot_nt)
    basis, offset = basis_of(dist)
    radial_part = jnp.sum(
        grad_basis * basis * (-offset / (sigma_width * sigma_width)), axis=1, keepdims=True
    )
    grad_dist = grad_env * slope + radial_part
    cell, slot, _ = edge_ids()
    q = jnp.broadcast_to(column(srcv_ref[...].astype(f32)), (E, 128)).astype(jnp.int32)
    lane = iota((E, 128), 1)
    from_slot = 2 * padded_cell(q, cell) + (q & 1)
    to_slot = 2 * padded_cell(jnp.full((E, 128), 26, jnp.int32), cell) + slot
    side = jnp.where(lane == from_slot, grad_dist, 0.0) - jnp.where(lane == to_slot, grad_dist, 0.0)
    force_ref[...] = jnp.zeros((8, 128), f32)
    for d in range(3):
        along_d = column(dir_ref[16 * d : 16 * d + 16, :])
        force_ref[d : d + 1, :] = jnp.sum(side * along_d, axis=0, keepdims=True)
    masks = lane_masks()

    def back(cell, carry):
        sums = [jnp.zeros((56, 128), f32), jnp.zeros((56, 128), f32)]
        for i in range(3):
            g = 3 * cell + i
            v = v_ref[g]
            lhs = jnp.concatenate([masked(v, m) for m in masks], axis=0)
            res = dot(lhs, h_ref[g])
            for e in range(8):
                scale = env_ref[pl.ds(8 * g + e, 1), :]
                sums[e & 1] = sums[e & 1] + res[64 * e : 64 * e + 56] * scale
        for s in range(2):
            occ = jnp.where(s < counts_ref[cell], 1.0, 0.0).astype(f32)
            own = fs_ref[pl.ds(98 * cell + s, 56, 2), :]
            us_ref[pl.ds(98 * cell + s, 56, 2), :] = (own + sums[s] * SCALE) * occ
        return carry

    lax.fori_loop(0, 8, back, 0)
    upd_ref[...] = us_ref[0:784, :].astype(bf16)


def fold_x(mid_ref, lo_ref, hi_ref, zlo_ref, zhi_ref, out_ref):
    for px in range(2):
        arrived = lo_ref if px == 0 else hi_ref
        for py in range(0, 4, 2):
            ends = {0: [], 3: []}
            for pj in range(2):
                for pz in range(4):
                    at = ((py + pj) * 4 + pz) * CR
                    both = mid_ref[px * 16 * CR + at : px * 16 * CR + at + CR, :]
                    if pz % 2 == 0:
                        pair = arrived[at : at + 2 * CR, :].astype(f32)
                    both = both + pair[(pz % 2) * CR : (pz % 2) * CR + CR]
                    if pz in ends:
                        ends[pz].append(both)
                    else:
                        to = ((px * 4 + py + pj) * 2 + pz - 1) * CR
                        out_ref[to : to + CR, :] = both
            to = (px * 4 + py) * CR
            zlo_ref[to : to + 2 * CR, :] = jnp.concatenate(ends[0], axis=0).astype(bf16)
            zhi_ref[to : to + 2 * CR, :] = jnp.concatenate(ends[3], axis=0).astype(bf16)


def fold_z(mid_ref, lo_ref, hi_ref, ylo_ref, yhi_ref, out_ref):
    for px in range(2):
        arrived = [[], []]
        for z, ref in enumerate((lo_ref, hi_ref)):
            for py in range(0, 4, 2):
                at = (px * 4 + py) * CR
                pair = ref[at : at + 2 * CR, :].astype(f32)
                arrived[z] += [pair[:CR], pair[CR:]]
        for py in range(4):
            done = []
            for z in range(2):
                at = ((px * 4 + py) * 2 + z) * CR
                done.append(mid_ref[at : at + CR, :] + arrived[z][py])
            if py in (0, 3):
                to = px * 2 * CR
                ref = ylo_ref if py == 0 else yhi_ref
                ref[to : to + 2 * CR, :] = jnp.concatenate(done, axis=0).astype(bf16)
            else:
                to = (px * 2 + py - 1) * 2 * CR
                out_ref[to : to + 2 * CR, :] = jnp.concatenate(done, axis=0)


def fold_y(mid_ref, lo_ref, hi_ref, out_ref):
    for px in range(2):
        for py, ref in enumerate((lo_ref, hi_ref)):
            pair = ref[px * 2 * CR : (px + 1) * 2 * CR, :].astype(f32)
            at = (px * 2 + py) * 2 * CR
            value = mid_ref[at : at + 2 * CR, :] + pair
            for z in range(2):
                to = ((px * 2 + py) * 2 + z) * 98
                out_ref[to : to + 98, :] = value[z * CR : z * CR + 98]


def fold_force(shift, bit, last):
    def kernel(mine_ref, lo_ref, hi_ref, out_ref):
        lane = iota((8, 128), 1)
        at = (lane >> bit) & 3
        lo = pltpu.roll(lo_ref[...], 128 - shift, 1)
        hi = pltpu.roll(hi_ref[...], shift, 1)
        total = mine_ref[...] + jnp.where(at == 1, lo, 0.0) + jnp.where(at == 2, hi, 0.0)
        if last:
            r = iota((128, 16), 0)
            o = iota((128, 16), 1)
            from_lane = ((o >> 3) + 1) * 32 + (((o >> 2) & 1) + 1) * 8 + (((o >> 1) & 1) + 1) * 2 + (o & 1)
            pick = (r == from_lane).astype(f32)
            out_ref[...] = lax.dot_general(
                total, pick, (((1,), (0,)), ((), ())), precision=lax.Precision.HIGHEST, preferred_element_type=f32
            )
        else:
            out_ref[...] = total

    return kernel


VM = pl.BlockSpec(memory_space=pltpu.VMEM)
SM = pl.BlockSpec(memory_space=pltpu.SMEM)
AN = pl.BlockSpec(memory_space=pl.ANY)


def shape(dims, dtype):
    return jax.ShapeDtypeStruct(dims, dtype)


def weights_scratch():
    return [pltpu.VMEM((896, 896), bf16), pltpu.VMEM((2, 768, 768), bf16), pltpu.VMEM((2, 640, 640), bf16)]


def call(kernel, out, specs, scratch, limit, name, cost=None):
    return pl.pallas_call(
        kernel,
        out_shape=out,
        in_specs=specs,
        out_specs=jax.tree.map(lambda _: VM, out),
        scratch_shapes=scratch,
        compiler_params=pltpu.CompilerParams(vmem_limit_bytes=limit),
        name=name,
        cost_estimate=cost,
    )


def run_a(wt, cot, dist, counts, src, rin, rout, w0, w1, w2):
    tab = jnp.asarray(rotation_table(), dtype=bf16)
    out = [
        shape((G, 256, 128), bf16), shape((G, 64, 256), bf16),
        shape((E, 896), bf16), shape((2 * E, 768), bf16), shape((2 * E, 640), bf16),
        shape((E, 896), f32), shape((E, 896), f32), shape((E, 128), f32),
        shape((16 * CR, 128), bf16), shape((16 * CR, 128), bf16), shape((32 * CR, 128), f32),
    ]
    scratch = weights_scratch() + [
        pltpu.VMEM((G, 256, 128), bf16), pltpu.VMEM((64 * CR + 16, 128), f32), pltpu.VMEM((800, 128), f32),
        pltpu.VMEM((E, 128), f32), pltpu.SemaphoreType.DMA((3,)),
    ]
    specs = [VM, VM, VM, VM, SM, SM, VM, VM, AN, AN, AN]
    return call(kernel_a, out, specs, scratch, 48 << 20, "backward_part",
                pl.CostEstimate(flops=2 * 10**10, bytes_accessed=20 << 20, transcendentals=10**5))(
        wt, tab, cot, dist, counts, src, rin, rout, w0, w1, w2
    )


def run_b(pieces, src, counts, dist, direction, saved, rin, rout, w0, w1, w2):
    out = [shape((784, 128), bf16), shape((8, 128), f32)]
    scratch = weights_scratch() + [
        pltpu.VMEM((6272 + 16, 128), f32),
        pltpu.VMEM((E, 896), bf16), pltpu.VMEM((2 * E, 768), bf16), pltpu.VMEM((2 * E, 640), bf16),
        pltpu.VMEM((E, 896), f32), pltpu.VMEM((G, 256, 128), bf16), pltpu.VMEM((E, 128), f32),
        pltpu.VMEM((800, 128), f32), pltpu.SemaphoreType.DMA((3,)),
    ]
    specs = [VM] * 7 + [SM, SM, SM] + [VM] * 13 + [AN] * 3
    return call(kernel_b, out, specs, scratch, 48 << 20, "forward_part",
                pl.CostEstimate(flops=2 * 10**10, bytes_accessed=20 << 20, transcendentals=10**5))(
        *pieces, jnp.asarray(base_table()), src, counts, src, dist, direction, *saved, rin, rout, w0, w1, w2
    )


def shifts(axis):
    n = lax.axis_size(axis)
    up = [(i, (i + 1) % n) for i in range(n)]
    return up, [(t, s) for s, t in up]


def exchange(to_up, to_down, axis):
    up, down = shifts(axis)
    return lax.ppermute(to_up, axis, up), lax.ppermute(to_down, axis, down)


def local(features, cotangent, counts, sources, wigner, distance, direction, w0, w1, w2, rin, rout):
    feats = jnp.transpose(features, (0, 1, 2, 4, 3, 5))
    ylo, yhi = exchange(feats[:, 1:2], feats[:, 0:1], "gy")
    tall = jnp.concatenate([ylo, feats, yhi], axis=1)
    zlo, zhi = exchange(tall[:, :, 1:2], tall[:, :, 0:1], "gz")
    top = jnp.concatenate([zlo[1:2], tall[1:2], zhi[1:2]], axis=2)
    low = jnp.concatenate([zlo[0:1], tall[0:1], zhi[0:1]], axis=2)
    xlo, xhi = exchange(top, low, "gx")
    rows = [p.reshape(-1, 128) for p in (feats, ylo, yhi, zlo, zhi, xlo, xhi)]

    cot = jnp.transpose(cotangent, (0, 1, 2, 4, 3, 5)).reshape(784, 128)
    wt = jnp.transpose(wigner, (1, 2, 3, 5, 4, 0)).reshape(E, -1)
    wt = jnp.pad(wt, ((0, 0), (0, 256 - wt.shape[1])))
    src = sources.reshape(16, 12)
    cnt = counts.reshape(8)
    dist = distance.reshape(16, 12)
    dirs = direction.reshape(48, 12)
    *saved, gxlo, gxhi, mid = run_a(wt, cot, dist, cnt, src, rin, rout, w0, w1, w2)
    updated, force = run_b(rows, src, cnt, dist, dirs, saved, rin, rout, w0, w1, w2)

    lo, hi = exchange(gxhi, gxlo, "gx")
    gzlo, gzhi, mid = call(
        fold_x,
        [shape((8 * CR, 128), bf16), shape((8 * CR, 128), bf16), shape((16 * CR, 128), f32)],
        [VM] * 3, [], 24 << 20, "fold_x",
    )(mid, lo, hi)
    lo, hi = exchange(gzhi, gzlo, "gz")
    gylo, gyhi, mid = call(
        fold_z,
        [shape((4 * CR, 128), bf16), shape((4 * CR, 128), bf16), shape((8 * CR, 128), f32)],
        [VM] * 3, [], 24 << 20, "fold_z",
    )(mid, lo, hi)
    lo, hi = exchange(gyhi, gylo, "gy")
    grads = call(fold_y, shape((784, 128), f32), [VM] * 3, [], 24 << 20, "fold_y")(mid, lo, hi)

    for axis, shift, bit in (("gx", 64, 5), ("gz", 4, 1), ("gy", 16, 3)):
        last = axis == "gy"
        lo, hi = exchange(force, force, axis)
        force = call(
            fold_force(shift, bit, last), shape((8, 16) if last else (8, 128), f32), [VM] * 3, [], 8 << 20,
            "fold_force_" + axis,
        )(force, lo, hi)
    forces = force[:3].reshape(3, 2, 2, 2, 2)

    def back(x):
        return jnp.transpose(x.reshape(2, 2, 2, 49, 2, 128), (0, 1, 2, 4, 3, 5))

    return back(updated), back(grads), forces


def solution(mesh):
    cells = P("gx", "gy", "gz")
    behind = P(None, "gx", "gy", "gz")
    in_specs = (cells, cells, cells, cells, behind, cells, behind, P(), P(), P(), P(), P())
    return jax.shard_map(local, mesh=mesh, in_specs=in_specs, out_specs=(cells, cells, behind), check_vma=False)
```

profile of v0, /device:TPU:32, one launch (start us, length us, event | category | flops | bytes accessed | tf_op | source)
XLA Modules:
  0.0 96.0 jit_solution(5735571145901941227)
XLA Ops:
  0.6 1.1 %fusion.4 = (bf16[2,1,2,49,2,128]{5,4,3,2,1,0:T(2,128)(2,1)S(1)}, bf16[2,1,2,49,2,128]{5,4,3,2,1,0:T(2,128)(2,1)S(1)}) fusion(bf16[2,2,2,49,2,128]{5,4,3,2,1,0:T(2,128)(2,1)} %bitcast.23), kind=kLoop, calls=%fused_computation.7 | loop fusion | bytes 401408 | tf_op jit(solution)/shard_map/slice | solution.py:568
  1.7 5.5 %collective-permute-start.1 = (bf16[2,1,2,49,2,128]{5,4,3,2,1,0:T(2,128)(2,1)S(1)}, bf16[2,1,2,49,2,128]{5,4,3,2,1,0:T(2,128)(2,1)S(1)}, u32[]{:S(2)}, u32[]{:S(2)}) collective-permute-start(bf16[2,1,2,49,2,128]{5,4,3,2,1,0:T(2,128)(2,1)S(1)} %get-tuple-element.55), channel_id=1, source_target_pairs={{8,0},{16,8},{24,16},{0,24},{9,1},{17,9},{25,17},{1,25},{10,2},{18... | collective-permute-start | bytes 301064 | tf_op jit(solution)/shard_map/ppermute | solution.py:563
  7.2 0.8 reshape.62.counts_ref
  8.0 1.0 %reshape.65 = bf16[192,235]{1,0:T(8,128)(2,1)S(1)} reshape(bf16[2,2,2,12,2,235]{5,4,3,2,1,0:T(2,128)(2,1)} %bitcast.40) | data formatting | bytes 180480 | tf_op jit(solution)/shard_map/reshape | solution.py:577
  9.0 1.0 %copy-done.2 = f32[128,896]{1,0:T(8,128)S(1)} copy-done((f32[128,896]{1,0:T(8,128)S(1)}, f32[128,896]{1,0:T(8,128)}, u32[]{:S(2)}) %copy-start.2) | copy-done | bytes 458776
  10.0 0.9 copy-done.4
  10.9 0.9 copy-done.5
  11.8 0.7 copy-done.8
  12.5 0.7 copy-done.10
  13.2 14.2 %backward_part.1 = (bf16[24,256,128]{2,1,0:T(8,128)(2,1)}, bf16[24,64,256]{2,1,0:T(8,128)(2,1)S(1)}, bf16[192,896]{1,0:T(8,128)(2,1)S(1)}, bf16[384,768]{1,0:T(8...) custom-call(bf16[192,256]{1,0:T(8,128)(2,1)S(1)} %pad.4.wt_ref, ...), custom_call_target="tpu_custom_call" | custom-call | flops 20000000000 | bytes 20971520 | tf_op jit(solution)/shard_map/backward_part/pallas_call | solution.py:534
  27.4 0.0 collective-permute-start.6
  27.5 2.9 %collective-permute-start.7 = (bf16[1664,128]{1,0:T(8,128)(2,1)S(1)}, bf16[1664,128]{1,0:T(8,128)(2,1)S(1)}, u32[]{:S(2)}, u32[]{:S(2)}) collective-permute-start(bf16[1664,128]{1,0:T(8,128)(2,1)S(1)} %get-tuple-element.33), channel_id=1, source_target_pairs={{32,0},{64,32},{96,64},{128,96},{160,128},{192,160},{224,192},{0,2... | collective-permute-start | bytes 1277960 | tf_op jit(solution)/shard_map/ppermute | solution.py:563
  30.4 0.6 pad_maximum_fusion
  31.0 0.3 fusion.1
  31.3 3.5 %collective-permute-start.3 = (bf16[2,4,1,49,2,128]{5,4,3,2,1,0:T(2,128)(2,1)S(1)}, bf16[2,4,1,49,2,128]{5,4,3,2,1,0:T(2,128)(2,1)S(1)}, u32[]{:S(2)}, u32[]{:S(2)}) collective-permute-start(bf16[2,4,1,49,2,128]{5,4,3,2,1,0:T(2,128)(2,1)S(1)} %get-tuple-element.49), channel_id=1, source_target_pairs={{1,0},{2,1},{3,2},{4,3},{5,4},{6,5},{7,6},{0,7},{9,8},{10,9},{11,1... | collective-permute-start | bytes 602120 | tf_op jit(solution)/shard_map/ppermute | solution.py:563
  34.9 0.3 fusion
  35.1 2.9 %collective-permute-done.3 = bf16[2,4,1,49,2,128]{5,4,3,2,1,0:T(2,128)(2,1)S(1)} collective-permute-done((bf16[2,4,1,49,2,128]{5,4,3,2,1,0:T(2,128)(2,1)S(1)}, bf16[2,4,1,49,2,128]{5,4,3,2,1,0:T(2,128)(2,1)S(1)}, u32[]{:S(2)}, u32[]{:S(2)}) %collective-permute-start.3) | collective-permute-done | bytes 200736 | tf_op jit(solution)/shard_map/ppermute | solution.py:563
  38.1 0.1 fusion.3
  38.2 4.4 %collective-permute-done.2 = bf16[2,4,1,49,2,128]{5,4,3,2,1,0:T(2,128)(2,1)S(1)} collective-permute-done((bf16[2,4,1,49,2,128]{5,4,3,2,1,0:T(2,128)(2,1)S(1)}, bf16[2,4,1,49,2,128]{5,4,3,2,1,0:T(2,128)(2,1)S(1)}, u32[]{:S(2)}, u32[]{:S(2)}) %collective-permute-start.2) | collective-permute-done | bytes 200736 | tf_op jit(solution)/shard_map/ppermute | solution.py:563
  42.7 0.1 fusion.2
  42.8 0.6 pad_maximum_fusion.1
  43.4 0.0 collective-permute-start.4
  43.4 0.6 pad_maximum_fusion.2
  44.0 2.9 %collective-permute-start.5 = (bf16[1,4,4,49,2,128]{5,4,3,2,1,0:T(2,128)(2,1)S(1)}, bf16[1,4,4,49,2,128]{5,4,3,2,1,0:T(2,128)(2,1)S(1)}, u32[]{:S(2)}, u32[]{:S(2)}) collective-permute-start(bf16[1,4,4,49,2,128]{5,4,3,2,1,0:T(2,128)(2,1)S(1)} %pad_maximum_fusion.2), channel_id=1, source_target_pairs={{32,0},{64,32},{96,64},{128,96},{160,128},{192,160},{224,192},{0,2... | collective-permute-start | bytes 1204232 | tf_op jit(solution)/shard_map/ppermute | solution.py:563
  47.0 0.1 fold_x.1
  47.2 0.1 collective-permute-start.8
  47.3 4.1 %collective-permute-start.9 = (bf16[832,128]{1,0:T(8,128)(2,1)S(1)}, bf16[832,128]{1,0:T(8,128)(2,1)S(1)}, u32[]{:S(2)}, u32[]{:S(2)}) collective-permute-start(bf16[832,128]{1,0:T(8,128)(2,1)S(1)} %get-tuple-element.36), channel_id=1, source_target_pairs={{1,0},{2,1},{3,2},{4,3},{5,4},{6,5},{7,6},{0,7},{9,8},{10,9},{11,1... | collective-permute-start | bytes 638984 | tf_op jit(solution)/shard_map/ppermute | solution.py:563
  51.4 3.8 %collective-permute-done.8.lo_ref = bf16[832,128]{1,0:T(8,128)(2,1)S(1)} collective-permute-done((bf16[832,128]{1,0:T(8,128)(2,1)S(1)}, bf16[832,128]{1,0:T(8,128)(2,1)S(1)}, u32[]{:S(2)}, u32[]{:S(2)}) %collective-permute-start.8) | collective-permute-done | bytes 213024 | tf_op jit(solution)/shard_map/ppermute | solution.py:563
  55.2 0.1 fold_z.1
  55.3 1.6 %collective-permute-start.10 = (bf16[416,128]{1,0:T(8,128)(2,1)S(1)}, bf16[416,128]{1,0:T(8,128)(2,1)S(1)}, u32[]{:S(2)}, u32[]{:S(2)}) collective-permute-start(bf16[416,128]{1,0:T(8,128)(2,1)S(1)} %get-tuple-element.38), channel_id=1, source_target_pairs={{0,8},{8,16},{16,24},{24,0},{1,9},{9,17},{17,25},{25,1},{2,10},{10... | collective-permute-start | bytes 319496 | tf_op jit(solution)/shard_map/ppermute | solution.py:563
  56.9 2.7 %collective-permute-start.11 = (bf16[416,128]{1,0:T(8,128)(2,1)S(1)}, bf16[416,128]{1,0:T(8,128)(2,1)S(1)}, u32[]{:S(2)}, u32[]{:S(2)}) collective-permute-start(bf16[416,128]{1,0:T(8,128)(2,1)S(1)} %get-tuple-element.39), channel_id=1, source_target_pairs={{8,0},{16,8},{24,16},{0,24},{9,1},{17,9},{25,17},{1,25},{10,2},{18... | collective-permute-start | bytes 319496 | tf_op jit(solution)/shard_map/ppermute | solution.py:563
  59.7 11.8 %forward_part.1 = (bf16[784,128]{1,0:T(8,128)(2,1)}, f32[8,128]{1,0:T(8,128)S(1)}) custom-call(bf16[784,128]{1,0:T(8,128)(2,1)S(1)} %bitcast.25, bf16[392,128]{1,0:T(8,128)(2,1)S(1)} %bitcast.29, bf16[392,128]{1,0:T(8,128)(2,1)S(1)} %bitcast.28, bf16[784,128]{1,0:T(8,128)(2,1)S(1)} %bitcast.27, bf16[784,128]{1,0:T(8,128)(2,1)S(1)} %bitcast.26, ...), custom_call_target="tpu_custom_call" | custom-call | flops 20000000000 | bytes 20971520 | tf_op jit(solution)/shard_map/forward_part/pallas_call | solution.py:549
  71.5 0.3 collective-permute-start.13
  71.8 0.2 collective-permute-start.12
  72.0 1.1 %collective-permute-done.13.hi_ref = f32[8,128]{1,0:T(8,128)S(1)} collective-permute-done((f32[8,128]{1,0:T(8,128)S(1)}, f32[8,128]{1,0:T(8,128)S(1)}, u32[]{:S(2)}, u32[]{:S(2)}) %collective-permute-start.13) | collective-permute-done | bytes 4128 | tf_op jit(solution)/shard_map/ppermute | solution.py:563
  73.1 2.9 %collective-permute-done.12.lo_ref = f32[8,128]{1,0:T(8,128)S(1)} collective-permute-done((f32[8,128]{1,0:T(8,128)S(1)}, f32[8,128]{1,0:T(8,128)S(1)}, u32[]{:S(2)}, u32[]{:S(2)}) %collective-permute-start.12) | collective-permute-done | bytes 4128 | tf_op jit(solution)/shard_map/ppermute | solution.py:563
  76.0 0.1 fold_force_gx.1.mine_ref
  76.1 3.9 %collective-permute-start.15 = (f32[8,128]{1,0:T(8,128)S(1)}, f32[8,128]{1,0:T(8,128)S(1)}, u32[]{:S(2)}, u32[]{:S(2)}) collective-permute-start(f32[8,128]{1,0:T(8,128)S(1)} %fold_force_gx.1.mine_ref), channel_id=1, source_target_pairs={{1,0},{2,1},{3,2},{4,3},{5,4},{6,5},{7,6},{0,7},{9,8},{10,9},{11,1... | collective-permute-start | bytes 12296 | tf_op jit(solution)/shard_map/ppermute | solution.py:563
  80.0 1.3 %collective-permute-done.15.hi_ref = f32[8,128]{1,0:T(8,128)S(1)} collective-permute-done((f32[8,128]{1,0:T(8,128)S(1)}, f32[8,128]{1,0:T(8,128)S(1)}, u32[]{:S(2)}, u32[]{:S(2)}) %collective-permute-start.15) | collective-permute-done | bytes 4128 | tf_op jit(solution)/shard_map/ppermute | solution.py:563
  81.3 4.4 %collective-permute-done.14.lo_ref = f32[8,128]{1,0:T(8,128)S(1)} collective-permute-done((f32[8,128]{1,0:T(8,128)S(1)}, f32[8,128]{1,0:T(8,128)S(1)}, u32[]{:S(2)}, u32[]{:S(2)}) %collective-permute-start.14) | collective-permute-done | bytes 4128 | tf_op jit(solution)/shard_map/ppermute | solution.py:563
  85.7 0.1 fold_force_gz.1.mine_ref
  85.8 2.8 %collective-permute-start.17 = (f32[8,128]{1,0:T(8,128)S(1)}, f32[8,128]{1,0:T(8,128)S(1)}, u32[]{:S(2)}, u32[]{:S(2)}) collective-permute-start(f32[8,128]{1,0:T(8,128)S(1)} %fold_force_gz.1.mine_ref), channel_id=1, source_target_pairs={{8,0},{16,8},{24,16},{0,24},{9,1},{17,9},{25,17},{1,25},{10,2},{18... | collective-permute-start | bytes 12296 | tf_op jit(solution)/shard_map/ppermute | solution.py:563
  88.6 0.1 collective-permute-start.16
  88.7 1.6 %collective-permute-done.17.hi_ref = f32[8,128]{1,0:T(8,128)S(1)} collective-permute-done((f32[8,128]{1,0:T(8,128)S(1)}, f32[8,128]{1,0:T(8,128)S(1)}, u32[]{:S(2)}, u32[]{:S(2)}) %collective-permute-start.17) | collective-permute-done | bytes 4128 | tf_op jit(solution)/shard_map/ppermute | solution.py:563
  90.3 4.0 %collective-permute-done.16.lo_ref = f32[8,128]{1,0:T(8,128)S(1)} collective-permute-done((f32[8,128]{1,0:T(8,128)S(1)}, f32[8,128]{1,0:T(8,128)S(1)}, u32[]{:S(2)}, u32[]{:S(2)}) %collective-permute-start.16) | collective-permute-done | bytes 4128 | tf_op jit(solution)/shard_map/ppermute | solution.py:563
  94.3 0.2 fold_force_gy.1
  94.5 0.7 copy.19
  95.3 0.8 fold_y.1
  (35 shorter events, 0.1 us)
Async XLA Ops:
  1.7 28.7 %collective-permute-start.1 = (bf16[2,1,2,49,2,128]{5,4,3,2,1,0:T(2,128)(2,1)S(1)}, bf16[2,1,2,49,2,128]{5,4,3,2,1,0:T(2,128)(2,1)S(1)}, u32[]{:S(2)}, u32[]{:S(2)}) collective-permute-start(bf16[2,1,2,49,2,128]{5,4,3,2,1,0:T(2,128)(2,1)S(1)} %get-tuple-element.55), channel_id=1, source_target_pairs={{8,0},{16,8},{24,16},{0,24},{9,1},{17,9},{25,17},{1,25},{10,2},{18... | collective-permute-start | bytes 301064 | tf_op jit(solution)/shard_map/ppermute | solution.py:563
  7.2 23.2 %collective-permute-start = (bf16[2,1,2,49,2,128]{5,4,3,2,1,0:T(2,128)(2,1)S(1)}, bf16[2,1,2,49,2,128]{5,4,3,2,1,0:T(2,128)(2,1)S(1)}, u32[]{:S(2)}, u32[]{:S(2)}) collective-permute-start(bf16[2,1,2,49,2,128]{5,4,3,2,1,0:T(2,128)(2,1)S(1)} %get-tuple-element.56), channel_id=1, source_target_pairs={{0,8},{8,16},{16,24},{24,0},{1,9},{9,17},{17,25},{25,1},{2,10},{10... | collective-permute-start | bytes 301064 | tf_op jit(solution)/shard_map/ppermute | solution.py:563
  9.0 1.0 %copy-start.2 = (f32[128,896]{1,0:T(8,128)S(1)}, f32[128,896]{1,0:T(8,128)}, u32[]{:S(2)}) copy-start(f32[128,896]{1,0:T(8,128)} %rout_ref.3) | copy-start | bytes 1376260
  10.0 0.9 copy-start.4
  10.9 0.9 copy-start.5
  11.8 0.7 copy-start.8
  12.5 0.7 copy-start.10
  13.2 17.2 %copy-start.1 = (bf16[2,2,2,2,49,128]{5,3,4,2,1,0:T(2,128)(2,1)S(1)}, bf16[2,2,2,2,49,128]{5,3,4,2,1,0:T(2,128)(2,1)}, u32[]{:S(2)}) copy-start(bf16[2,2,2,2,49,128]{5,3,4,2,1,0:T(2,128)(2,1)} %param.14) | copy-start | bytes 602116
  27.4 19.5 %collective-permute-start.6 = (bf16[1664,128]{1,0:T(8,128)(2,1)S(1)}, bf16[1664,128]{1,0:T(8,128)(2,1)S(1)}, u32[]{:S(2)}, u32[]{:S(2)}) collective-permute-start(bf16[1664,128]{1,0:T(8,128)(2,1)S(1)} %get-tuple-element.32), channel_id=1, source_target_pairs={{0,32},{32,64},{64,96},{96,128},{128,160},{160,192},{192,224},{224... | collective-permute-start | bytes 1277960 | tf_op jit(solution)/shard_map/ppermute | solution.py:563
  27.5 19.5 %collective-permute-start.7 = (bf16[1664,128]{1,0:T(8,128)(2,1)S(1)}, bf16[1664,128]{1,0:T(8,128)(2,1)S(1)}, u32[]{:S(2)}, u32[]{:S(2)}) collective-permute-start(bf16[1664,128]{1,0:T(8,128)(2,1)S(1)} %get-tuple-element.33), channel_id=1, source_target_pairs={{32,0},{64,32},{96,64},{128,96},{160,128},{192,160},{224,192},{0,2... | collective-permute-start | bytes 1277960 | tf_op jit(solution)/shard_map/ppermute | solution.py:563
  31.3 15.7 %copy-start = (f32[3328,128]{1,0:T(8,128)S(1)}, f32[3328,128]{1,0:T(8,128)}, u32[]{:S(2)}) copy-start(f32[3328,128]{1,0:T(8,128)} %get-tuple-element.31.mid_ref) | copy-start | bytes 5111812
  31.3 6.8 %collective-permute-start.3 = (bf16[2,4,1,49,2,128]{5,4,3,2,1,0:T(2,128)(2,1)S(1)}, bf16[2,4,1,49,2,128]{5,4,3,2,1,0:T(2,128)(2,1)S(1)}, u32[]{:S(2)}, u32[]{:S(2)}) collective-permute-start(bf16[2,4,1,49,2,128]{5,4,3,2,1,0:T(2,128)(2,1)S(1)} %get-tuple-element.49), channel_id=1, source_target_pairs={{1,0},{2,1},{3,2},{4,3},{5,4},{6,5},{7,6},{0,7},{9,8},{10,9},{11,1... | collective-permute-start | bytes 602120 | tf_op jit(solution)/shard_map/ppermute | solution.py:563
  34.8 7.8 %collective-permute-start.2 = (bf16[2,4,1,49,2,128]{5,4,3,2,1,0:T(2,128)(2,1)S(1)}, bf16[2,4,1,49,2,128]{5,4,3,2,1,0:T(2,128)(2,1)S(1)}, u32[]{:S(2)}, u32[]{:S(2)}) collective-permute-start(bf16[2,4,1,49,2,128]{5,4,3,2,1,0:T(2,128)(2,1)S(1)} %get-tuple-element.50), channel_id=1, source_target_pairs={{0,1},{1,2},{2,3},{3,4},{4,5},{5,6},{6,7},{7,0},{8,9},{9,10},{10,1... | collective-permute-start | bytes 602120 | tf_op jit(solution)/shard_map/ppermute | solution.py:563
  43.4 16.2 %collective-permute-start.4 = (bf16[1,4,4,49,2,128]{5,4,3,2,1,0:T(2,128)(2,1)S(1)}, bf16[1,4,4,49,2,128]{5,4,3,2,1,0:T(2,128)(2,1)S(1)}, u32[]{:S(2)}, u32[]{:S(2)}) collective-permute-start(bf16[1,4,4,49,2,128]{5,4,3,2,1,0:T(2,128)(2,1)S(1)} %pad_maximum_fusion.1), channel_id=1, source_target_pairs={{0,32},{32,64},{64,96},{96,128},{128,160},{160,192},{192,224},{224... | collective-permute-start | bytes 1204232 | tf_op jit(solution)/shard_map/ppermute | solution.py:563
  44.0 15.6 %collective-permute-start.5 = (bf16[1,4,4,49,2,128]{5,4,3,2,1,0:T(2,128)(2,1)S(1)}, bf16[1,4,4,49,2,128]{5,4,3,2,1,0:T(2,128)(2,1)S(1)}, u32[]{:S(2)}, u32[]{:S(2)}) collective-permute-start(bf16[1,4,4,49,2,128]{5,4,3,2,1,0:T(2,128)(2,1)S(1)} %pad_maximum_fusion.2), channel_id=1, source_target_pairs={{32,0},{64,32},{96,64},{128,96},{160,128},{192,160},{224,192},{0,2... | collective-permute-start | bytes 1204232 | tf_op jit(solution)/shard_map/ppermute | solution.py:563
  47.0 12.6 %copy-start.3 = (f32[128,896]{1,0:T(8,128)S(1)}, f32[128,896]{1,0:T(8,128)}, u32[]{:S(2)}) copy-start(f32[128,896]{1,0:T(8,128)} %rout_ref.3) | copy-start | bytes 1376260
  47.0 12.6 %copy-start.6 = (f32[256,128]{1,0:T(8,128)S(1)}, f32[256,128]{1,0:T(8,128)}, u32[]{:S(2)}) copy-start(f32[256,128]{1,0:T(8,128)} %rin_ref.3) | copy-start | bytes 393220
  47.0 12.6 %copy-start.7 = (f32[3,2,2,2,2,12]{5,4,3,2,1,0:T(2,128)S(1)}, f32[3,2,2,2,2,12]{5,4,3,2,1,0:T(2,128)}, u32[]{:S(2)}) copy-start(f32[3,2,2,2,2,12]{5,4,3,2,1,0:T(2,128)} %param.20) | copy-start | bytes 6916
  47.0 12.6 %copy-start.9 = (s32[2,2,2,2,12]{4,3,2,1,0:T(2,128)S(1)}, s32[2,2,2,2,12]{4,3,2,1,0:T(2,128)}, u32[]{:S(2)}) copy-start(s32[2,2,2,2,12]{4,3,2,1,0:T(2,128)} %param.17) | copy-start | bytes 2308
  47.0 12.6 %copy-start.11 = (f32[2,2,2,2,12]{4,3,2,1,0:T(2,128)S(1)}, f32[2,2,2,2,12]{4,3,2,1,0:T(2,128)}, u32[]{:S(2)}) copy-start(f32[2,2,2,2,12]{4,3,2,1,0:T(2,128)} %param.19) | copy-start | bytes 2308
  47.0 12.6 %copy-start.12 = (s32[64]{0:T(128)S(1)}, s32[64]{0:T(128)}, u32[]{:S(2)}) copy-start(s32[64]{0:T(128)} %constant.8.clone.base_ref) | copy-start | bytes 772
  47.2 8.0 %collective-permute-start.8 = (bf16[832,128]{1,0:T(8,128)(2,1)S(1)}, bf16[832,128]{1,0:T(8,128)(2,1)S(1)}, u32[]{:S(2)}, u32[]{:S(2)}) collective-permute-start(bf16[832,128]{1,0:T(8,128)(2,1)S(1)} %get-tuple-element.35), channel_id=1, source_target_pairs={{0,1},{1,2},{2,3},{3,4},{4,5},{5,6},{6,7},{7,0},{8,9},{9,10},{10,1... | collective-permute-start | bytes 638984 | tf_op jit(solution)/shard_map/ppermute | solution.py:563
  47.3 7.9 %collective-permute-start.9 = (bf16[832,128]{1,0:T(8,128)(2,1)S(1)}, bf16[832,128]{1,0:T(8,128)(2,1)S(1)}, u32[]{:S(2)}, u32[]{:S(2)}) collective-permute-start(bf16[832,128]{1,0:T(8,128)(2,1)S(1)} %get-tuple-element.36), channel_id=1, source_target_pairs={{1,0},{2,1},{3,2},{4,3},{5,4},{6,5},{7,6},{0,7},{9,8},{10,9},{11,1... | collective-permute-start | bytes 638984 | tf_op jit(solution)/shard_map/ppermute | solution.py:563
  55.3 40.0 %collective-permute-start.10 = (bf16[416,128]{1,0:T(8,128)(2,1)S(1)}, bf16[416,128]{1,0:T(8,128)(2,1)S(1)}, u32[]{:S(2)}, u32[]{:S(2)}) collective-permute-start(bf16[416,128]{1,0:T(8,128)(2,1)S(1)} %get-tuple-element.38), channel_id=1, source_target_pairs={{0,8},{8,16},{16,24},{24,0},{1,9},{9,17},{17,25},{25,1},{2,10},{10... | collective-permute-start | bytes 319496 | tf_op jit(solution)/shard_map/ppermute | solution.py:563
  56.9 38.4 %collective-permute-start.11 = (bf16[416,128]{1,0:T(8,128)(2,1)S(1)}, bf16[416,128]{1,0:T(8,128)(2,1)S(1)}, u32[]{:S(2)}, u32[]{:S(2)}) collective-permute-start(bf16[416,128]{1,0:T(8,128)(2,1)S(1)} %get-tuple-element.39), channel_id=1, source_target_pairs={{8,0},{16,8},{24,16},{0,24},{9,1},{17,9},{25,17},{1,25},{10,2},{18... | collective-permute-start | bytes 319496 | tf_op jit(solution)/shard_map/ppermute | solution.py:563
  71.5 1.7 %collective-permute-start.13 = (f32[8,128]{1,0:T(8,128)S(1)}, f32[8,128]{1,0:T(8,128)S(1)}, u32[]{:S(2)}, u32[]{:S(2)}) collective-permute-start(f32[8,128]{1,0:T(8,128)S(1)} %get-tuple-element.40.mine_ref), channel_id=1, source_target_pairs={{32,0},{64,32},{96,64},{128,96},{160,128},{192,160},{224,192},{0,2... | collective-permute-start | bytes 12296 | tf_op jit(solution)/shard_map/ppermute | solution.py:563
  71.8 4.2 %collective-permute-start.12 = (f32[8,128]{1,0:T(8,128)S(1)}, f32[8,128]{1,0:T(8,128)S(1)}, u32[]{:S(2)}, u32[]{:S(2)}) collective-permute-start(f32[8,128]{1,0:T(8,128)S(1)} %get-tuple-element.40.mine_ref), channel_id=1, source_target_pairs={{0,32},{32,64},{64,96},{96,128},{128,160},{160,192},{192,224},{224... | collective-permute-start | bytes 12296 | tf_op jit(solution)/shard_map/ppermute | solution.py:563
  76.1 5.2 %collective-permute-start.15 = (f32[8,128]{1,0:T(8,128)S(1)}, f32[8,128]{1,0:T(8,128)S(1)}, u32[]{:S(2)}, u32[]{:S(2)}) collective-permute-start(f32[8,128]{1,0:T(8,128)S(1)} %fold_force_gx.1.mine_ref), channel_id=1, source_target_pairs={{1,0},{2,1},{3,2},{4,3},{5,4},{6,5},{7,6},{0,7},{9,8},{10,9},{11,1... | collective-permute-start | bytes 12296 | tf_op jit(solution)/shard_map/ppermute | solution.py:563
  80.0 5.7 %collective-permute-start.14 = (f32[8,128]{1,0:T(8,128)S(1)}, f32[8,128]{1,0:T(8,128)S(1)}, u32[]{:S(2)}, u32[]{:S(2)}) collective-permute-start(f32[8,128]{1,0:T(8,128)S(1)} %fold_force_gx.1.mine_ref), channel_id=1, source_target_pairs={{0,1},{1,2},{2,3},{3,4},{4,5},{5,6},{6,7},{7,0},{8,9},{9,10},{10,1... | collective-permute-start | bytes 12296 | tf_op jit(solution)/shard_map/ppermute | solution.py:563
  85.8 4.5 %collective-permute-start.17 = (f32[8,128]{1,0:T(8,128)S(1)}, f32[8,128]{1,0:T(8,128)S(1)}, u32[]{:S(2)}, u32[]{:S(2)}) collective-permute-start(f32[8,128]{1,0:T(8,128)S(1)} %fold_force_gz.1.mine_ref), channel_id=1, source_target_pairs={{8,0},{16,8},{24,16},{0,24},{9,1},{17,9},{25,17},{1,25},{10,2},{18... | collective-permute-start | bytes 12296 | tf_op jit(solution)/shard_map/ppermute | solution.py:563
  88.6 5.7 %collective-permute-start.16 = (f32[8,128]{1,0:T(8,128)S(1)}, f32[8,128]{1,0:T(8,128)S(1)}, u32[]{:S(2)}, u32[]{:S(2)}) collective-permute-start(f32[8,128]{1,0:T(8,128)S(1)} %fold_force_gz.1.mine_ref), channel_id=1, source_target_pairs={{0,8},{8,16},{16,24},{24,0},{1,9},{9,17},{17,25},{25,1},{2,10},{10... | collective-permute-start | bytes 12296 | tf_op jit(solution)/shard_map/ppermute | solution.py:563
where the time goes:
time: 97.9 us; the launch traced here: 96 us
  starting transfers between devices  30.8 us (31%)
  Pallas kernels  27.4 us (28%)
  waiting for transfers between devices  26.6 us (27%)
  local copies, waits for them, and re-layouts  8.68 us (9%)
  other arithmetic  1.76 us (2%)
    ppermute x18, starting transfers between devices, exchange(): return (lax.ppermute(to_up, axis, up), lax.ppermute(to_down, axis, down))  30.8 us
    ppermute x18, waiting for transfers between devices, exchange(): return (lax.ppermute(to_up, axis, up), lax.ppermute(to_down, axis, down))  26.6 us
    pallas_call x1, Pallas kernels, run_a(): call(kernel_a, out, specs, scratch, 48 << 20, 'backward_part', pl.CostEst...  14.2 us
    pallas_call x1, Pallas kernels, run_b(): call(kernel_b, out, specs, scratch, 48 << 20, 'forward_part', pl.CostEsti...  11.8 us
    unnamed x27, local copies, waits for them, and re-layouts  4.98 us
  transfers between devices with their start and end apart: 18, of which 9 were waited for; matrix products, arithmetic and copies ran while one was open for 5% of the time, Pallas kernels for 28%

commit v1 on v0

--- a/solution.py
+++ b/solution.py
@@ -110,7 +110,7 @@
     cell, slot, _ = edge_ids()
     out = jnp.zeros((E, 128), f32)
     for c in range(8):
-        out = jnp.where((cell == c) & (slot < counts_ref[c]), 1.0, out)
+        out = jnp.where((cell == c) & (slot < counts_ref[c >> 2, (c >> 1) & 1, c & 1]), 1.0, out)
     return out
 
 
@@ -158,25 +158,39 @@
     return abs(m), (0 if m > 0 else E), (degree - abs(m)) * 128
 
 
-def kernel_a(
-    wt_ref, tab_ref, cot_ref, dist_ref, counts_ref, src_ref, rin_ref, rout_ref, w0_ref, w1_ref, w2_ref,
-    u_ref, v_ref, z0_ref, z1_ref, z2_ref, gi0_ref, rad_ref, inner_ref, xlo_ref, xhi_ref, mid_ref,
-    w0v, w1v, w2v, gr_ref, acc_ref, cs_ref, env_ref, sems,
-):
-    copies = [
-        pltpu.make_async_copy(src, dst, sems.at[i])
-        for i, (src, dst) in enumerate(((w0_ref, w0v), (w1_ref, w1v), (w2_ref, w2v)))
-    ]
+def start_copies(pairs, sems):
+    copies = [pltpu.make_async_copy(src, dst, sems.at[i]) for i, (src, dst) in enumerate(pairs)]
     for c in copies:
         c.start()
+    return copies
+
+
+def kernel_a1(
+    wt_ref, tab_ref, cot_ref, dist_ref, counts_ref, srcv_ref, dir_ref, rin_ref, rout_ref,
+    u_ref, v_ref, z0_ref, z1_ref, z2_ref, rad_ref, dsilu_ref, wb_ref, ratio_ref, envo_ref, side_ref, cs_ref,
+    env_ref,
+):
     zs = (z0_ref, z1_ref, z2_ref)
     dist = column(dist_ref[...])
-    basis, _ = basis_of(dist)
+    basis, offset = basis_of(dist)
+    wb_ref[...] = basis * (-offset / (sigma_width * sigma_width))
     inner = dot3(basis, rin_ref[...])
-    inner_ref[...] = inner
-    rad_ref[...] = dot3(inner * jax.nn.sigmoid(inner), rout_ref[...])
-    env = 0.5 * (jnp.cos(jnp.broadcast_to(dist, (E, 128)) * (math.pi / cutoff)) + 1.0)
+    sig = jax.nn.sigmoid(inner)
+    dsilu_ref[...] = sig * (1.0 + inner * (1.0 - sig))
+    rad_ref[...] = dot3(inner * sig, rout_ref[...])
+    angle = jnp.broadcast_to(dist, (E, 128)) * (math.pi / cutoff)
+    env = 0.5 * (jnp.cos(angle) + 1.0)
+    envo_ref[...] = env
+    ratio_ref[...] = (-0.5 * math.pi / cutoff) * jnp.sin(angle) / env
     env_ref[...] = env * (occupied_edges(counts_ref) * SCALE)
+    cell, slot, _ = edge_ids()
+    q = jnp.broadcast_to(column(srcv_ref[...].astype(f32)), (E, 128)).astype(jnp.int32)
+    lane = iota((E, 128), 1)
+    from_slot = 2 * padded_cell(q, cell) + (q & 1)
+    to_slot = 2 * padded_cell(jnp.full((E, 128), 26, jnp.int32), cell) + slot
+    sign = jnp.where(lane == from_slot, 1.0, 0.0) - jnp.where(lane == to_slot, 1.0, 0.0)
+    for d in range(3):
+        side_ref[d] = sign * column(dir_ref[16 * d : 16 * d + 16, :])
     wt = wt_ref[...]
     for q in range(15):
         res = dot(wt, tab_ref[:, 256 * q : 256 * q + 256])
@@ -222,10 +236,14 @@
         return carry
 
     lax.fori_loop(0, 4, rotate, 0)
-    for c in copies:
-        c.wait()
+
+
+def kernel_a2(z0_ref, z1_ref, z2_ref, rad_ref, w0_ref, w1_ref, w2_ref, gi0_ref, gr_ref, w0v, w1v, w2v, sems):
+    copies = start_copies(((w0_ref, w0v), (w1_ref, w1v), (w2_ref, w2v)), sems)
+    zs = (z0_ref, z1_ref, z2_ref)
     gr_ref[:, 240:256, :] = jnp.zeros((G, 16, 128), bf16)
     z0 = z0_ref[...]
+    copies[0].wait()
     for q in range(4):
         width = 256 if q < 3 else 128
         at = 256 * q
@@ -235,6 +253,7 @@
         second = gr[:, 128:] if q < 3 else jnp.zeros((E, 128), f32)
         gr_ref[:, 16 * q : 16 * q + 16, :] = pair_block(gr[:, :128], second)
     for m, wv, first in ((1, w1v, 4), (2, w2v, 10)):
+        copies[m].wait()
         z = zs[m][...]
         count = 7 - m
         for l0 in range(0, count, 2):
@@ -248,12 +267,15 @@
                 gr_ref[:, 16 * q : 16 * q + 16, :] = pair_block(
                     gp[:, 128 * i : 128 * i + 128], gn[:, 128 * i : 128 * i + 128]
                 )
+
+
+def kernel_a3(v_ref, gr_ref, cs_ref, counts_ref, src_ref, xlo_ref, xhi_ref, mid_ref, acc_ref):
     acc_ref[...] = jnp.zeros(acc_ref.shape, f32)
     row_ok = iota((56, 128), 0) < 49
     for cell in range(8):
         p = (((cell >> 2) + 1) * 4 + ((cell >> 1) & 1) + 1) * 4 + (cell & 1) + 1
         for s in range(2):
-            occ = jnp.where(s < counts_ref[cell], 1.0, 0.0).astype(f32)
+            occ = jnp.where(s < counts_ref[cell >> 2, (cell >> 1) & 1, cell & 1], 1.0, 0.0).astype(f32)
             acc_ref[pl.ds(p * CR + s, 56, 2), :] = jnp.where(
                 row_ok, cs_ref[pl.ds(98 * cell + s, 56, 2), :] * occ, 0.0
             )
@@ -277,19 +299,14 @@
     mid_ref[...] = acc_ref[16 * CR : 48 * CR, :]
 
 
-def kernel_b(
-    own_ref, ylo_ref, yhi_ref, zlo_ref, zhi_ref, xlo_ref, xhi_ref,
-    base_ref, src_ref, counts_ref, srcv_ref, dist_ref, dir_ref,
-    u_ref, v_ref, g0_ref, g1_ref, g2_ref, gi0_ref, rad_ref, inner_ref, rin_ref, rout_ref, w0_ref, w1_ref, w2_ref,
-    upd_ref, force_ref,
-    w0v, w1v, w2v, fs_ref, x0_ref, x1_ref, x2_ref, p0_ref, h_ref, env_ref, us_ref, sems,
+def kernel_b1(
+    own_ref, ylo_ref, yhi_ref, zlo_ref, zhi_ref, xlo_ref, xhi_ref, base_ref, src_ref,
+    u_ref, g0_ref, g1_ref, g2_ref, gi0_ref, rad_ref, dsilu_ref, wb_ref, ratio_ref, side_ref, rin_ref, rout_ref,
+    w0_ref, w1_ref, w2_ref,
+    h_ref, force_ref,
+    w0v, w1v, w2v, fs_ref, x0_ref, x1_ref, x2_ref, p0_ref, sems,
 ):
-    copies = [
-        pltpu.make_async_copy(src, dst, sems.at[i])
-        for i, (src, dst) in enumerate(((w0_ref, w0v), (w1_ref, w1v), (w2_ref, w2v)))
-    ]
-    for c in copies:
-        c.start()
+    copies = start_copies(((w0_ref, w0v), (w1_ref, w1v), (w2_ref, w2v)), sems)
     at = 0
     for piece in (own_ref, ylo_ref, yhi_ref, zlo_ref, zhi_ref, xlo_ref, xhi_ref):
         n = piece.shape[0]
@@ -332,14 +349,13 @@
         return carry
 
     lax.fori_loop(0, 4, rotate, 0)
-    for c in copies:
-        c.wait()
     h_ref[:, 240:256, :] = jnp.zeros((G, 16, 128), bf16)
     along = jnp.zeros((E, 128), f32)
 
     def rounded(x):
         return x.astype(bf16).astype(f32)
 
+    copies[0].wait()
     x0 = x0_ref[...]
     for q in range(4):
         width = 256 if q < 3 else 128
@@ -352,6 +368,7 @@
         second = hid[:, 128:] if q < 3 else jnp.zeros((E, 128), f32)
         h_ref[:, 16 * q : 16 * q + 16, :] = pair_block(hid[:, :128], second)
     for m, wv, first in ((1, w1v, 4), (2, w2v, 10)):
+        copies[m].wait()
         x = xs[m][...]
         count = 7 - m
         for l0 in range(0, count, 2):
@@ -368,32 +385,19 @@
                 along = along + prod[:, cut]
                 q = first + l0 + i
                 h_ref[:, 16 * q : 16 * q + 16, :] = pair_block(hp[:, cut], hn[:, cut])
-    dist = column(dist_ref[...])
-    angle = jnp.broadcast_to(dist, (E, 128)) * (math.pi / cutoff)
-    env = 0.5 * (jnp.cos(angle) + 1.0)
-    env_ref[...] = env
-    slope = (-0.5 * math.pi / cutoff) * jnp.sin(angle)
-    grad_env = jnp.sum(along, axis=1, keepdims=True) / env
-    inner = inner_ref[...]
     grad_act = dot3(gi0_ref[...] * p0_ref[...], rout_ref[...], dot_nt)
-    sig = jax.nn.sigmoid(inner)
-    grad_inner = grad_act * sig * (1.0 + inner * (1.0 - sig))
-    grad_basis = dot3(grad_inner, rin_ref[...], dot_nt)
-    basis, offset = basis_of(dist)
-    radial_part = jnp.sum(
-        grad_basis * basis * (-offset / (sigma_width * sigma_width)), axis=1, keepdims=True
-    )
-    grad_dist = grad_env * slope + radial_part
-    cell, slot, _ = edge_ids()
-    q = jnp.broadcast_to(column(srcv_ref[...].astype(f32)), (E, 128)).astype(jnp.int32)
-    lane = iota((E, 128), 1)
-    from_slot = 2 * padded_cell(q, cell) + (q & 1)
-    to_slot = 2 * padded_cell(jnp.full((E, 128), 26, jnp.int32), cell) + slot
-    side = jnp.where(lane == from_slot, grad_dist, 0.0) - jnp.where(lane == to_slot, grad_dist, 0.0)
+    grad_basis = dot3(grad_act * dsilu_ref[...], rin_ref[...], dot_nt)
+    parts = grad_basis * wb_ref[...]
+    total = along * ratio_ref[...] + parts[:, :128] + parts[:, 128:]
+    grad_dist = jnp.sum(total, axis=1, keepdims=True)
     force_ref[...] = jnp.zeros((8, 128), f32)
     for d in range(3):
-        along_d = column(dir_ref[16 * d : 16 * d + 16, :])
-        force_ref[d : d + 1, :] = jnp.sum(side * along_d, axis=0, keepdims=True)
+        force_ref[d : d + 1, :] = jnp.sum(side_ref[d] * grad_dist, axis=0, keepdims=True)
+
+
+def kernel_b2(own_ref, v_ref, h_ref, envo_ref, counts_ref, upd_ref, fs_ref, us_ref):
+    fs_ref[0:784, :] = own_ref[...].astype(f32)
+    fs_ref[784:800, :] = jnp.zeros((16, 128), f32)
     masks = lane_masks()
 
     def back(cell, carry):
@@ -404,10 +408,10 @@
             lhs = jnp.concatenate([masked(v, m) for m in masks], axis=0)
             res = dot(lhs, h_ref[g])
             for e in range(8):
-                scale = env_ref[pl.ds(8 * g + e, 1), :]
+                scale = envo_ref[pl.ds(8 * g + e, 1), :]
                 sums[e & 1] = sums[e & 1] + res[64 * e : 64 * e + 56] * scale
         for s in range(2):
-            occ = jnp.where(s < counts_ref[cell], 1.0, 0.0).astype(f32)
+            occ = jnp.where(s < counts_ref[cell >> 2, (cell >> 1) & 1, cell & 1], 1.0, 0.0).astype(f32)
             own = fs_ref[pl.ds(98 * cell + s, 56, 2), :]
             us_ref[pl.ds(98 * cell + s, 56, 2), :] = (own + sums[s] * SCALE) * occ
         return carry
@@ -479,13 +483,13 @@
         hi = pltpu.roll(hi_ref[...], shift, 1)
         total = mine_ref[...] + jnp.where(at == 1, lo, 0.0) + jnp.where(at == 2, hi, 0.0)
         if last:
-            r = iota((128, 16), 0)
-            o = iota((128, 16), 1)
+            r = iota((16, 128), 1)
+            o = iota((16, 128), 0)
             from_lane = ((o >> 3) + 1) * 32 + (((o >> 2) & 1) + 1) * 8 + (((o >> 1) & 1) + 1) * 2 + (o & 1)
             pick = (r == from_lane).astype(f32)
             out_ref[...] = lax.dot_general(
-                total, pick, (((1,), (0,)), ((), ())), precision=lax.Precision.HIGHEST, preferred_element_type=f32
-            )
+                pick, total, (((1,), (1,)), ((), ())), precision=lax.Precision.HIGHEST, preferred_element_type=f32
+            )[:, :3]
         else:
             out_ref[...] = total
 
@@ -518,37 +522,57 @@
     )
 
 
-def run_a(wt, cot, dist, counts, src, rin, rout, w0, w1, w2):
+def cost(us):
+    return pl.CostEstimate(flops=int(us * 10**9), bytes_accessed=1 << 20, transcendentals=0)
+
+
+def run_a1(wt, cot, dist, counts, src, dirs, rin, rout):
     tab = jnp.asarray(rotation_table(), dtype=bf16)
     out = [
         shape((G, 256, 128), bf16), shape((G, 64, 256), bf16),
         shape((E, 896), bf16), shape((2 * E, 768), bf16), shape((2 * E, 640), bf16),
-        shape((E, 896), f32), shape((E, 896), f32), shape((E, 128), f32),
-        shape((16 * CR, 128), bf16), shape((16 * CR, 128), bf16), shape((32 * CR, 128), f32),
+        shape((E, 896), f32), shape((E, 128), f32), shape((E, NB), f32), shape((E, 128), f32), shape((E, 128), f32),
+        shape((3, E, 128), f32), shape((800, 128), f32),
     ]
-    scratch = weights_scratch() + [
-        pltpu.VMEM((G, 256, 128), bf16), pltpu.VMEM((64 * CR + 16, 128), f32), pltpu.VMEM((800, 128), f32),
-        pltpu.VMEM((E, 128), f32), pltpu.SemaphoreType.DMA((3,)),
-    ]
-    specs = [VM, VM, VM, VM, SM, SM, VM, VM, AN, AN, AN]
-    return call(kernel_a, out, specs, scratch, 48 << 20, "backward_part",
-                pl.CostEstimate(flops=2 * 10**10, bytes_accessed=20 << 20, transcendentals=10**5))(
-        wt, tab, cot, dist, counts, src, rin, rout, w0, w1, w2
+    specs = [VM, VM, VM, VM, SM, VM, VM, VM, VM]
+    return call(kernel_a1, out, specs, [pltpu.VMEM((E, 128), f32)], 24 << 20, "rotations", cost(8))(
+        wt, tab, cot, dist, counts, src, dirs, rin, rout
     )
 
 
-def run_b(pieces, src, counts, dist, direction, saved, rin, rout, w0, w1, w2):
-    out = [shape((784, 128), bf16), shape((8, 128), f32)]
+def run_a2(z0, z1, z2, rad, w0, w1, w2):
+    out = [shape((E, 896), f32), shape((G, 256, 128), bf16)]
+    scratch = weights_scratch() + [pltpu.SemaphoreType.DMA((3,))]
+    return call(kernel_a2, out, [VM] * 4 + [AN] * 3, scratch, 24 << 20, "mix_backward", cost(5))(
+        z0, z1, z2, rad, w0, w1, w2
+    )
+
+
+def run_a3(v, gr, cs, counts, src):
+    out = [shape((16 * CR, 128), bf16), shape((16 * CR, 128), bf16), shape((32 * CR, 128), f32)]
+    scratch = [pltpu.VMEM((64 * CR + 16, 128), f32)]
+    return call(kernel_a3, out, [VM, VM, VM, SM, SM], scratch, 20 << 20, "source_gradients", cost(4))(
+        v, gr, cs, counts, src
+    )
+
+
+def run_b1(pieces, src, saved, rin, rout, w0, w1, w2):
+    out = [shape((G, 256, 128), bf16), shape((8, 128), f32)]
     scratch = weights_scratch() + [
         pltpu.VMEM((6272 + 16, 128), f32),
         pltpu.VMEM((E, 896), bf16), pltpu.VMEM((2 * E, 768), bf16), pltpu.VMEM((2 * E, 640), bf16),
-        pltpu.VMEM((E, 896), f32), pltpu.VMEM((G, 256, 128), bf16), pltpu.VMEM((E, 128), f32),
-        pltpu.VMEM((800, 128), f32), pltpu.SemaphoreType.DMA((3,)),
+        pltpu.VMEM((E, 896), f32), pltpu.SemaphoreType.DMA((3,)),
     ]
-    specs = [VM] * 7 + [SM, SM, SM] + [VM] * 13 + [AN] * 3
-    return call(kernel_b, out, specs, scratch, 48 << 20, "forward_part",
-                pl.CostEstimate(flops=2 * 10**10, bytes_accessed=20 << 20, transcendentals=10**5))(
-        *pieces, jnp.asarray(base_table()), src, counts, src, dist, direction, *saved, rin, rout, w0, w1, w2
+    specs = [VM] * 7 + [SM, SM] + [VM] * 12 + [AN] * 3
+    return call(kernel_b1, out, specs, scratch, 36 << 20, "hidden_and_forces", cost(9))(
+        *pieces, jnp.asarray(base_table()), src, *saved, rin, rout, w0, w1, w2
+    )
+
+
+def run_b2(own, v, h, envo, counts):
+    scratch = [pltpu.VMEM((800, 128), f32), pltpu.VMEM((800, 128), f32)]
+    return call(kernel_b2, shape((784, 128), bf16), [VM] * 4 + [SM], scratch, 16 << 20, "updated", cost(3))(
+        own, v, h, envo, counts
     )
 
 
@@ -563,49 +587,77 @@
     return lax.ppermute(to_up, axis, up), lax.ppermute(to_down, axis, down)
 
 
+def add_force(force, lo, hi, shift, bit, last=False):
+    out = shape((16, 3) if last else (8, 128), f32)
+    return call(fold_force(shift, bit, last), out, [VM] * 3, [], 8 << 20, "fold_force", cost(0.2))(force, lo, hi)
+
+
+def tie(*values):
+    return lax.optimization_barrier(values)
+
+
+def test_run(pieces, wt, cot, src, cnt, dist, dirs, w0, w1, w2, rin, rout):
+    cnt = cnt.reshape(2, 2, 2)
+    u, v, z0, z1, z2, rad, dsilu, wb, ratio, envo, side, cs = run_a1(wt, cot, dist, cnt, src, dirs, rin, rout)
+    gi0, gr = run_a2(z0, z1, z2, rad, w0, w1, w2)
+    gxlo, gxhi, mid = run_a3(v, gr, cs, cnt, src)
+    h, force = run_b1(pieces, src, (u, z0, z1, z2, gi0, rad, dsilu, wb, ratio, side), rin, rout, w0, w1, w2)
+    return run_b2(pieces[0], v, h, envo, cnt), force, gxlo, gxhi, mid
+
+
 def local(features, cotangent, counts, sources, wigner, distance, direction, w0, w1, w2, rin, rout):
-    feats = jnp.transpose(features, (0, 1, 2, 4, 3, 5))
-    ylo, yhi = exchange(feats[:, 1:2], feats[:, 0:1], "gy")
-    tall = jnp.concatenate([ylo, feats, yhi], axis=1)
-    zlo, zhi = exchange(tall[:, :, 1:2], tall[:, :, 0:1], "gz")
-    top = jnp.concatenate([zlo[1:2], tall[1:2], zhi[1:2]], axis=2)
-    low = jnp.concatenate([zlo[0:1], tall[0:1], zhi[0:1]], axis=2)
-    xlo, xhi = exchange(top, low, "gx")
-    rows = [p.reshape(-1, 128) for p in (feats, ylo, yhi, zlo, zhi, xlo, xhi)]
-
     cot = jnp.transpose(cotangent, (0, 1, 2, 4, 3, 5)).reshape(784, 128)
     wt = jnp.transpose(wigner, (1, 2, 3, 5, 4, 0)).reshape(E, -1)
     wt = jnp.pad(wt, ((0, 0), (0, 256 - wt.shape[1])))
     src = sources.reshape(16, 12)
-    cnt = counts.reshape(8)
     dist = distance.reshape(16, 12)
     dirs = direction.reshape(48, 12)
-    *saved, gxlo, gxhi, mid = run_a(wt, cot, dist, cnt, src, rin, rout, w0, w1, w2)
-    updated, force = run_b(rows, src, cnt, dist, dirs, saved, rin, rout, w0, w1, w2)
+    feats = jnp.transpose(features, (0, 1, 2, 4, 3, 5))
+
+    ylo, yhi = exchange(feats[:, 1:2], feats[:, 0:1], "gy")
+    a1 = run_a1(wt, cot, dist, counts, src, dirs, rin, rout)
+    a1, ylo, yhi = tie(a1, ylo, yhi)
+    u, v, z0, z1, z2, rad, dsilu, wb, ratio, envo, side, cs = a1
+    tall = jnp.concatenate([ylo, feats, yhi], axis=1)
+    up, down = tall[:, :, 1:2], tall[:, :, 0:1]
+    (z0, z1, z2, rad), up, down = tie((z0, z1, z2, rad), up, down)
+    zlo, zhi = exchange(up, down, "gz")
+    gi0, gr = run_a2(z0, z1, z2, rad, w0, w1, w2)
+    gr, zlo, zhi = tie(gr, zlo, zhi)
+    top = jnp.concatenate([zlo[1:2], tall[1:2], zhi[1:2]], axis=2)
+    low = jnp.concatenate([zlo[0:1], tall[0:1], zhi[0:1]], axis=2)
+    gr, top, low = tie(gr, top, low)
+    xlo, xhi = exchange(top, low, "gx")
+    gxlo, gxhi, mid = run_a3(v, gr, cs, counts, src)
+    gxlo, gxhi, mid, xlo, xhi = tie(gxlo, gxhi, mid, xlo, xhi)
 
     lo, hi = exchange(gxhi, gxlo, "gx")
+    rows = [p.reshape(-1, 128) for p in (feats, ylo, yhi, zlo, zhi, xlo, xhi)]
+    h, force = run_b1(rows, src, (u, z0, z1, z2, gi0, rad, dsilu, wb, ratio, side), rin, rout, w0, w1, w2)
+    h, force, lo, hi = tie(h, force, lo, hi)
+    flo, fhi = exchange(force, force, "gx")
     gzlo, gzhi, mid = call(
         fold_x,
         [shape((8 * CR, 128), bf16), shape((8 * CR, 128), bf16), shape((16 * CR, 128), f32)],
-        [VM] * 3, [], 24 << 20, "fold_x",
+        [VM] * 3, [], 16 << 20, "fold_x", cost(1),
     )(mid, lo, hi)
     lo, hi = exchange(gzhi, gzlo, "gz")
+    force = add_force(force, flo, fhi, 64, 5)
+    force, h = tie(force, h)
+    flo, fhi = exchange(force, force, "gz")
+    updated = run_b2(rows[0], v, h, envo, counts)
+    updated, flo, fhi = tie(updated, flo, fhi)
+    force = add_force(force, flo, fhi, 4, 1)
+    flo, fhi = exchange(force, force, "gy")
     gylo, gyhi, mid = call(
         fold_z,
         [shape((4 * CR, 128), bf16), shape((4 * CR, 128), bf16), shape((8 * CR, 128), f32)],
-        [VM] * 3, [], 24 << 20, "fold_z",
+        [VM] * 3, [], 16 << 20, "fold_z", cost(1),
     )(mid, lo, hi)
     lo, hi = exchange(gyhi, gylo, "gy")
-    grads = call(fold_y, shape((784, 128), f32), [VM] * 3, [], 24 << 20, "fold_y")(mid, lo, hi)
-
-    for axis, shift, bit in (("gx", 64, 5), ("gz", 4, 1), ("gy", 16, 3)):
-        last = axis == "gy"
-        lo, hi = exchange(force, force, axis)
-        force = call(
-            fold_force(shift, bit, last), shape((8, 16) if last else (8, 128), f32), [VM] * 3, [], 8 << 20,
-            "fold_force_" + axis,
-        )(force, lo, hi)
-    forces = force[:3].reshape(3, 2, 2, 2, 2)
+    force = add_force(force, flo, fhi, 16, 3, True)
+    grads = call(fold_y, shape((784, 128), f32), [VM] * 3, [], 16 << 20, "fold_y", cost(1))(mid, lo, hi)
+    forces = jnp.moveaxis(force.reshape(2, 2, 2, 2, 3), 4, 0)
 
     def back(x):
         return jnp.transpose(x.reshape(2, 2, 2, 49, 2, 128), (0, 1, 2, 4, 3, 5))

time: 97.9 us -> 83.3 us (0.85)
  waiting for transfers between devices: 26.6 us -> 10.9 us
  local copies, waits for them, and re-layouts: 8.68 us -> 10.2 us
  starting transfers between devices: 30.8 us -> 29.7 us
  Pallas kernels: 27.4 us -> 28.4 us
    ppermute x18, waiting for transfers between devices: 26.6 us -> 10.9 us  [exchange(): return (lax.ppermute(to_up, axis, up), lax.ppermute(to_down, axis, down))]
    unnamed x27 -> x34, local copies, waits for them, and re-layouts: 4.98 us -> 7.24 us
    ppermute x18, starting transfers between devices: 30.8 us -> 29.7 us  [exchange(): return (lax.ppermute(to_up, axis, up), lax.ppermute(to_down, axis, down))]
    pallas_call x6 -> x9, Pallas kernels: 27.1 us -> 28.1 us  [the longest x1 7.8 us: run_b1(): call(kernel_b1, out, specs, scratch, 36 << 20, 'hidden_and_forces', cost(9))]
  transfers between devices with their start and end apart: 18 -> 18, of which waited for: 9 -> 6; matrix products, arithmetic and copies ran while one was open for 5% -> 2% of each run, Pallas kernels for 28% -> 33%
where the time goes in v1:
time: 83.3 us; the launch traced here: 81.8 us
  starting transfers between devices  29.7 us (36%)
  Pallas kernels  28.4 us (34%)
  waiting for transfers between devices  10.9 us (13%)
  local copies, waits for them, and re-layouts  10.2 us (12%)
  other arithmetic  1.76 us (2%)
  between operations  0.85 us (1%)
    ppermute x18, starting transfers between devices, exchange(): return (lax.ppermute(to_up, axis, up), lax.ppermute(to_down, axis, down))  29.7 us
    ppermute x18, waiting for transfers between devices, exchange(): return (lax.ppermute(to_up, axis, up), lax.ppermute(to_down, axis, down))  10.9 us
    pallas_call x1, Pallas kernels, run_b1(): call(kernel_b1, out, specs, scratch, 36 << 20, 'hidden_and_forces', cost(9))  7.8 us
    unnamed x34, local copies, waits for them, and re-layouts  7.24 us
    pallas_call x1, Pallas kernels, run_a1(): call(kernel_a1, out, specs, [pltpu.VMEM((E, 128), f32)], 24 << 20, 'rotat...  5.72 us
    pallas_call x1, Pallas kernels, run_a3(): call(kernel_a3, out, [VM, VM, VM, SM, SM], scratch, 20 << 20, 'source_gra...  4.44 us
    pallas_call x1, Pallas kernels, run_b2(): call(kernel_b2, shape((784, 128), bf16), [VM] * 4 + [SM], scratch, 16 <<...  4.34 us
    pallas_call x1, Pallas kernels, run_a2(): call(kernel_a2, out, [VM] * 4 + [AN] * 3, scratch, 24 << 20, 'mix_backwar...  4.06 us
  transfers between devices with their start and end apart: 18, of which 6 were waited for; matrix products, arithmetic and copies ran while one was open for 2% of the time, Pallas kernels for 33%

profile of v1, /device:TPU:32, one launch (start us, length us, event | category | flops | bytes accessed | tf_op | source)
XLA Modules:
  0.0 81.8 jit_solution(7061678521095519954)
XLA Ops:
  0.6 1.1 %fusion.4 = (bf16[2,1,2,49,2,128]{5,4,3,2,1,0:T(2,128)(2,1)S(1)}, bf16[2,1,2,49,2,128]{5,4,3,2,1,0:T(2,128)(2,1)S(1)}) fusion(bf16[2,2,2,49,2,128]{5,4,3,2,1,0:T(2,128)(2,1)} %bitcast.26), kind=kLoop, calls=%fused_computation.7 | loop fusion | bytes 401408 | tf_op jit(solution)/shard_map/slice | solution.py:617
  1.7 5.5 %collective-permute-start.1 = (bf16[2,1,2,49,2,128]{5,4,3,2,1,0:T(2,128)(2,1)S(1)}, bf16[2,1,2,49,2,128]{5,4,3,2,1,0:T(2,128)(2,1)S(1)}, u32[]{:S(2)}, u32[]{:S(2)}) collective-permute-start(bf16[2,1,2,49,2,128]{5,4,3,2,1,0:T(2,128)(2,1)S(1)} %get-tuple-element.147), channel_id=1, source_target_pairs={{8,0},{16,8},{24,16},{0,24},{9,1},{17,9},{25,17},{1,25},{10,2},{18... | collective-permute-start | bytes 301064 | tf_op jit(solution)/shard_map/ppermute | solution.py:587
  7.2 1.0 %reshape.52 = bf16[192,235]{1,0:T(8,128)(2,1)S(1)} reshape(bf16[2,2,2,12,2,235]{5,4,3,2,1,0:T(2,128)(2,1)} %bitcast.42) | data formatting | bytes 180480 | tf_op jit(solution)/shard_map/reshape | solution.py:610
  8.2 1.0 %copy-done.4 = f32[128,896]{1,0:T(8,128)S(1)} copy-done((f32[128,896]{1,0:T(8,128)S(1)}, f32[128,896]{1,0:T(8,128)}, u32[]{:S(2)}) %copy-start.4) | copy-done | bytes 458776
  9.2 0.9 %copy-done.6 = bf16[2,2,2,2,49,128]{5,3,4,2,1,0:T(2,128)(2,1)S(1)} copy-done((bf16[2,2,2,2,49,128]{5,3,4,2,1,0:T(2,128)(2,1)S(1)}, bf16[2,2,2,2,49,128]{5,3,4,2,1,0:T(2,128)(2,1)}, u32[]{:S(2)}) %copy-start.6) | copy-done | bytes 200728
  10.2 0.9 %copy-done.7 = f32[256,128]{1,0:T(8,128)S(1)} copy-done((f32[256,128]{1,0:T(8,128)S(1)}, f32[256,128]{1,0:T(8,128)}, u32[]{:S(2)}) %copy-start.7) | copy-done | bytes 131096
  11.1 0.7 copy-done.9
  11.8 0.7 copy-done.10
  12.5 0.7 copy-done.11
  13.2 0.7 copy-done.13
  13.9 1.5 %copy-done.15 = bf16[256,3840]{1,0:T(8,128)(2,1)S(1)} copy-done((bf16[256,3840]{1,0:T(8,128)(2,1)S(1)}, bf16[256,3840]{1,0:T(8,128)(2,1)}, u32[]{:S(2)}) %copy-start.15) | copy-done | bytes 1966104
  15.4 5.7 %rotations.1 = (bf16[24,256,128]{2,1,0:T(8,128)(2,1)S(1)}, bf16[24,64,256]{2,1,0:T(8,128)(2,1)S(1)}, bf16[192,896]{1,0:T(8,128)(2,1)S(1)}, bf16[384,768]{1,0:T(8...) custom-call(bf16[192,256]{1,0:T(8,128)(2,1)S(1)} %pad.4.wt_ref, ...), custom_call_target="tpu_custom_call" | custom-call | flops 8000000000 | bytes 1048576 | tf_op jit(solution)/shard_map/rotations/pallas_call | solution.py:538
  21.2 0.6 pad_maximum_fusion
  21.8 0.3 fusion.1
  22.1 1.6 %collective-permute-start.2 = (bf16[2,4,1,49,2,128]{5,4,3,2,1,0:T(2,128)(2,1)S(1)}, bf16[2,4,1,49,2,128]{5,4,3,2,1,0:T(2,128)(2,1)S(1)}, u32[]{:S(2)}, u32[]{:S(2)}) collective-permute-start(bf16[2,4,1,49,2,128]{5,4,3,2,1,0:T(2,128)(2,1)S(1)} %get-tuple-element.92), channel_id=1, source_target_pairs={{0,1},{1,2},{2,3},{3,4},{4,5},{5,6},{6,7},{7,0},{8,9},{9,10},{10,1... | collective-permute-start | bytes 602120 | tf_op jit(solution)/shard_map/ppermute | solution.py:587
  23.7 2.6 %collective-permute-start.3 = (bf16[2,4,1,49,2,128]{5,4,3,2,1,0:T(2,128)(2,1)S(1)}, bf16[2,4,1,49,2,128]{5,4,3,2,1,0:T(2,128)(2,1)S(1)}, u32[]{:S(2)}, u32[]{:S(2)}) collective-permute-start(bf16[2,4,1,49,2,128]{5,4,3,2,1,0:T(2,128)(2,1)S(1)} %get-tuple-element.93), channel_id=1, source_target_pairs={{1,0},{2,1},{3,2},{4,3},{5,4},{6,5},{7,6},{0,7},{9,8},{10,9},{11,1... | collective-permute-start | bytes 602120 | tf_op jit(solution)/shard_map/ppermute | solution.py:587
  26.3 4.1 %mix_backward.1 = (f32[192,896]{1,0:T(8,128)S(1)}, bf16[24,256,128]{2,1,0:T(8,128)(2,1)S(1)}) custom-call(bf16[192,896]{1,0:T(8,128)(2,1)S(1)} %get-tuple-element.87.z0_ref.g0_ref, bf16[384,768]{1,0:T(8,128)(2,1)S(1)} %get-tuple-element.88.z1_ref.g1_ref, bf16[384,640]{1,0:T(8,128)(2,1)S(1)} %get-tuple-element.89.z2_ref.g2_ref, ...), custom_call_target="tpu_custom_call" | custom-call | flops 5000000000 | bytes 1048576 | tf_op jit(solution)/shard_map/mix_backward/pallas_call | solution.py:546
  30.4 0.3 fusion
  30.7 0.3 fusion.2
  31.0 0.6 pad_maximum_fusion.2
  31.6 0.6 pad_maximum_fusion.1
  32.3 2.9 %collective-permute-start.5 = (bf16[1,4,4,49,2,128]{5,4,3,2,1,0:T(2,128)(2,1)S(1)}, bf16[1,4,4,49,2,128]{5,4,3,2,1,0:T(2,128)(2,1)S(1)}, u32[]{:S(2)}, u32[]{:S(2)}) collective-permute-start(bf16[1,4,4,49,2,128]{5,4,3,2,1,0:T(2,128)(2,1)S(1)} %pad_maximum_fusion.2), channel_id=1, source_target_pairs={{32,0},{64,32},{96,64},{128,96},{160,128},{192,160},{224,192},{0,2... | collective-permute-start | bytes 1204232 | tf_op jit(solution)/shard_map/ppermute | solution.py:587
  35.2 4.4 %source_gradients.1 = (bf16[1664,128]{1,0:T(8,128)(2,1)S(1)}, bf16[1664,128]{1,0:T(8,128)(2,1)S(1)}, f32[3328,128]{1,0:T(8,128)S(1)}) custom-call(bf16[24,64,256]{2,1,0:T(8,128)(2,1)S(1)} %get-tuple-element.80.v_ref, bf16[24,256,128]{2,1,0:T(8,128)(2,1)S(1)} %get-tuple-element.97.gr_ref, f32[800,128]{1,0:T(8,128)S(1)} %get-tuple-element.98.cs_ref, ...), custom_call_target="tpu_custom_call" | custom-call | flops 4000000000 | bytes 1048576 | tf_op jit(solution)/shard_map/source_gradients/pallas_call | solution.py:554
  39.6 1.1 %collective-permute-done.4 = bf16[1,4,4,49,2,128]{5,4,3,2,1,0:T(2,128)(2,1)S(1)} collective-permute-done((bf16[1,4,4,49,2,128]{5,4,3,2,1,0:T(2,128)(2,1)S(1)}, bf16[1,4,4,49,2,128]{5,4,3,2,1,0:T(2,128)(2,1)S(1)}, u32[]{:S(2)}, u32[]{:S(2)}) %collective-permute-start.4) | collective-permute-done | bytes 401440 | tf_op jit(solution)/shard_map/ppermute | solution.py:587
  40.7 0.4 collective-permute-start.6
  41.1 2.6 %collective-permute-start.7 = (bf16[1664,128]{1,0:T(8,128)(2,1)S(1)}, bf16[1664,128]{1,0:T(8,128)(2,1)S(1)}, u32[]{:S(2)}, u32[]{:S(2)}) collective-permute-start(bf16[1664,128]{1,0:T(8,128)(2,1)S(1)} %get-tuple-element.115), channel_id=1, source_target_pairs={{32,0},{64,32},{96,64},{128,96},{160,128},{192,160},{224,192},{0,2... | collective-permute-start | bytes 1277960 | tf_op jit(solution)/shard_map/ppermute | solution.py:587
  43.7 7.8 %hidden_and_forces.1 = (bf16[24,256,128]{2,1,0:T(8,128)(2,1)S(1)}, f32[8,128]{1,0:T(8,128)S(1)}) custom-call(bf16[784,128]{1,0:T(8,128)(2,1)S(1)} %bitcast.28, bf16[392,128]{1,0:T(8,128)(2,1)S(1)} %bitcast.33, bf16[392,128]{1,0:T(8,128)(2,1)S(1)} %bitcast.32, bf16[784,128]{1,0:T(8,128)(2,1)S(1)} %bitcast.30, bf16[784,128]{1,0:T(8,128)(2,1)S(1)} %bitcast.31, ...), custom_call_target="tpu_custom_call" | custom-call | flops 8999999488 | bytes 1048576 | tf_op jit(solution)/shard_map/hidden_and_forces/pallas_call | solution.py:567
  51.5 0.2 fold_x.1
  51.7 0.8 %collective-permute-start.12 = (bf16[832,128]{1,0:T(8,128)(2,1)S(1)}, bf16[832,128]{1,0:T(8,128)(2,1)S(1)}, u32[]{:S(2)}, u32[]{:S(2)}) collective-permute-start(bf16[832,128]{1,0:T(8,128)(2,1)S(1)} %get-tuple-element.126), channel_id=1, source_target_pairs={{0,1},{1,2},{2,3},{3,4},{4,5},{5,6},{6,7},{7,0},{8,9},{9,10},{10,1... | collective-permute-start | bytes 638984 | tf_op jit(solution)/shard_map/ppermute | solution.py:587
  52.6 3.4 %collective-permute-start.13 = (bf16[832,128]{1,0:T(8,128)(2,1)S(1)}, bf16[832,128]{1,0:T(8,128)(2,1)S(1)}, u32[]{:S(2)}, u32[]{:S(2)}) collective-permute-start(bf16[832,128]{1,0:T(8,128)(2,1)S(1)} %get-tuple-element.127), channel_id=1, source_target_pairs={{1,0},{2,1},{3,2},{4,3},{5,4},{6,5},{7,6},{0,7},{9,8},{10,9},{11,1... | collective-permute-start | bytes 638984 | tf_op jit(solution)/shard_map/ppermute | solution.py:587
  55.9 0.4 collective-permute-start.9
  56.4 0.1 collective-permute-start.8
  56.5 1.3 %collective-permute-done.9.hi_ref = f32[8,128]{1,0:T(8,128)S(1)} collective-permute-done((f32[8,128]{1,0:T(8,128)S(1)}, f32[8,128]{1,0:T(8,128)S(1)}, u32[]{:S(2)}, u32[]{:S(2)}) %collective-permute-start.9) | collective-permute-done | bytes 4128 | tf_op jit(solution)/shard_map/ppermute | solution.py:587
  57.7 2.9 %collective-permute-done.8.lo_ref = f32[8,128]{1,0:T(8,128)S(1)} collective-permute-done((f32[8,128]{1,0:T(8,128)S(1)}, f32[8,128]{1,0:T(8,128)S(1)}, u32[]{:S(2)}, u32[]{:S(2)}) %collective-permute-start.8) | collective-permute-done | bytes 4128 | tf_op jit(solution)/shard_map/ppermute | solution.py:587
  60.6 0.1 fold_force.3.mine_ref
  60.7 1.7 %collective-permute-start.11 = (f32[8,128]{1,0:T(8,128)S(1)}, f32[8,128]{1,0:T(8,128)S(1)}, u32[]{:S(2)}, u32[]{:S(2)}) collective-permute-start(f32[8,128]{1,0:T(8,128)S(1)} %fold_force.3.mine_ref), channel_id=1, source_target_pairs={{1,0},{2,1},{3,2},{4,3},{5,4},{6,5},{7,6},{0,7},{9,8},{10,9},{11,1... | collective-permute-start | bytes 12296 | tf_op jit(solution)/shard_map/ppermute | solution.py:587
  62.4 0.4 collective-permute-start.10
  62.8 0.1 fold_z.1
  62.8 2.2 %collective-permute-start.14 = (bf16[416,128]{1,0:T(8,128)(2,1)S(1)}, bf16[416,128]{1,0:T(8,128)(2,1)S(1)}, u32[]{:S(2)}, u32[]{:S(2)}) collective-permute-start(bf16[416,128]{1,0:T(8,128)(2,1)S(1)} %get-tuple-element.129), channel_id=1, source_target_pairs={{0,8},{8,16},{16,24},{24,0},{1,9},{9,17},{17,25},{25,1},{2,10},{10... | collective-permute-start | bytes 319496 | tf_op jit(solution)/shard_map/ppermute | solution.py:587
  65.0 2.3 %collective-permute-start.15 = (bf16[416,128]{1,0:T(8,128)(2,1)S(1)}, bf16[416,128]{1,0:T(8,128)(2,1)S(1)}, u32[]{:S(2)}, u32[]{:S(2)}) collective-permute-start(bf16[416,128]{1,0:T(8,128)(2,1)S(1)} %get-tuple-element.130), channel_id=1, source_target_pairs={{8,0},{16,8},{24,16},{0,24},{9,1},{17,9},{25,17},{1,25},{10,2},{18... | collective-permute-start | bytes 319496 | tf_op jit(solution)/shard_map/ppermute | solution.py:587
  67.3 4.3 %updated.1 = bf16[784,128]{1,0:T(8,128)(2,1)} custom-call(bf16[784,128]{1,0:T(8,128)(2,1)S(1)} %bitcast.29, bf16[24,64,256]{2,1,0:T(8,128)(2,1)S(1)} %get-tuple-element.80.v_ref, bf16[24,256,128]{2,1,0:T(8,128)(2,1)S(1)} %get-tuple-element.118.h_ref, f32[192,128]{1,0:T(8,128)S(1)} %get-tuple-element.119.envo_ref, s32[2,2,2]{2,1,0:T(2,128)S(1)} %copy-done.14), custom_call_target="tpu_custom_call" | custom-call | flops 3000000000 | bytes 1048576 | tf_op jit(solution)/shard_map/updated/pallas_call | solution.py:574
  71.6 0.1 fold_force.4.mine_ref
  71.7 2.8 %collective-permute-start.17 = (f32[8,128]{1,0:T(8,128)S(1)}, f32[8,128]{1,0:T(8,128)S(1)}, u32[]{:S(2)}, u32[]{:S(2)}) collective-permute-start(f32[8,128]{1,0:T(8,128)S(1)} %fold_force.4.mine_ref), channel_id=1, source_target_pairs={{8,0},{16,8},{24,16},{0,24},{9,1},{17,9},{25,17},{1,25},{10,2},{18... | collective-permute-start | bytes 12296 | tf_op jit(solution)/shard_map/ppermute | solution.py:587
  74.5 0.1 collective-permute-start.16
  74.6 1.6 %collective-permute-done.17.hi_ref = f32[8,128]{1,0:T(8,128)S(1)} collective-permute-done((f32[8,128]{1,0:T(8,128)S(1)}, f32[8,128]{1,0:T(8,128)S(1)}, u32[]{:S(2)}, u32[]{:S(2)}) %collective-permute-start.17) | collective-permute-done | bytes 4128 | tf_op jit(solution)/shard_map/ppermute | solution.py:587
  76.2 4.0 %collective-permute-done.16.lo_ref = f32[8,128]{1,0:T(8,128)S(1)} collective-permute-done((f32[8,128]{1,0:T(8,128)S(1)}, f32[8,128]{1,0:T(8,128)S(1)}, u32[]{:S(2)}, u32[]{:S(2)}) %collective-permute-start.16) | collective-permute-done | bytes 4128 | tf_op jit(solution)/shard_map/ppermute | solution.py:587
  80.2 0.8 fold_force.5
  81.0 0.8 fold_y.1
  (42 shorter events, 0.2 us)
Async XLA Ops:
  1.7 19.5 %collective-permute-start.1 = (bf16[2,1,2,49,2,128]{5,4,3,2,1,0:T(2,128)(2,1)S(1)}, bf16[2,1,2,49,2,128]{5,4,3,2,1,0:T(2,128)(2,1)S(1)}, u32[]{:S(2)}, u32[]{:S(2)}) collective-permute-start(bf16[2,1,2,49,2,128]{5,4,3,2,1,0:T(2,128)(2,1)S(1)} %get-tuple-element.147), channel_id=1, source_target_pairs={{8,0},{16,8},{24,16},{0,24},{9,1},{17,9},{25,17},{1,25},{10,2},{18... | collective-permute-start | bytes 301064 | tf_op jit(solution)/shard_map/ppermute | solution.py:587
  7.2 14.0 %collective-permute-start = (bf16[2,1,2,49,2,128]{5,4,3,2,1,0:T(2,128)(2,1)S(1)}, bf16[2,1,2,49,2,128]{5,4,3,2,1,0:T(2,128)(2,1)S(1)}, u32[]{:S(2)}, u32[]{:S(2)}) collective-permute-start(bf16[2,1,2,49,2,128]{5,4,3,2,1,0:T(2,128)(2,1)S(1)} %get-tuple-element.148), channel_id=1, source_target_pairs={{0,8},{8,16},{16,24},{24,0},{1,9},{9,17},{17,25},{25,1},{2,10},{10... | collective-permute-start | bytes 301064 | tf_op jit(solution)/shard_map/ppermute | solution.py:587
  8.2 1.0 %copy-start.4 = (f32[128,896]{1,0:T(8,128)S(1)}, f32[128,896]{1,0:T(8,128)}, u32[]{:S(2)}) copy-start(f32[128,896]{1,0:T(8,128)} %rout_ref.3) | copy-start | bytes 1376260
  9.2 0.9 %copy-start.6 = (bf16[2,2,2,2,49,128]{5,3,4,2,1,0:T(2,128)(2,1)S(1)}, bf16[2,2,2,2,49,128]{5,3,4,2,1,0:T(2,128)(2,1)}, u32[]{:S(2)}) copy-start(bf16[2,2,2,2,49,128]{5,3,4,2,1,0:T(2,128)(2,1)} %param.15) | copy-start | bytes 602116
  10.2 0.9 %copy-start.7 = (f32[256,128]{1,0:T(8,128)S(1)}, f32[256,128]{1,0:T(8,128)}, u32[]{:S(2)}) copy-start(f32[256,128]{1,0:T(8,128)} %rin_ref.3) | copy-start | bytes 393220
  11.1 0.7 copy-start.9
  11.8 0.7 copy-start.10
  12.5 0.7 copy-start.11
  13.2 0.7 copy-start.13
  13.9 1.5 %copy-start.15 = (bf16[256,3840]{1,0:T(8,128)(2,1)S(1)}, bf16[256,3840]{1,0:T(8,128)(2,1)}, u32[]{:S(2)}) copy-start(bf16[256,3840]{1,0:T(8,128)(2,1)} %constant.7.clone.tab_ref) | copy-start | bytes 5898244
  15.4 5.8 %copy-start = (bf16[2,2,2,2,49,128]{5,3,4,2,1,0:T(2,128)(2,1)S(1)}, bf16[2,2,2,2,49,128]{5,3,4,2,1,0:T(2,128)(2,1)}, u32[]{:S(2)}) copy-start(bf16[2,2,2,2,49,128]{5,3,4,2,1,0:T(2,128)(2,1)} %param.14) | copy-start | bytes 602116
  15.4 10.9 %copy-start.1 = (bf16[2,768,768]{2,1,0:T(8,128)(2,1)S(1)}, bf16[2,768,768]{2,1,0:T(8,128)(2,1)}, u32[]{:S(2)}) copy-start(bf16[2,768,768]{2,1,0:T(8,128)(2,1)} %w1_ref.3) | copy-start | bytes 7077892
  15.4 10.9 %copy-start.2 = (bf16[2,640,640]{2,1,0:T(8,128)(2,1)S(1)}, bf16[2,640,640]{2,1,0:T(8,128)(2,1)}, u32[]{:S(2)}) copy-start(bf16[2,640,640]{2,1,0:T(8,128)(2,1)} %w2_ref.3) | copy-start | bytes 4915204
  15.4 10.9 %copy-start.3 = (bf16[896,896]{1,0:T(8,128)(2,1)S(1)}, bf16[896,896]{1,0:T(8,128)(2,1)}, u32[]{:S(2)}) copy-start(bf16[896,896]{1,0:T(8,128)(2,1)} %w0_ref.3) | copy-start | bytes 4816900
  22.1 8.6 %collective-permute-start.2 = (bf16[2,4,1,49,2,128]{5,4,3,2,1,0:T(2,128)(2,1)S(1)}, bf16[2,4,1,49,2,128]{5,4,3,2,1,0:T(2,128)(2,1)S(1)}, u32[]{:S(2)}, u32[]{:S(2)}) collective-permute-start(bf16[2,4,1,49,2,128]{5,4,3,2,1,0:T(2,128)(2,1)S(1)} %get-tuple-element.92), channel_id=1, source_target_pairs={{0,1},{1,2},{2,3},{3,4},{4,5},{5,6},{6,7},{7,0},{8,9},{9,10},{10,1... | collective-permute-start | bytes 602120 | tf_op jit(solution)/shard_map/ppermute | solution.py:587
  23.7 7.0 %collective-permute-start.3 = (bf16[2,4,1,49,2,128]{5,4,3,2,1,0:T(2,128)(2,1)S(1)}, bf16[2,4,1,49,2,128]{5,4,3,2,1,0:T(2,128)(2,1)S(1)}, u32[]{:S(2)}, u32[]{:S(2)}) collective-permute-start(bf16[2,4,1,49,2,128]{5,4,3,2,1,0:T(2,128)(2,1)S(1)} %get-tuple-element.93), channel_id=1, source_target_pairs={{1,0},{2,1},{3,2},{4,3},{5,4},{6,5},{7,6},{0,7},{9,8},{10,9},{11,1... | collective-permute-start | bytes 602120 | tf_op jit(solution)/shard_map/ppermute | solution.py:587
  32.2 11.5 %copy-start.5 = (f32[128,896]{1,0:T(8,128)S(1)}, f32[128,896]{1,0:T(8,128)}, u32[]{:S(2)}) copy-start(f32[128,896]{1,0:T(8,128)} %rout_ref.3) | copy-start | bytes 1376260
  32.2 11.5 %copy-start.8 = (f32[256,128]{1,0:T(8,128)S(1)}, f32[256,128]{1,0:T(8,128)}, u32[]{:S(2)}) copy-start(f32[256,128]{1,0:T(8,128)} %rin_ref.3) | copy-start | bytes 393220
  32.2 11.5 %copy-start.12 = (s32[2,2,2,2,12]{4,3,2,1,0:T(2,128)S(1)}, s32[2,2,2,2,12]{4,3,2,1,0:T(2,128)}, u32[]{:S(2)}) copy-start(s32[2,2,2,2,12]{4,3,2,1,0:T(2,128)} %param.17) | copy-start | bytes 2308
  32.2 11.5 %copy-start.16 = (s32[64]{0:T(128)S(1)}, s32[64]{0:T(128)}, u32[]{:S(2)}) copy-start(s32[64]{0:T(128)} %constant.8.clone.base_ref) | copy-start | bytes 772
  32.2 8.5 %collective-permute-start.4 = (bf16[1,4,4,49,2,128]{5,4,3,2,1,0:T(2,128)(2,1)S(1)}, bf16[1,4,4,49,2,128]{5,4,3,2,1,0:T(2,128)(2,1)S(1)}, u32[]{:S(2)}, u32[]{:S(2)}) collective-permute-start(bf16[1,4,4,49,2,128]{5,4,3,2,1,0:T(2,128)(2,1)S(1)} %pad_maximum_fusion.1), channel_id=1, source_target_pairs={{0,32},{32,64},{64,96},{96,128},{128,160},{160,192},{192,224},{224... | collective-permute-start | bytes 1204232 | tf_op jit(solution)/shard_map/ppermute | solution.py:587
  32.3 8.5 %collective-permute-start.5 = (bf16[1,4,4,49,2,128]{5,4,3,2,1,0:T(2,128)(2,1)S(1)}, bf16[1,4,4,49,2,128]{5,4,3,2,1,0:T(2,128)(2,1)S(1)}, u32[]{:S(2)}, u32[]{:S(2)}) collective-permute-start(bf16[1,4,4,49,2,128]{5,4,3,2,1,0:T(2,128)(2,1)S(1)} %pad_maximum_fusion.2), channel_id=1, source_target_pairs={{32,0},{64,32},{96,64},{128,96},{160,128},{192,160},{224,192},{0,2... | collective-permute-start | bytes 1204232 | tf_op jit(solution)/shard_map/ppermute | solution.py:587
  40.7 10.8 %collective-permute-start.6 = (bf16[1664,128]{1,0:T(8,128)(2,1)S(1)}, bf16[1664,128]{1,0:T(8,128)(2,1)S(1)}, u32[]{:S(2)}, u32[]{:S(2)}) collective-permute-start(bf16[1664,128]{1,0:T(8,128)(2,1)S(1)} %get-tuple-element.114), channel_id=1, source_target_pairs={{0,32},{32,64},{64,96},{96,128},{128,160},{160,192},{192,224},{224... | collective-permute-start | bytes 1277960 | tf_op jit(solution)/shard_map/ppermute | solution.py:587
  41.1 10.4 %collective-permute-start.7 = (bf16[1664,128]{1,0:T(8,128)(2,1)S(1)}, bf16[1664,128]{1,0:T(8,128)(2,1)S(1)}, u32[]{:S(2)}, u32[]{:S(2)}) collective-permute-start(bf16[1664,128]{1,0:T(8,128)(2,1)S(1)} %get-tuple-element.115), channel_id=1, source_target_pairs={{32,0},{64,32},{96,64},{128,96},{160,128},{192,160},{224,192},{0,2... | collective-permute-start | bytes 1277960 | tf_op jit(solution)/shard_map/ppermute | solution.py:587
  51.7 11.0 %collective-permute-start.12 = (bf16[832,128]{1,0:T(8,128)(2,1)S(1)}, bf16[832,128]{1,0:T(8,128)(2,1)S(1)}, u32[]{:S(2)}, u32[]{:S(2)}) collective-permute-start(bf16[832,128]{1,0:T(8,128)(2,1)S(1)} %get-tuple-element.126), channel_id=1, source_target_pairs={{0,1},{1,2},{2,3},{3,4},{4,5},{5,6},{6,7},{7,0},{8,9},{9,10},{10,1... | collective-permute-start | bytes 638984 | tf_op jit(solution)/shard_map/ppermute | solution.py:587
  52.6 10.2 %collective-permute-start.13 = (bf16[832,128]{1,0:T(8,128)(2,1)S(1)}, bf16[832,128]{1,0:T(8,128)(2,1)S(1)}, u32[]{:S(2)}, u32[]{:S(2)}) collective-permute-start(bf16[832,128]{1,0:T(8,128)(2,1)S(1)} %get-tuple-element.127), channel_id=1, source_target_pairs={{1,0},{2,1},{3,2},{4,3},{5,4},{6,5},{7,6},{0,7},{9,8},{10,9},{11,1... | collective-permute-start | bytes 638984 | tf_op jit(solution)/shard_map/ppermute | solution.py:587
  55.9 1.8 %collective-permute-start.9 = (f32[8,128]{1,0:T(8,128)S(1)}, f32[8,128]{1,0:T(8,128)S(1)}, u32[]{:S(2)}, u32[]{:S(2)}) collective-permute-start(f32[8,128]{1,0:T(8,128)S(1)} %get-tuple-element.116.mine_ref), channel_id=1, source_target_pairs={{32,0},{64,32},{96,64},{128,96},{160,128},{192,160},{224,192},{0,2... | collective-permute-start | bytes 12296 | tf_op jit(solution)/shard_map/ppermute | solution.py:587
  56.4 4.2 %collective-permute-start.8 = (f32[8,128]{1,0:T(8,128)S(1)}, f32[8,128]{1,0:T(8,128)S(1)}, u32[]{:S(2)}, u32[]{:S(2)}) collective-permute-start(f32[8,128]{1,0:T(8,128)S(1)} %get-tuple-element.116.mine_ref), channel_id=1, source_target_pairs={{0,32},{32,64},{64,96},{96,128},{128,160},{160,192},{192,224},{224... | collective-permute-start | bytes 12296 | tf_op jit(solution)/shard_map/ppermute | solution.py:587
  60.7 10.9 %collective-permute-start.11 = (f32[8,128]{1,0:T(8,128)S(1)}, f32[8,128]{1,0:T(8,128)S(1)}, u32[]{:S(2)}, u32[]{:S(2)}) collective-permute-start(f32[8,128]{1,0:T(8,128)S(1)} %fold_force.3.mine_ref), channel_id=1, source_target_pairs={{1,0},{2,1},{3,2},{4,3},{5,4},{6,5},{7,6},{0,7},{9,8},{10,9},{11,1... | collective-permute-start | bytes 12296 | tf_op jit(solution)/shard_map/ppermute | solution.py:587
  62.4 9.2 %collective-permute-start.10 = (f32[8,128]{1,0:T(8,128)S(1)}, f32[8,128]{1,0:T(8,128)S(1)}, u32[]{:S(2)}, u32[]{:S(2)}) collective-permute-start(f32[8,128]{1,0:T(8,128)S(1)} %fold_force.3.mine_ref), channel_id=1, source_target_pairs={{0,1},{1,2},{2,3},{3,4},{4,5},{5,6},{6,7},{7,0},{8,9},{9,10},{10,1... | collective-permute-start | bytes 12296 | tf_op jit(solution)/shard_map/ppermute | solution.py:587
  62.8 4.5 %copy-start.14 = (s32[2,2,2]{2,1,0:T(2,128)S(1)}, s32[2,2,2]{2,1,0:T(2,128)}, u32[]{:S(2)}) copy-start(s32[2,2,2]{2,1,0:T(2,128)} %counts_ref.5) | copy-start | bytes 100
  62.8 18.2 %collective-permute-start.14 = (bf16[416,128]{1,0:T(8,128)(2,1)S(1)}, bf16[416,128]{1,0:T(8,128)(2,1)S(1)}, u32[]{:S(2)}, u32[]{:S(2)}) collective-permute-start(bf16[416,128]{1,0:T(8,128)(2,1)S(1)} %get-tuple-element.129), channel_id=1, source_target_pairs={{0,8},{8,16},{16,24},{24,0},{1,9},{9,17},{17,25},{25,1},{2,10},{10... | collective-permute-start | bytes 319496 | tf_op jit(solution)/shard_map/ppermute | solution.py:587
  65.0 16.0 %collective-permute-start.15 = (bf16[416,128]{1,0:T(8,128)(2,1)S(1)}, bf16[416,128]{1,0:T(8,128)(2,1)S(1)}, u32[]{:S(2)}, u32[]{:S(2)}) collective-permute-start(bf16[416,128]{1,0:T(8,128)(2,1)S(1)} %get-tuple-element.130), channel_id=1, source_target_pairs={{8,0},{16,8},{24,16},{0,24},{9,1},{17,9},{25,17},{1,25},{10,2},{18... | collective-permute-start | bytes 319496 | tf_op jit(solution)/shard_map/ppermute | solution.py:587
  71.7 4.5 %collective-permute-start.17 = (f32[8,128]{1,0:T(8,128)S(1)}, f32[8,128]{1,0:T(8,128)S(1)}, u32[]{:S(2)}, u32[]{:S(2)}) collective-permute-start(f32[8,128]{1,0:T(8,128)S(1)} %fold_force.4.mine_ref), channel_id=1, source_target_pairs={{8,0},{16,8},{24,16},{0,24},{9,1},{17,9},{25,17},{1,25},{10,2},{18... | collective-permute-start | bytes 12296 | tf_op jit(solution)/shard_map/ppermute | solution.py:587
  74.5 5.7 %collective-permute-start.16 = (f32[8,128]{1,0:T(8,128)S(1)}, f32[8,128]{1,0:T(8,128)S(1)}, u32[]{:S(2)}, u32[]{:S(2)}) collective-permute-start(f32[8,128]{1,0:T(8,128)S(1)} %fold_force.4.mine_ref), channel_id=1, source_target_pairs={{0,8},{8,16},{16,24},{24,0},{1,9},{9,17},{17,25},{25,1},{2,10},{10... | collective-permute-start | bytes 12296 | tf_op jit(solution)/shard_map/ppermute | solution.py:587

commit v2 on v1

--- a/solution.py
+++ b/solution.py
@@ -26,24 +26,34 @@
 )
 
 
-def rotation_table():
+def row_starts():
     starts = []
     total = 0
     for degree in range(LMAX + 1):
         starts.append(total)
         total += min(2 * degree + 1, 5) * (2 * degree + 1)
-    table = np.zeros((256, 30 * 128), np.float32)
-    for q, pair in enumerate(PAIRS):
-        for half, (m, degree) in enumerate(pair):
+    out = []
+    for pair in PAIRS:
+        for m, degree in pair:
             if degree > LMAX:
-                continue
-            breadth = 2 * degree + 1
-            row = m + min(degree, 2)
-            for col in range(breadth):
-                for copy in range(2):
-                    at = (2 * q + half) * 128 + copy * 64 + degree * degree + col
-                    table[starts[degree] + row * breadth + col, at] = 1.0
-    return table
+                out.append((-1, 0))
+            else:
+                out.append((starts[degree] + (m + min(degree, 2)) * (2 * degree + 1), degree))
+    return out
+
+
+def expansion(q):
+    rows = row_starts()
+    lane = iota((1, 256), 1)
+    j = lane & 63
+    target = jnp.full((1, 256), -1, jnp.int32)
+    for h in range(2):
+        start, degree = rows[2 * q + h]
+        if start >= 0:
+            low = degree * degree
+            inside = ((lane >> 7) == h) & (j >= low) & (j < low + 2 * degree + 1)
+            target = jnp.where(inside, start + j - low, target)
+    return jnp.where(iota((256, 256), 0) == target, 1.0, 0.0).astype(bf16)
 
 
 def base_table():
@@ -121,9 +131,9 @@
 
 
 def row_masks():
-    r = iota((16, 128), 0) & 7
+    r = iota((16, 128), 0) & 3
     h = iota((16, 128), 1) >> 6
-    return [jnp.where(r == 2 * t + h, 1.0, 0.0).astype(bf16) for t in range(4)]
+    return [jnp.where(r == 2 * t + h, 1.0, 0.0).astype(bf16) for t in range(2)]
 
 
 def lane_masks():
@@ -166,42 +176,43 @@
 
 
 def kernel_a1(
-    wt_ref, tab_ref, cot_ref, dist_ref, counts_ref, srcv_ref, dir_ref, rin_ref, rout_ref,
-    u_ref, v_ref, z0_ref, z1_ref, z2_ref, rad_ref, dsilu_ref, wb_ref, ratio_ref, envo_ref, side_ref, cs_ref,
-    env_ref,
+    wt_ref, counts_hbm, dist_hbm, rin_hbm, rout_hbm, cot_hbm,
+    u_ref, z0_ref, z1_ref, z2_ref, rad_ref, dsilu_ref, wb_ref, ratio_ref, envl_ref, cs_ref,
+    dist_ref, rin_ref, rout_ref, cot_ref, counts_ref, env_ref, sems,
 ):
+    copies = start_copies(
+        ((dist_hbm, dist_ref), (rin_hbm, rin_ref), (rout_hbm, rout_ref), (cot_hbm, cot_ref), (counts_hbm, counts_ref)), sems
+    )
     zs = (z0_ref, z1_ref, z2_ref)
+    copies[0].wait()
+    copies[1].wait()
     dist = column(dist_ref[...])
     basis, offset = basis_of(dist)
     wb_ref[...] = basis * (-offset / (sigma_width * sigma_width))
     inner = dot3(basis, rin_ref[...])
     sig = jax.nn.sigmoid(inner)
     dsilu_ref[...] = sig * (1.0 + inner * (1.0 - sig))
+    copies[2].wait()
+    copies[4].wait()
     rad_ref[...] = dot3(inner * sig, rout_ref[...])
     angle = jnp.broadcast_to(dist, (E, 128)) * (math.pi / cutoff)
     env = 0.5 * (jnp.cos(angle) + 1.0)
-    envo_ref[...] = env
+    pick = ((iota((G, E), 1) >> 3) == iota((G, E), 0)).astype(f32)
+    spread = jnp.where(
+        (iota((E, 256), 0) & 7) == (iota((E, 256), 1) & 7), jnp.concatenate([env, env], axis=1) * SCALE, 0.0
+    )
+    envl_ref[...] = lax.dot_general(
+        pick, spread, (((1,), (0,)), ((), ())), precision=lax.Precision.HIGHEST, preferred_element_type=f32
+    )
     ratio_ref[...] = (-0.5 * math.pi / cutoff) * jnp.sin(angle) / env
     env_ref[...] = env * (occupied_edges(counts_ref) * SCALE)
-    cell, slot, _ = edge_ids()
-    q = jnp.broadcast_to(column(srcv_ref[...].astype(f32)), (E, 128)).astype(jnp.int32)
-    lane = iota((E, 128), 1)
-    from_slot = 2 * padded_cell(q, cell) + (q & 1)
-    to_slot = 2 * padded_cell(jnp.full((E, 128), 26, jnp.int32), cell) + slot
-    sign = jnp.where(lane == from_slot, 1.0, 0.0) - jnp.where(lane == to_slot, 1.0, 0.0)
-    for d in range(3):
-        side_ref[d] = sign * column(dir_ref[16 * d : 16 * d + 16, :])
     wt = wt_ref[...]
     for q in range(15):
-        res = dot(wt, tab_ref[:, 256 * q : 256 * q + 256])
+        res = dot(wt, expansion(q))
         u_ref[:, 16 * q : 16 * q + 16, :] = pair_block(res[:, :128], res[:, 128:])
     u_ref[:, 240:256, :] = jnp.zeros((G, 16, 128), bf16)
 
-    def turn(g, carry):
-        v_ref[g] = u_ref[g].T[:64]
-        return carry
-
-    lax.fori_loop(0, G, turn, 0)
+    copies[3].wait()
     cs_ref[0:784, :] = cot_ref[...].astype(f32)
     cs_ref[784:800, :] = jnp.zeros((16, 128), f32)
     m_rot = jnp.where((iota((16, 128), 0) & 1) == (iota((16, 128), 1) >> 6), 1.0, 0.0).astype(bf16)
@@ -238,12 +249,25 @@
     lax.fori_loop(0, 4, rotate, 0)
 
 
-def kernel_a2(z0_ref, z1_ref, z2_ref, rad_ref, w0_ref, w1_ref, w2_ref, gi0_ref, gr_ref, w0v, w1v, w2v, sems):
-    copies = start_copies(((w0_ref, w0v), (w1_ref, w1v), (w2_ref, w2v)), sems)
+def halves(k0, k1):
+    low = (iota((1, 8, 128), 1) < 4)
+    return jnp.where(low, k0, pltpu.roll(k1, 4, 1)), jnp.where(low, pltpu.roll(k0, 4, 1), k1)
+
+
+def kernel_a2(u_ref, z0_ref, z1_ref, z2_ref, rad_ref, w0v, w1v, w2v, gi0_ref, gr_ref, v_ref, u4_ref):
+    def turn(g, carry):
+        u = u_ref[g]
+        v_ref[g] = u.T[:64]
+        pairs = u.astype(f32).reshape(16, 2, 8, 128)
+        a, b = halves(pairs[:, 0], pairs[:, 1])
+        u4_ref[g, 0] = a.reshape(128, 128).astype(bf16)
+        u4_ref[g, 1] = b.reshape(128, 128).astype(bf16)
+        return carry
+
+    lax.fori_loop(0, G, turn, 0)
     zs = (z0_ref, z1_ref, z2_ref)
     gr_ref[:, 240:256, :] = jnp.zeros((G, 16, 128), bf16)
     z0 = z0_ref[...]
-    copies[0].wait()
     for q in range(4):
         width = 256 if q < 3 else 128
         at = 256 * q
@@ -253,7 +277,6 @@
         second = gr[:, 128:] if q < 3 else jnp.zeros((E, 128), f32)
         gr_ref[:, 16 * q : 16 * q + 16, :] = pair_block(gr[:, :128], second)
     for m, wv, first in ((1, w1v, 4), (2, w2v, 10)):
-        copies[m].wait()
         z = zs[m][...]
         count = 7 - m
         for l0 in range(0, count, 2):
@@ -269,7 +292,19 @@
                 )
 
 
-def kernel_a3(v_ref, gr_ref, cs_ref, counts_ref, src_ref, xlo_ref, xhi_ref, mid_ref, acc_ref):
+def kernel_a3(
+    v_ref, gr_ref, cs_ref, counts_ref, src_ref, srcv_ref, dir_ref,
+    xlo_ref, xhi_ref, mid_ref, side_ref, acc_ref,
+):
+    cell, slot, _ = edge_ids()
+    q = jnp.broadcast_to(column(srcv_ref[...].astype(f32)), (E, 128)).astype(jnp.int32)
+    lane = iota((E, 128), 1)
+    from_slot = 2 * padded_cell(q, cell) + (q & 1)
+    to_slot = 2 * padded_cell(jnp.full((E, 128), 26, jnp.int32), cell) + slot
+    sign = jnp.where(lane == from_slot, 1.0, 0.0) - jnp.where(lane == to_slot, 1.0, 0.0)
+    for d in range(3):
+        side_ref[d] = sign * column(dir_ref[16 * d : 16 * d + 16, :])
+
     acc_ref[...] = jnp.zeros(acc_ref.shape, f32)
     row_ok = iota((56, 128), 0) < 49
     for cell in range(8):
@@ -301,12 +336,11 @@
 
 def kernel_b1(
     own_ref, ylo_ref, yhi_ref, zlo_ref, zhi_ref, xlo_ref, xhi_ref, base_ref, src_ref,
-    u_ref, g0_ref, g1_ref, g2_ref, gi0_ref, rad_ref, dsilu_ref, wb_ref, ratio_ref, side_ref, rin_ref, rout_ref,
-    w0_ref, w1_ref, w2_ref,
+    u4_ref, g0_ref, g1_ref, g2_ref, gi0_ref, rad_ref, dsilu_ref, wb_ref, ratio_ref, side_ref, rin_ref, rout_ref,
+    w0v, w1v, w2v,
     h_ref, force_ref,
-    w0v, w1v, w2v, fs_ref, x0_ref, x1_ref, x2_ref, p0_ref, sems,
+    fs_ref, x0_ref, x1_ref, x2_ref, p0_ref,
 ):
-    copies = start_copies(((w0_ref, w0v), (w1_ref, w1v), (w2_ref, w2v)), sems)
     at = 0
     for piece in (own_ref, ylo_ref, yhi_ref, zlo_ref, zhi_ref, xlo_ref, xhi_ref):
         n = piece.shape[0]
@@ -324,24 +358,27 @@
             cell = 2 * cp + half
             for i in range(3):
                 g = 3 * cell + i
-                rows = []
-                for e in range(8):
-                    q = src_ref[2 * cell + (e & 1), 4 * i + (e >> 1)]
-                    base = base_ref[padded_cell(q, cell)] + (q & 1)
-                    rows += [fs_ref[pl.ds(base, 56, 2), :], zero8]
-                rhs = jnp.concatenate(rows, axis=0).astype(bf16)
-                u = u_ref[g, 0:240, :]
-                lhs = jnp.concatenate([masked(u, m) for m in masks_r], axis=1)
-                parts.append(dot(lhs, rhs).reshape(30, 8, 128))
+                res = []
+                for half4 in range(2):
+                    rows = []
+                    for e in range(4 * half4, 4 * half4 + 4):
+                        q = src_ref[2 * cell + (e & 1), 4 * i + (e >> 1)]
+                        base = base_ref[padded_cell(q, cell)] + (q & 1)
+                        rows += [fs_ref[pl.ds(base, 56, 2), :], zero8]
+                    rhs = jnp.concatenate(rows, axis=0).astype(bf16)
+                    u = u4_ref[g, half4]
+                    lhs = jnp.concatenate([masked(u, m) for m in masks_r], axis=1)
+                    res.append(dot(lhs, rhs).reshape(16, 8, 128))
+                parts.append(halves(*res))
         for j in range(3):
-            both = jnp.concatenate([parts[2 * j], parts[2 * j + 1]], axis=1)
+            both = [jnp.concatenate([parts[2 * j][h], parts[2 * j + 1][h]], axis=1) for h in range(2)]
             row = pl.multiple_of(48 * cp + 16 * j, 16)
             for q, pair in enumerate(PAIRS):
                 for h, (m, degree) in enumerate(pair):
                     if degree > LMAX:
                         continue
                     z, up, col = z_place(m, degree)
-                    value = both[2 * q + h]
+                    value = both[h][q]
                     if m == 0:
                         p0_ref[pl.ds(row, 16), col : col + 128] = value
                         value = value * rad_ref[pl.ds(row, 16), col : col + 128]
@@ -355,7 +392,6 @@
     def rounded(x):
         return x.astype(bf16).astype(f32)
 
-    copies[0].wait()
     x0 = x0_ref[...]
     for q in range(4):
         width = 256 if q < 3 else 128
@@ -368,7 +404,6 @@
         second = hid[:, 128:] if q < 3 else jnp.zeros((E, 128), f32)
         h_ref[:, 16 * q : 16 * q + 16, :] = pair_block(hid[:, :128], second)
     for m, wv, first in ((1, w1v, 4), (2, w2v, 10)):
-        copies[m].wait()
         x = xs[m][...]
         count = 7 - m
         for l0 in range(0, count, 2):
@@ -395,25 +430,22 @@
         force_ref[d : d + 1, :] = jnp.sum(side_ref[d] * grad_dist, axis=0, keepdims=True)
 
 
-def kernel_b2(own_ref, v_ref, h_ref, envo_ref, counts_ref, upd_ref, fs_ref, us_ref):
+def kernel_b2(own_ref, v_ref, h_ref, envl_ref, counts_ref, upd_ref, fs_ref, us_ref):
     fs_ref[0:784, :] = own_ref[...].astype(f32)
     fs_ref[784:800, :] = jnp.zeros((16, 128), f32)
-    masks = lane_masks()
+    slot = iota((64, 256), 1) & 1
 
     def back(cell, carry):
-        sums = [jnp.zeros((56, 128), f32), jnp.zeros((56, 128), f32)]
+        sums = jnp.zeros((128, 128), f32)
         for i in range(3):
             g = 3 * cell + i
-            v = v_ref[g]
-            lhs = jnp.concatenate([masked(v, m) for m in masks], axis=0)
-            res = dot(lhs, h_ref[g])
-            for e in range(8):
-                scale = envo_ref[pl.ds(8 * g + e, 1), :]
-                sums[e & 1] = sums[e & 1] + res[64 * e : 64 * e + 56] * scale
+            v = v_ref[g].astype(f32) * envl_ref[pl.ds(g, 1), :]
+            lhs = jnp.concatenate([jnp.where(slot == s, v, 0.0) for s in range(2)], axis=0).astype(bf16)
+            sums = sums + dot(lhs, h_ref[g])
         for s in range(2):
             occ = jnp.where(s < counts_ref[cell >> 2, (cell >> 1) & 1, cell & 1], 1.0, 0.0).astype(f32)
             own = fs_ref[pl.ds(98 * cell + s, 56, 2), :]
-            us_ref[pl.ds(98 * cell + s, 56, 2), :] = (own + sums[s] * SCALE) * occ
+            us_ref[pl.ds(98 * cell + s, 56, 2), :] = (own + sums[64 * s : 64 * s + 56]) * occ
         return carry
 
     lax.fori_loop(0, 8, back, 0)
@@ -442,7 +474,25 @@
             zhi_ref[to : to + 2 * CR, :] = jnp.concatenate(ends[3], axis=0).astype(bf16)
 
 
-def fold_z(mid_ref, lo_ref, hi_ref, ylo_ref, yhi_ref, out_ref):
+def force_sum(mine, lo, hi, shift, bit):
+    at = (iota((8, 128), 1) >> bit) & 3
+    lo = pltpu.roll(lo, 128 - shift, 1)
+    hi = pltpu.roll(hi, shift, 1)
+    return mine + jnp.where(at == 1, lo, 0.0) + jnp.where(at == 2, hi, 0.0)
+
+
+def fold_force_x(mine_ref, lo_ref, hi_ref, out_ref):
+    out_ref[...] = force_sum(mine_ref[...], lo_ref[...], hi_ref[...], 64, 5)
+
+
+def fold_z(
+    mid_ref, lo_ref, hi_ref, force_ref, flo_ref, fhi_ref, ylo_ref, yhi_ref, out_ref, fout_ref,
+):
+    force = force_sum(force_ref[...], flo_ref[...], fhi_ref[...], 4, 1)
+    fout_ref[...] = force
+    rest = force - force.astype(bf16).astype(f32)
+    for ref in (ylo_ref, yhi_ref):
+        ref[4 * CR : 4 * CR + 16, :] = jnp.concatenate([force, rest], axis=0).astype(bf16)
     for px in range(2):
         arrived = [[], []]
         for z, ref in enumerate((lo_ref, hi_ref)):
@@ -464,7 +514,19 @@
                 out_ref[to : to + 2 * CR, :] = jnp.concatenate(done, axis=0)
 
 
-def fold_y(mid_ref, lo_ref, hi_ref, out_ref):
+def fold_y(mid_ref, force_ref, lo_ref, hi_ref, out_ref, fout_ref):
+    sides = []
+    for ref in (lo_ref, hi_ref):
+        both = ref[4 * CR : 4 * CR + 16, :].astype(f32)
+        sides.append(both[:8] + both[8:])
+    total = force_sum(force_ref[...], sides[0], sides[1], 16, 3)
+    r = iota((16, 128), 1)
+    o = iota((16, 128), 0)
+    from_lane = ((o >> 3) + 1) * 32 + (((o >> 2) & 1) + 1) * 8 + (((o >> 1) & 1) + 1) * 2 + (o & 1)
+    pick = (r == from_lane).astype(f32)
+    fout_ref[...] = lax.dot_general(
+        pick, total, (((1,), (1,)), ((), ())), precision=lax.Precision.HIGHEST, preferred_element_type=f32
+    )[:, :3]
     for px in range(2):
         for py, ref in enumerate((lo_ref, hi_ref)):
             pair = ref[px * 2 * CR : (px + 1) * 2 * CR, :].astype(f32)
@@ -475,30 +537,9 @@
                 out_ref[to : to + 98, :] = value[z * CR : z * CR + 98]
 
 
-def fold_force(shift, bit, last):
-    def kernel(mine_ref, lo_ref, hi_ref, out_ref):
-        lane = iota((8, 128), 1)
-        at = (lane >> bit) & 3
-        lo = pltpu.roll(lo_ref[...], 128 - shift, 1)
-        hi = pltpu.roll(hi_ref[...], shift, 1)
-        total = mine_ref[...] + jnp.where(at == 1, lo, 0.0) + jnp.where(at == 2, hi, 0.0)
-        if last:
-            r = iota((16, 128), 1)
-            o = iota((16, 128), 0)
-            from_lane = ((o >> 3) + 1) * 32 + (((o >> 2) & 1) + 1) * 8 + (((o >> 1) & 1) + 1) * 2 + (o & 1)
-            pick = (r == from_lane).astype(f32)
-            out_ref[...] = lax.dot_general(
-                pick, total, (((1,), (1,)), ((), ())), precision=lax.Precision.HIGHEST, preferred_element_type=f32
-            )[:, :3]
-        else:
-            out_ref[...] = total
-
-    return kernel
-
-
 VM = pl.BlockSpec(memory_space=pltpu.VMEM)
 SM = pl.BlockSpec(memory_space=pltpu.SMEM)
-AN = pl.BlockSpec(memory_space=pl.ANY)
+HB = pl.BlockSpec(memory_space=pltpu.HBM)
 
 
 def shape(dims, dtype):
@@ -526,53 +567,58 @@
     return pl.CostEstimate(flops=int(us * 10**9), bytes_accessed=1 << 20, transcendentals=0)
 
 
-def run_a1(wt, cot, dist, counts, src, dirs, rin, rout):
-    tab = jnp.asarray(rotation_table(), dtype=bf16)
+def run_a1(wt, counts, dist, rin, rout, cot):
     out = [
-        shape((G, 256, 128), bf16), shape((G, 64, 256), bf16),
+        shape((G, 256, 128), bf16),
         shape((E, 896), bf16), shape((2 * E, 768), bf16), shape((2 * E, 640), bf16),
-        shape((E, 896), f32), shape((E, 128), f32), shape((E, NB), f32), shape((E, 128), f32), shape((E, 128), f32),
-        shape((3, E, 128), f32), shape((800, 128), f32),
+        shape((E, 896), f32), shape((E, 128), f32), shape((E, NB), f32), shape((E, 128), f32), shape((G, 256), f32),
+        shape((800, 128), f32),
     ]
-    specs = [VM, VM, VM, VM, SM, VM, VM, VM, VM]
-    return call(kernel_a1, out, specs, [pltpu.VMEM((E, 128), f32)], 24 << 20, "rotations", cost(8))(
-        wt, tab, cot, dist, counts, src, dirs, rin, rout
-    )
-
-
-def run_a2(z0, z1, z2, rad, w0, w1, w2):
-    out = [shape((E, 896), f32), shape((G, 256, 128), bf16)]
-    scratch = weights_scratch() + [pltpu.SemaphoreType.DMA((3,))]
-    return call(kernel_a2, out, [VM] * 4 + [AN] * 3, scratch, 24 << 20, "mix_backward", cost(5))(
-        z0, z1, z2, rad, w0, w1, w2
-    )
-
-
-def run_a3(v, gr, cs, counts, src):
-    out = [shape((16 * CR, 128), bf16), shape((16 * CR, 128), bf16), shape((32 * CR, 128), f32)]
+    scratch = [
+        pltpu.VMEM((16, 12), f32), pltpu.VMEM((NB, 128), f32), pltpu.VMEM((128, 896), f32),
+        pltpu.VMEM((784, 128), bf16), pltpu.SMEM((2, 2, 2), jnp.int32), pltpu.VMEM((E, 128), f32),
+        pltpu.SemaphoreType.DMA((5,)),
+    ]
+    return call(kernel_a1, out, [VM] + [HB] * 5, scratch, 24 << 20, "rotations", cost(6))(
+        wt, *[pltpu.with_memory_space_constraint(x, pltpu.HBM) for x in (counts, dist, rin, rout, cot)]
+    )
+
+
+def run_a2(u, z0, z1, z2, rad, w0, w1, w2):
+    out = [
+        shape((E, 896), f32), shape((G, 256, 128), bf16), shape((G, 64, 256), bf16), shape((G, 2, 128, 128), bf16),
+    ]
+    return call(kernel_a2, out, [VM] * 8, [], 20 << 20, "mix_backward", cost(4))(u, z0, z1, z2, rad, w0, w1, w2)
+
+
+def run_a3(v, gr, cs, counts, src, dirs):
+    out = [
+        shape((16 * CR, 128), bf16), shape((16 * CR, 128), bf16), shape((32 * CR, 128), f32),
+        shape((3, E, 128), f32),
+    ]
     scratch = [pltpu.VMEM((64 * CR + 16, 128), f32)]
-    return call(kernel_a3, out, [VM, VM, VM, SM, SM], scratch, 20 << 20, "source_gradients", cost(4))(
-        v, gr, cs, counts, src
+    return call(kernel_a3, out, [VM, VM, VM, SM, SM, VM, VM], scratch, 20 << 20, "source_gradients", cost(5))(
+        v, gr, cs, counts, src, src, dirs
     )
 
 
 def run_b1(pieces, src, saved, rin, rout, w0, w1, w2):
     out = [shape((G, 256, 128), bf16), shape((8, 128), f32)]
-    scratch = weights_scratch() + [
+    scratch = [
         pltpu.VMEM((6272 + 16, 128), f32),
         pltpu.VMEM((E, 896), bf16), pltpu.VMEM((2 * E, 768), bf16), pltpu.VMEM((2 * E, 640), bf16),
-        pltpu.VMEM((E, 896), f32), pltpu.SemaphoreType.DMA((3,)),
+        pltpu.VMEM((E, 896), f32),
     ]
-    specs = [VM] * 7 + [SM, SM] + [VM] * 12 + [AN] * 3
-    return call(kernel_b1, out, specs, scratch, 36 << 20, "hidden_and_forces", cost(9))(
+    specs = [VM] * 7 + [SM, SM] + [VM] * 15
+    return call(kernel_b1, out, specs, scratch, 28 << 20, "hidden_and_forces", cost(7))(
         *pieces, jnp.asarray(base_table()), src, *saved, rin, rout, w0, w1, w2
     )
 
 
-def run_b2(own, v, h, envo, counts):
+def run_b2(own, v, h, envl, counts):
     scratch = [pltpu.VMEM((800, 128), f32), pltpu.VMEM((800, 128), f32)]
-    return call(kernel_b2, shape((784, 128), bf16), [VM] * 4 + [SM], scratch, 16 << 20, "updated", cost(3))(
-        own, v, h, envo, counts
+    return call(kernel_b2, shape((784, 128), bf16), [VM] * 4 + [SM], scratch, 16 << 20, "updated", cost(2))(
+        own, v, h, envl, counts
     )
 
 
@@ -587,22 +633,17 @@
     return lax.ppermute(to_up, axis, up), lax.ppermute(to_down, axis, down)
 
 
-def add_force(force, lo, hi, shift, bit, last=False):
-    out = shape((16, 3) if last else (8, 128), f32)
-    return call(fold_force(shift, bit, last), out, [VM] * 3, [], 8 << 20, "fold_force", cost(0.2))(force, lo, hi)
-
-
 def tie(*values):
     return lax.optimization_barrier(values)
 
 
 def test_run(pieces, wt, cot, src, cnt, dist, dirs, w0, w1, w2, rin, rout):
     cnt = cnt.reshape(2, 2, 2)
-    u, v, z0, z1, z2, rad, dsilu, wb, ratio, envo, side, cs = run_a1(wt, cot, dist, cnt, src, dirs, rin, rout)
-    gi0, gr = run_a2(z0, z1, z2, rad, w0, w1, w2)
-    gxlo, gxhi, mid = run_a3(v, gr, cs, cnt, src)
-    h, force = run_b1(pieces, src, (u, z0, z1, z2, gi0, rad, dsilu, wb, ratio, side), rin, rout, w0, w1, w2)
-    return run_b2(pieces[0], v, h, envo, cnt), force, gxlo, gxhi, mid
+    u, z0, z1, z2, rad, dsilu, wb, ratio, envl, cs = run_a1(wt, cnt, dist, rin, rout, cot)
+    gi0, gr, v, u4 = run_a2(u, z0, z1, z2, rad, w0, w1, w2)
+    gxlo, gxhi, mid, side = run_a3(v, gr, cs, cnt, src, dirs)
+    h, force = run_b1(pieces, src, (u4, z0, z1, z2, gi0, rad, dsilu, wb, ratio, side), rin, rout, w0, w1, w2)
+    return run_b2(pieces[0], v, h, envl, cnt), force, gxlo, gxhi, mid
 
 
 def local(features, cotangent, counts, sources, wigner, distance, direction, w0, w1, w2, rin, rout):
@@ -615,48 +656,49 @@
     feats = jnp.transpose(features, (0, 1, 2, 4, 3, 5))
 
     ylo, yhi = exchange(feats[:, 1:2], feats[:, 0:1], "gy")
-    a1 = run_a1(wt, cot, dist, counts, src, dirs, rin, rout)
+    a1 = run_a1(wt, counts, dist, rin, rout, cot)
     a1, ylo, yhi = tie(a1, ylo, yhi)
-    u, v, z0, z1, z2, rad, dsilu, wb, ratio, envo, side, cs = a1
+    u, z0, z1, z2, rad, dsilu, wb, ratio, envl, cs = a1
     tall = jnp.concatenate([ylo, feats, yhi], axis=1)
     up, down = tall[:, :, 1:2], tall[:, :, 0:1]
-    (z0, z1, z2, rad), up, down = tie((z0, z1, z2, rad), up, down)
+    (u, z0, z1, z2, rad), up, down = tie((u, z0, z1, z2, rad), up, down)
     zlo, zhi = exchange(up, down, "gz")
-    gi0, gr = run_a2(z0, z1, z2, rad, w0, w1, w2)
+    gi0, gr, v, u4 = run_a2(u, z0, z1, z2, rad, w0, w1, w2)
     gr, zlo, zhi = tie(gr, zlo, zhi)
     top = jnp.concatenate([zlo[1:2], tall[1:2], zhi[1:2]], axis=2)
     low = jnp.concatenate([zlo[0:1], tall[0:1], zhi[0:1]], axis=2)
     gr, top, low = tie(gr, top, low)
     xlo, xhi = exchange(top, low, "gx")
-    gxlo, gxhi, mid = run_a3(v, gr, cs, counts, src)
-    gxlo, gxhi, mid, xlo, xhi = tie(gxlo, gxhi, mid, xlo, xhi)
+    gxlo, gxhi, mid, side = run_a3(v, gr, cs, counts, src, dirs)
 
     lo, hi = exchange(gxhi, gxlo, "gx")
     rows = [p.reshape(-1, 128) for p in (feats, ylo, yhi, zlo, zhi, xlo, xhi)]
-    h, force = run_b1(rows, src, (u, z0, z1, z2, gi0, rad, dsilu, wb, ratio, side), rin, rout, w0, w1, w2)
+    h, force = run_b1(rows, src, (u4, z0, z1, z2, gi0, rad, dsilu, wb, ratio, side), rin, rout, w0, w1, w2)
     h, force, lo, hi = tie(h, force, lo, hi)
     flo, fhi = exchange(force, force, "gx")
     gzlo, gzhi, mid = call(
         fold_x,
         [shape((8 * CR, 128), bf16), shape((8 * CR, 128), bf16), shape((16 * CR, 128), f32)],
-        [VM] * 3, [], 16 << 20, "fold_x", cost(1),
+        [VM] * 3, [], 16 << 20, "fold_x", cost(4),
     )(mid, lo, hi)
     lo, hi = exchange(gzhi, gzlo, "gz")
-    force = add_force(force, flo, fhi, 64, 5)
+    force = call(fold_force_x, shape((8, 128), f32), [VM] * 3, [], 8 << 20, "fold_force", cost(0.2))(force, flo, fhi)
+    flo, fhi = exchange(force, force, "gz")
+    gylo, gyhi, mid, force = call(
+        fold_z,
+        [
+            shape((4 * CR + 16, 128), bf16), shape((4 * CR + 16, 128), bf16), shape((8 * CR, 128), f32),
+            shape((8, 128), f32),
+        ],
+        [VM] * 6, [], 16 << 20, "fold_z", cost(1),
+    )(mid, lo, hi, force, flo, fhi)
     force, h = tie(force, h)
-    flo, fhi = exchange(force, force, "gz")
-    updated = run_b2(rows[0], v, h, envo, counts)
-    updated, flo, fhi = tie(updated, flo, fhi)
-    force = add_force(force, flo, fhi, 4, 1)
-    flo, fhi = exchange(force, force, "gy")
-    gylo, gyhi, mid = call(
-        fold_z,
-        [shape((4 * CR, 128), bf16), shape((4 * CR, 128), bf16), shape((8 * CR, 128), f32)],
-        [VM] * 3, [], 16 << 20, "fold_z", cost(1),
-    )(mid, lo, hi)
     lo, hi = exchange(gyhi, gylo, "gy")
-    force = add_force(force, flo, fhi, 16, 3, True)
-    grads = call(fold_y, shape((784, 128), f32), [VM] * 3, [], 16 << 20, "fold_y", cost(1))(mid, lo, hi)
+    updated = run_b2(rows[0], v, h, envl, counts)
+    updated, lo, hi = tie(updated, lo, hi)
+    grads, force = call(
+        fold_y, [shape((784, 128), f32), shape((16, 3), f32)], [VM] * 4, [], 16 << 20, "fold_y", cost(1),
+    )(mid, force, lo, hi)
     forces = jnp.moveaxis(force.reshape(2, 2, 2, 2, 3), 4, 0)
 
     def back(x):

time: 83.3 us -> 71.3 us (0.86); the launches traced: 81.8 us -> 71.2 us
  local copies, waits for them, and re-layouts: 10.2 us -> 2.99 us
  Pallas kernels: 28.4 us -> 24 us
  waiting for transfers between devices: 10.9 us -> 13.6 us
  starting transfers between devices: 29.7 us -> 27.9 us
    unnamed x34 -> x20, local copies, waits for them, and re-layouts: 7.24 us -> 0.06 us
    pallas_call x9 -> x7, Pallas kernels: 23.8 us -> 20.9 us  [the longest x1 6.27 us: run_b1(): call(kernel_b1, out, specs, scratch, 28 << 20, 'hidden_and_forces', cost(7))]
    ppermute x18 -> x16, waiting for transfers between devices: 10.9 us -> 13.6 us  [exchange(): return (lax.ppermute(to_up, axis, up), lax.ppermute(to_down, axis, down))]
    ppermute x18 -> x16, starting transfers between devices: 29.7 us -> 27.9 us  [exchange(): return (lax.ppermute(to_up, axis, up), lax.ppermute(to_down, axis, down))]
    pallas_call x1, Pallas kernels: 4.34 us -> 2.94 us  [run_b2(): call(kernel_b2, shape((784, 128), bf16), [VM] * 4 + [SM], scratch, 16 <<...]
  transfers between devices with their start and end apart: 18 -> 16, of which waited for: 6 -> 6; matrix products, arithmetic and copies ran while one was open for 2% -> 2% of each run, Pallas kernels for 33% -> 32%
where the time goes in v2:
time: 71.3 us; the launch traced here: 71.2 us
  starting transfers between devices  27.9 us (39%)
  Pallas kernels  24 us (34%)
  waiting for transfers between devices  13.6 us (19%)
  local copies, waits for them, and re-layouts  2.99 us (4%)
  other arithmetic  1.76 us (2%)
  between operations  0.89 us (1%)
    ppermute x16, starting transfers between devices, exchange(): return (lax.ppermute(to_up, axis, up), lax.ppermute(to_down, axis, down))  27.9 us
    ppermute x16, waiting for transfers between devices, exchange(): return (lax.ppermute(to_up, axis, up), lax.ppermute(to_down, axis, down))  13.6 us
    pallas_call x1, Pallas kernels, run_b1(): call(kernel_b1, out, specs, scratch, 28 << 20, 'hidden_and_forces', cost(7))  6.27 us
    pallas_call x1, Pallas kernels, run_a3(): call(kernel_a3, out, [VM, VM, VM, SM, SM, VM, VM], scratch, 20 << 20, 'so...  5.03 us
    pallas_call x1, Pallas kernels, run_a1(): call(kernel_a1, out, [VM] + [HB] * 5, scratch, 24 << 20, 'rotations', cos...  4.56 us
    pallas_call x1, Pallas kernels, run_a2(): call(kernel_a2, out, [VM] * 8, [], 20 << 20, 'mix_backward', cost(4))  4.03 us
    pallas_call x1, Pallas kernels, run_b2(): call(kernel_b2, shape((784, 128), bf16), [VM] * 4 + [SM], scratch, 16 <<...  2.94 us
  transfers between devices with their start and end apart: 16, of which 6 were waited for; matrix products, arithmetic and copies ran while one was open for 2% of the time, Pallas kernels for 32%

profile of v2, /device:TPU:32, one launch (start us, length us, event | category | flops | bytes accessed | tf_op | source)
XLA Modules:
  0.0 71.2 jit_solution(6119470748432151450)
XLA Ops:
  0.6 1.1 %fusion.4 = (bf16[2,1,2,49,2,128]{5,4,3,2,1,0:T(2,128)(2,1)S(1)}, bf16[2,1,2,49,2,128]{5,4,3,2,1,0:T(2,128)(2,1)S(1)}) fusion(bf16[2,2,2,49,2,128]{5,4,3,2,1,0:T(2,128)(2,1)} %bitcast.26), kind=kLoop, calls=%fused_computation.7 | loop fusion | bytes 401408 | tf_op jit(solution)/shard_map/slice | solution.py:658
  1.7 5.5 %collective-permute-start.1 = (bf16[2,1,2,49,2,128]{5,4,3,2,1,0:T(2,128)(2,1)S(1)}, bf16[2,1,2,49,2,128]{5,4,3,2,1,0:T(2,128)(2,1)S(1)}, u32[]{:S(2)}, u32[]{:S(2)}) collective-permute-start(bf16[2,1,2,49,2,128]{5,4,3,2,1,0:T(2,128)(2,1)S(1)} %get-tuple-element.143), channel_id=1, source_target_pairs={{8,0},{16,8},{24,16},{0,24},{9,1},{17,9},{25,17},{1,25},{10,2},{18... | collective-permute-start | bytes 301064 | tf_op jit(solution)/shard_map/ppermute | solution.py:633
  7.2 1.0 %reshape.52 = bf16[192,235]{1,0:T(8,128)(2,1)S(1)} reshape(bf16[2,2,2,12,2,235]{5,4,3,2,1,0:T(2,128)(2,1)} %bitcast.40) | data formatting | bytes 180480 | tf_op jit(solution)/shard_map/reshape | solution.py:651
  8.2 0.0 copy-start
  8.2 0.0 copy-start.1
  8.2 0.0 copy-start.2
  8.3 4.6 %rotations.1 = (bf16[24,256,128]{2,1,0:T(8,128)(2,1)S(1)}, bf16[192,896]{1,0:T(8,128)(2,1)S(1)}, bf16[384,768]{1,0:T(8,128)(2,1)S(1)}, bf16[384,640]{1,0:T(8,128...) custom-call(bf16[192,256]{1,0:T(8,128)(2,1)S(1)} %pad.4.wt_ref, ...), custom_call_target="tpu_custom_call" | custom-call | flops 6000000000 | bytes 1048576 | tf_op jit(solution)/shard_map/rotations/pallas_call | solution.py:582
  12.8 0.0 copy-start.3
  12.8 0.0 collective-permute-done.1
  12.8 2.9 %collective-permute-done = bf16[2,1,2,49,2,128]{5,4,3,2,1,0:T(2,128)(2,1)S(1)} collective-permute-done((bf16[2,1,2,49,2,128]{5,4,3,2,1,0:T(2,128)(2,1)S(1)}, bf16[2,1,2,49,2,128]{5,4,3,2,1,0:T(2,128)(2,1)S(1)}, u32[]{:S(2)}, u32[]{:S(2)}) %collective-permute-start) | collective-permute-done | bytes 100384 | tf_op jit(solution)/shard_map/ppermute | solution.py:633
  15.8 0.6 pad_maximum_fusion
  16.4 0.3 fusion.1
  16.6 1.7 %collective-permute-start.2 = (bf16[2,4,1,49,2,128]{5,4,3,2,1,0:T(2,128)(2,1)S(1)}, bf16[2,4,1,49,2,128]{5,4,3,2,1,0:T(2,128)(2,1)S(1)}, u32[]{:S(2)}, u32[]{:S(2)}) collective-permute-start(bf16[2,4,1,49,2,128]{5,4,3,2,1,0:T(2,128)(2,1)S(1)} %get-tuple-element.90), channel_id=1, source_target_pairs={{0,1},{1,2},{2,3},{3,4},{4,5},{5,6},{6,7},{7,0},{8,9},{9,10},{10,1... | collective-permute-start | bytes 602120 | tf_op jit(solution)/shard_map/ppermute | solution.py:633
  18.3 2.6 %collective-permute-start.3 = (bf16[2,4,1,49,2,128]{5,4,3,2,1,0:T(2,128)(2,1)S(1)}, bf16[2,4,1,49,2,128]{5,4,3,2,1,0:T(2,128)(2,1)S(1)}, u32[]{:S(2)}, u32[]{:S(2)}) collective-permute-start(bf16[2,4,1,49,2,128]{5,4,3,2,1,0:T(2,128)(2,1)S(1)} %get-tuple-element.91), channel_id=1, source_target_pairs={{1,0},{2,1},{3,2},{4,3},{5,4},{6,5},{7,6},{0,7},{9,8},{10,9},{11,1... | collective-permute-start | bytes 602120 | tf_op jit(solution)/shard_map/ppermute | solution.py:633
  20.9 4.0 %mix_backward.1 = (f32[192,896]{1,0:T(8,128)S(1)}, bf16[24,256,128]{2,1,0:T(8,128)(2,1)S(1)}, bf16[24,64,256]{2,1,0:T(8,128)(2,1)S(1)}, bf16[24,2,128,128]{3,2,1,0:T(8,128)(2,1)S(1)}) custom-call(bf16[24,256,128]{2,1,0:T(8,128)(2,1)S(1)} %get-tuple-element.83.u_ref, bf16[192,896]{1,0:T(8,128)(2,1)S(1)} %get-tuple-element.84.z0_ref.g0_ref, ...), custom_call_target="tpu_custom_call" | custom-call | flops 4000000000 | bytes 1048576 | tf_op jit(solution)/shard_map/mix_backward/pallas_call | solution.py:591
  24.9 0.0 copy-start.6
  24.9 0.0 copy-start.7
  24.9 0.0 copy-start.8
  24.9 0.3 fusion
  25.2 0.0 collective-permute-done.2
  25.2 0.3 fusion.2
  25.5 0.6 pad_maximum_fusion.2
  26.1 0.6 pad_maximum_fusion.1
  26.7 0.0 collective-permute-start.4
  26.7 2.9 %collective-permute-start.5 = (bf16[1,4,4,49,2,128]{5,4,3,2,1,0:T(2,128)(2,1)S(1)}, bf16[1,4,4,49,2,128]{5,4,3,2,1,0:T(2,128)(2,1)S(1)}, u32[]{:S(2)}, u32[]{:S(2)}) collective-permute-start(bf16[1,4,4,49,2,128]{5,4,3,2,1,0:T(2,128)(2,1)S(1)} %pad_maximum_fusion.2), channel_id=1, source_target_pairs={{32,0},{64,32},{96,64},{128,96},{160,128},{192,160},{224,192},{0,2... | collective-permute-start | bytes 1204232 | tf_op jit(solution)/shard_map/ppermute | solution.py:633
  29.7 0.0 copy-start.5
  29.7 0.0 copy-start.9
  29.7 5.0 %source_gradients.1 = (bf16[1664,128]{1,0:T(8,128)(2,1)S(1)}, bf16[1664,128]{1,0:T(8,128)(2,1)S(1)}, f32[3328,128]{1,0:T(8,128)S(1)}, f32[3,192,128]{2,1,0:T(8,128)S(1)}) custom-call(bf16[24,64,256]{2,1,0:T(8,128)(2,1)S(1)} %get-tuple-element.88.v_ref, bf16[24,256,128]{2,1,0:T(8,128)(2,1)S(1)} %get-tuple-element.95.gr_ref, ...), custom_call_target="tpu_custom_call" | custom-call | flops 5000000000 | bytes 1048576 | tf_op jit(solution)/shard_map/source_gradients/pallas_call | solution.py:600
  34.7 0.0 collective-permute-start.6
  34.8 2.9 %collective-permute-start.7 = (bf16[1664,128]{1,0:T(8,128)(2,1)S(1)}, bf16[1664,128]{1,0:T(8,128)(2,1)S(1)}, u32[]{:S(2)}, u32[]{:S(2)}) collective-permute-start(bf16[1664,128]{1,0:T(8,128)(2,1)S(1)} %get-tuple-element.109), channel_id=1, source_target_pairs={{32,0},{64,32},{96,64},{128,96},{160,128},{192,160},{224,192},{0,2... | collective-permute-start | bytes 1277960 | tf_op jit(solution)/shard_map/ppermute | solution.py:633
  37.7 6.3 %hidden_and_forces.1 = (bf16[24,256,128]{2,1,0:T(8,128)(2,1)S(1)}, f32[8,128]{1,0:T(8,128)S(1)}) custom-call(bf16[784,128]{1,0:T(8,128)(2,1)S(1)} %bitcast.28, bf16[392,128]{1,0:T(8,128)(2,1)S(1)} %bitcast.33, bf16[392,128]{1,0:T(8,128)(2,1)S(1)} %bitcast.32, bf16[784,128]{1,0:T(8,128)(2,1)S(1)} %bitcast.30, bf16[784,128]{1,0:T(8,128)(2,1)S(1)} %bitcast.31, ...), custom_call_target="tpu_custom_call" | custom-call | flops 7000000000 | bytes 1048576 | tf_op jit(solution)/shard_map/hidden_and_forces/pallas_call | solution.py:613
  44.0 0.2 fold_x.1
  44.2 0.6 collective-permute-start.8
  44.8 3.6 %collective-permute-start.9 = (bf16[832,128]{1,0:T(8,128)(2,1)S(1)}, bf16[832,128]{1,0:T(8,128)(2,1)S(1)}, u32[]{:S(2)}, u32[]{:S(2)}) collective-permute-start(bf16[832,128]{1,0:T(8,128)(2,1)S(1)} %get-tuple-element.114), channel_id=1, source_target_pairs={{1,0},{2,1},{3,2},{4,3},{5,4},{6,5},{7,6},{0,7},{9,8},{10,9},{11,1... | collective-permute-start | bytes 638984 | tf_op jit(solution)/shard_map/ppermute | solution.py:633
  48.4 1.9 %collective-permute-start.11 = (f32[8,128]{1,0:T(8,128)S(1)}, f32[8,128]{1,0:T(8,128)S(1)}, u32[]{:S(2)}, u32[]{:S(2)}) collective-permute-start(f32[8,128]{1,0:T(8,128)S(1)} %get-tuple-element.115.mine_ref), channel_id=1, source_target_pairs={{32,0},{64,32},{96,64},{128,96},{160,128},{192,160},{224,192},{0,2... | collective-permute-start | bytes 12296 | tf_op jit(solution)/shard_map/ppermute | solution.py:633
  50.3 1.3 %collective-permute-done.11.hi_ref = f32[8,128]{1,0:T(8,128)S(1)} collective-permute-done((f32[8,128]{1,0:T(8,128)S(1)}, f32[8,128]{1,0:T(8,128)S(1)}, u32[]{:S(2)}, u32[]{:S(2)}) %collective-permute-start.11) | collective-permute-done | bytes 4128 | tf_op jit(solution)/shard_map/ppermute | solution.py:633
  51.6 2.9 %collective-permute-done.10.lo_ref = f32[8,128]{1,0:T(8,128)S(1)} collective-permute-done((f32[8,128]{1,0:T(8,128)S(1)}, f32[8,128]{1,0:T(8,128)S(1)}, u32[]{:S(2)}, u32[]{:S(2)}) %collective-permute-start.10) | collective-permute-done | bytes 4128 | tf_op jit(solution)/shard_map/ppermute | solution.py:633
  54.6 0.1 fold_force.1.force_ref
  54.6 1.5 %collective-permute-start.13 = (f32[8,128]{1,0:T(8,128)S(1)}, f32[8,128]{1,0:T(8,128)S(1)}, u32[]{:S(2)}, u32[]{:S(2)}) collective-permute-start(f32[8,128]{1,0:T(8,128)S(1)} %fold_force.1.force_ref), channel_id=1, source_target_pairs={{1,0},{2,1},{3,2},{4,3},{5,4},{6,5},{7,6},{0,7},{9,8},{10,9},{11,1... | collective-permute-start | bytes 12296 | tf_op jit(solution)/shard_map/ppermute | solution.py:633
  56.1 0.5 collective-permute-start.12
  56.7 1.6 %collective-permute-done.13.fhi_ref = f32[8,128]{1,0:T(8,128)S(1)} collective-permute-done((f32[8,128]{1,0:T(8,128)S(1)}, f32[8,128]{1,0:T(8,128)S(1)}, u32[]{:S(2)}, u32[]{:S(2)}) %collective-permute-start.13) | collective-permute-done | bytes 4128 | tf_op jit(solution)/shard_map/ppermute | solution.py:633
  58.3 3.8 %collective-permute-done.12.flo_ref = f32[8,128]{1,0:T(8,128)S(1)} collective-permute-done((f32[8,128]{1,0:T(8,128)S(1)}, f32[8,128]{1,0:T(8,128)S(1)}, u32[]{:S(2)}, u32[]{:S(2)}) %collective-permute-start.12) | collective-permute-done | bytes 4128 | tf_op jit(solution)/shard_map/ppermute | solution.py:633
  62.1 0.1 fold_z.1
  62.2 0.1 collective-permute-start.14
  62.3 4.1 %collective-permute-start.15 = (bf16[432,128]{1,0:T(8,128)(2,1)S(1)}, bf16[432,128]{1,0:T(8,128)(2,1)S(1)}, u32[]{:S(2)}, u32[]{:S(2)}) collective-permute-start(bf16[432,128]{1,0:T(8,128)(2,1)S(1)} %get-tuple-element.121), channel_id=1, source_target_pairs={{8,0},{16,8},{24,16},{0,24},{9,1},{17,9},{25,17},{1,25},{10,2},{18... | collective-permute-start | bytes 331784 | tf_op jit(solution)/shard_map/ppermute | solution.py:633
  66.4 2.9 %updated.1 = bf16[784,128]{1,0:T(8,128)(2,1)} custom-call(bf16[784,128]{1,0:T(8,128)(2,1)S(1)} %bitcast.29, bf16[24,64,256]{2,1,0:T(8,128)(2,1)S(1)} %get-tuple-element.88.v_ref, bf16[24,256,128]{2,1,0:T(8,128)(2,1)S(1)} %get-tuple-element.118.h_ref, f32[24,256]{1,0:T(8,128)S(1)} %get-tuple-element.119.envl_ref, s32[2,2,2]{2,1,0:T(2,128)S(1)} %copy-done.8), custom_call_target="tpu_custom_call" | custom-call | flops 2000000000 | bytes 1048576 | tf_op jit(solution)/shard_map/updated/pallas_call | solution.py:620
  69.4 1.0 %collective-permute-done.14.lo_ref = bf16[432,128]{1,0:T(8,128)(2,1)S(1)} collective-permute-done((bf16[432,128]{1,0:T(8,128)(2,1)S(1)}, bf16[432,128]{1,0:T(8,128)(2,1)S(1)}, u32[]{:S(2)}, u32[]{:S(2)}) %collective-permute-start.14) | collective-permute-done | bytes 110624 | tf_op jit(solution)/shard_map/ppermute | solution.py:633
  70.3 0.9 %fold_y.1 = (f32[784,128]{1,0:T(8,128)}, f32[16,3]{1,0:T(8,128)}) custom-call(f32[832,128]{1,0:T(8,128)S(1)} %get-tuple-element.123.mid_ref, f32[8,128]{1,0:T(8,128)S(1)} %get-tuple-element.124.force_ref, bf16[432,128]{1,0:T(8,128)(2,1)S(1)} %collective-permute-done.14.lo_ref, bf16[432,128]{1,0:T(8,128)(2,1)S(1)} %collective-permute-done.15.hi_ref), custom_call_target="tpu_custom_call" | custom-call | flops 1000000000 | bytes 1048576 | tf_op jit(solution)/shard_map/fold_y/pallas_call | solution.py:699
  (22 shorter events, 0.1 us)
Async XLA Ops:
  1.7 11.1 %collective-permute-start.1 = (bf16[2,1,2,49,2,128]{5,4,3,2,1,0:T(2,128)(2,1)S(1)}, bf16[2,1,2,49,2,128]{5,4,3,2,1,0:T(2,128)(2,1)S(1)}, u32[]{:S(2)}, u32[]{:S(2)}) collective-permute-start(bf16[2,1,2,49,2,128]{5,4,3,2,1,0:T(2,128)(2,1)S(1)} %get-tuple-element.143), channel_id=1, source_target_pairs={{8,0},{16,8},{24,16},{0,24},{9,1},{17,9},{25,17},{1,25},{10,2},{18... | collective-permute-start | bytes 301064 | tf_op jit(solution)/shard_map/ppermute | solution.py:633
  7.2 8.6 %collective-permute-start = (bf16[2,1,2,49,2,128]{5,4,3,2,1,0:T(2,128)(2,1)S(1)}, bf16[2,1,2,49,2,128]{5,4,3,2,1,0:T(2,128)(2,1)S(1)}, u32[]{:S(2)}, u32[]{:S(2)}) collective-permute-start(bf16[2,1,2,49,2,128]{5,4,3,2,1,0:T(2,128)(2,1)S(1)} %get-tuple-element.144), channel_id=1, source_target_pairs={{0,8},{8,16},{16,24},{24,0},{1,9},{9,17},{17,25},{25,1},{2,10},{10... | collective-permute-start | bytes 301064 | tf_op jit(solution)/shard_map/ppermute | solution.py:633
  8.2 7.5 %copy-start = (bf16[2,2,2,2,49,128]{5,3,4,2,1,0:T(2,128)(2,1)S(1)}, bf16[2,2,2,2,49,128]{5,3,4,2,1,0:T(2,128)(2,1)}, u32[]{:S(2)}) copy-start(bf16[2,2,2,2,49,128]{5,3,4,2,1,0:T(2,128)(2,1)} %param.13) | copy-start | bytes 602116
  8.2 12.6 %copy-start.1 = (bf16[2,768,768]{2,1,0:T(8,128)(2,1)S(1)}, bf16[2,768,768]{2,1,0:T(8,128)(2,1)}, u32[]{:S(2)}) copy-start(bf16[2,768,768]{2,1,0:T(8,128)(2,1)} %w1v.3) | copy-start | bytes 7077892
  8.2 12.6 %copy-start.2 = (bf16[2,640,640]{2,1,0:T(8,128)(2,1)S(1)}, bf16[2,640,640]{2,1,0:T(8,128)(2,1)}, u32[]{:S(2)}) copy-start(bf16[2,640,640]{2,1,0:T(8,128)(2,1)} %w2v.3) | copy-start | bytes 4915204
  12.8 8.0 %copy-start.3 = (bf16[896,896]{1,0:T(8,128)(2,1)S(1)}, bf16[896,896]{1,0:T(8,128)(2,1)}, u32[]{:S(2)}) copy-start(bf16[896,896]{1,0:T(8,128)(2,1)} %w0v.3) | copy-start | bytes 4816900
  16.6 8.6 %collective-permute-start.2 = (bf16[2,4,1,49,2,128]{5,4,3,2,1,0:T(2,128)(2,1)S(1)}, bf16[2,4,1,49,2,128]{5,4,3,2,1,0:T(2,128)(2,1)S(1)}, u32[]{:S(2)}, u32[]{:S(2)}) collective-permute-start(bf16[2,4,1,49,2,128]{5,4,3,2,1,0:T(2,128)(2,1)S(1)} %get-tuple-element.90), channel_id=1, source_target_pairs={{0,1},{1,2},{2,3},{3,4},{4,5},{5,6},{6,7},{7,0},{8,9},{9,10},{10,1... | collective-permute-start | bytes 602120 | tf_op jit(solution)/shard_map/ppermute | solution.py:633
  18.3 6.9 %collective-permute-start.3 = (bf16[2,4,1,49,2,128]{5,4,3,2,1,0:T(2,128)(2,1)S(1)}, bf16[2,4,1,49,2,128]{5,4,3,2,1,0:T(2,128)(2,1)S(1)}, u32[]{:S(2)}, u32[]{:S(2)}) collective-permute-start(bf16[2,4,1,49,2,128]{5,4,3,2,1,0:T(2,128)(2,1)S(1)} %get-tuple-element.91), channel_id=1, source_target_pairs={{1,0},{2,1},{3,2},{4,3},{5,4},{6,5},{7,6},{0,7},{9,8},{10,9},{11,1... | collective-permute-start | bytes 602120 | tf_op jit(solution)/shard_map/ppermute | solution.py:633
  24.9 4.8 %copy-start.6 = (f32[3,2,2,2,2,12]{5,4,3,2,1,0:T(2,128)S(1)}, f32[3,2,2,2,2,12]{5,4,3,2,1,0:T(2,128)}, u32[]{:S(2)}) copy-start(f32[3,2,2,2,2,12]{5,4,3,2,1,0:T(2,128)} %param.19) | copy-start | bytes 6916
  24.9 4.8 %copy-start.7 = (s32[2,2,2,2,12]{4,3,2,1,0:T(2,128)S(1)}, s32[2,2,2,2,12]{4,3,2,1,0:T(2,128)}, u32[]{:S(2)}) copy-start(s32[2,2,2,2,12]{4,3,2,1,0:T(2,128)} %param.16) | copy-start | bytes 2308
  24.9 4.7 %copy-start.8 = (s32[2,2,2]{2,1,0:T(2,128)S(1)}, s32[2,2,2]{2,1,0:T(2,128)}, u32[]{:S(2)}) copy-start(s32[2,2,2]{2,1,0:T(2,128)} %counts_ref.3) | copy-start | bytes 100
  26.7 11.0 %collective-permute-start.4 = (bf16[1,4,4,49,2,128]{5,4,3,2,1,0:T(2,128)(2,1)S(1)}, bf16[1,4,4,49,2,128]{5,4,3,2,1,0:T(2,128)(2,1)S(1)}, u32[]{:S(2)}, u32[]{:S(2)}) collective-permute-start(bf16[1,4,4,49,2,128]{5,4,3,2,1,0:T(2,128)(2,1)S(1)} %pad_maximum_fusion.1), channel_id=1, source_target_pairs={{0,32},{32,64},{64,96},{96,128},{128,160},{160,192},{192,224},{224... | collective-permute-start | bytes 1204232 | tf_op jit(solution)/shard_map/ppermute | solution.py:633
  26.7 11.0 %collective-permute-start.5 = (bf16[1,4,4,49,2,128]{5,4,3,2,1,0:T(2,128)(2,1)S(1)}, bf16[1,4,4,49,2,128]{5,4,3,2,1,0:T(2,128)(2,1)S(1)}, u32[]{:S(2)}, u32[]{:S(2)}) collective-permute-start(bf16[1,4,4,49,2,128]{5,4,3,2,1,0:T(2,128)(2,1)S(1)} %pad_maximum_fusion.2), channel_id=1, source_target_pairs={{32,0},{64,32},{96,64},{128,96},{160,128},{192,160},{224,192},{0,2... | collective-permute-start | bytes 1204232 | tf_op jit(solution)/shard_map/ppermute | solution.py:633
  29.7 8.0 %copy-start.4 = (f32[128,896]{1,0:T(8,128)S(1)}, f32[128,896]{1,0:T(8,128)}, u32[]{:S(2)}) copy-start(f32[128,896]{1,0:T(8,128)} %rout_ref.1) | copy-start | bytes 1376260
  29.7 8.0 %copy-start.5 = (f32[256,128]{1,0:T(8,128)S(1)}, f32[256,128]{1,0:T(8,128)}, u32[]{:S(2)}) copy-start(f32[256,128]{1,0:T(8,128)} %rin_ref.1) | copy-start | bytes 393220
  29.7 8.0 %copy-start.9 = (s32[64]{0:T(128)S(1)}, s32[64]{0:T(128)}, u32[]{:S(2)}) copy-start(s32[64]{0:T(128)} %constant.5.clone.base_ref) | copy-start | bytes 772
  34.7 9.3 %collective-permute-start.6 = (bf16[1664,128]{1,0:T(8,128)(2,1)S(1)}, bf16[1664,128]{1,0:T(8,128)(2,1)S(1)}, u32[]{:S(2)}, u32[]{:S(2)}) collective-permute-start(bf16[1664,128]{1,0:T(8,128)(2,1)S(1)} %get-tuple-element.108), channel_id=1, source_target_pairs={{0,32},{32,64},{64,96},{96,128},{128,160},{160,192},{192,224},{224... | collective-permute-start | bytes 1277960 | tf_op jit(solution)/shard_map/ppermute | solution.py:633
  34.8 9.3 %collective-permute-start.7 = (bf16[1664,128]{1,0:T(8,128)(2,1)S(1)}, bf16[1664,128]{1,0:T(8,128)(2,1)S(1)}, u32[]{:S(2)}, u32[]{:S(2)}) collective-permute-start(bf16[1664,128]{1,0:T(8,128)(2,1)S(1)} %get-tuple-element.109), channel_id=1, source_target_pairs={{32,0},{64,32},{96,64},{128,96},{160,128},{192,160},{224,192},{0,2... | collective-permute-start | bytes 1277960 | tf_op jit(solution)/shard_map/ppermute | solution.py:633
  44.2 17.9 %collective-permute-start.8 = (bf16[832,128]{1,0:T(8,128)(2,1)S(1)}, bf16[832,128]{1,0:T(8,128)(2,1)S(1)}, u32[]{:S(2)}, u32[]{:S(2)}) collective-permute-start(bf16[832,128]{1,0:T(8,128)(2,1)S(1)} %get-tuple-element.113), channel_id=1, source_target_pairs={{0,1},{1,2},{2,3},{3,4},{4,5},{5,6},{6,7},{7,0},{8,9},{9,10},{10,1... | collective-permute-start | bytes 638984 | tf_op jit(solution)/shard_map/ppermute | solution.py:633
  44.8 17.3 %collective-permute-start.9 = (bf16[832,128]{1,0:T(8,128)(2,1)S(1)}, bf16[832,128]{1,0:T(8,128)(2,1)S(1)}, u32[]{:S(2)}, u32[]{:S(2)}) collective-permute-start(bf16[832,128]{1,0:T(8,128)(2,1)S(1)} %get-tuple-element.114), channel_id=1, source_target_pairs={{1,0},{2,1},{3,2},{4,3},{5,4},{6,5},{7,6},{0,7},{9,8},{10,9},{11,1... | collective-permute-start | bytes 638984 | tf_op jit(solution)/shard_map/ppermute | solution.py:633
  48.4 3.2 %collective-permute-start.11 = (f32[8,128]{1,0:T(8,128)S(1)}, f32[8,128]{1,0:T(8,128)S(1)}, u32[]{:S(2)}, u32[]{:S(2)}) collective-permute-start(f32[8,128]{1,0:T(8,128)S(1)} %get-tuple-element.115.mine_ref), channel_id=1, source_target_pairs={{32,0},{64,32},{96,64},{128,96},{160,128},{192,160},{224,192},{0,2... | collective-permute-start | bytes 12296 | tf_op jit(solution)/shard_map/ppermute | solution.py:633
  50.3 4.2 %collective-permute-start.10 = (f32[8,128]{1,0:T(8,128)S(1)}, f32[8,128]{1,0:T(8,128)S(1)}, u32[]{:S(2)}, u32[]{:S(2)}) collective-permute-start(f32[8,128]{1,0:T(8,128)S(1)} %get-tuple-element.115.mine_ref), channel_id=1, source_target_pairs={{0,32},{32,64},{64,96},{96,128},{128,160},{160,192},{192,224},{224... | collective-permute-start | bytes 12296 | tf_op jit(solution)/shard_map/ppermute | solution.py:633
  54.6 3.6 %collective-permute-start.13 = (f32[8,128]{1,0:T(8,128)S(1)}, f32[8,128]{1,0:T(8,128)S(1)}, u32[]{:S(2)}, u32[]{:S(2)}) collective-permute-start(f32[8,128]{1,0:T(8,128)S(1)} %fold_force.1.force_ref), channel_id=1, source_target_pairs={{1,0},{2,1},{3,2},{4,3},{5,4},{6,5},{7,6},{0,7},{9,8},{10,9},{11,1... | collective-permute-start | bytes 12296 | tf_op jit(solution)/shard_map/ppermute | solution.py:633
  56.1 6.0 %collective-permute-start.12 = (f32[8,128]{1,0:T(8,128)S(1)}, f32[8,128]{1,0:T(8,128)S(1)}, u32[]{:S(2)}, u32[]{:S(2)}) collective-permute-start(f32[8,128]{1,0:T(8,128)S(1)} %fold_force.1.force_ref), channel_id=1, source_target_pairs={{0,1},{1,2},{2,3},{3,4},{4,5},{5,6},{6,7},{7,0},{8,9},{9,10},{10,1... | collective-permute-start | bytes 12296 | tf_op jit(solution)/shard_map/ppermute | solution.py:633
  62.2 8.1 %collective-permute-start.14 = (bf16[432,128]{1,0:T(8,128)(2,1)S(1)}, bf16[432,128]{1,0:T(8,128)(2,1)S(1)}, u32[]{:S(2)}, u32[]{:S(2)}) collective-permute-start(bf16[432,128]{1,0:T(8,128)(2,1)S(1)} %get-tuple-element.120), channel_id=1, source_target_pairs={{0,8},{8,16},{16,24},{24,0},{1,9},{9,17},{17,25},{25,1},{2,10},{10... | collective-permute-start | bytes 331784 | tf_op jit(solution)/shard_map/ppermute | solution.py:633
  62.3 8.0 %collective-permute-start.15 = (bf16[432,128]{1,0:T(8,128)(2,1)S(1)}, bf16[432,128]{1,0:T(8,128)(2,1)S(1)}, u32[]{:S(2)}, u32[]{:S(2)}) collective-permute-start(bf16[432,128]{1,0:T(8,128)(2,1)S(1)} %get-tuple-element.121), channel_id=1, source_target_pairs={{8,0},{16,8},{24,16},{0,24},{9,1},{17,9},{25,17},{1,25},{10,2},{18... | collective-permute-start | bytes 331784 | tf_op jit(solution)/shard_map/ppermute | solution.py:633

commit v3 on v2

--- a/solution.py
+++ b/solution.py
@@ -246,7 +246,7 @@
                         zs[z][pl.ds(row + up, 16), col : col + 128] = both[2 * q + h]
         return carry
 
-    lax.fori_loop(0, 4, rotate, 0)
+    lax.fori_loop(0, 4, rotate, 0, unroll=True)
 
 
 def halves(k0, k1):
@@ -264,7 +264,7 @@
         u4_ref[g, 1] = b.reshape(128, 128).astype(bf16)
         return carry
 
-    lax.fori_loop(0, G, turn, 0)
+    lax.fori_loop(0, G, turn, 0, unroll=4)
     zs = (z0_ref, z1_ref, z2_ref)
     gr_ref[:, 240:256, :] = jnp.zeros((G, 16, 128), bf16)
     z0 = z0_ref[...]
@@ -328,7 +328,7 @@
                 acc_ref[pl.ds(row, 56, 2), :] += res[64 * e : 64 * e + 56]
         return carry
 
-    lax.fori_loop(0, 8, back, 0)
+    lax.fori_loop(0, 8, back, 0, unroll=2)
     xlo_ref[...] = acc_ref[0 : 16 * CR, :].astype(bf16)
     xhi_ref[...] = acc_ref[48 * CR : 64 * CR, :].astype(bf16)
     mid_ref[...] = acc_ref[16 * CR : 48 * CR, :]
@@ -385,7 +385,7 @@
                     xs[z][pl.ds(row + up, 16), col : col + 128] = value.astype(bf16)
         return carry
 
-    lax.fori_loop(0, 4, rotate, 0)
+    lax.fori_loop(0, 4, rotate, 0, unroll=True)
     h_ref[:, 240:256, :] = jnp.zeros((G, 16, 128), bf16)
     along = jnp.zeros((E, 128), f32)
 
@@ -448,7 +448,7 @@
             us_ref[pl.ds(98 * cell + s, 56, 2), :] = (own + sums[64 * s : 64 * s + 56]) * occ
         return carry
 
-    lax.fori_loop(0, 8, back, 0)
+    lax.fori_loop(0, 8, back, 0, unroll=4)
     upd_ref[...] = us_ref[0:784, :].astype(bf16)
 
 
@@ -674,15 +674,15 @@
     lo, hi = exchange(gxhi, gxlo, "gx")
     rows = [p.reshape(-1, 128) for p in (feats, ylo, yhi, zlo, zhi, xlo, xhi)]
     h, force = run_b1(rows, src, (u4, z0, z1, z2, gi0, rad, dsilu, wb, ratio, side), rin, rout, w0, w1, w2)
-    h, force, lo, hi = tie(h, force, lo, hi)
+    h, lo, hi = tie(h, lo, hi)
     flo, fhi = exchange(force, force, "gx")
     gzlo, gzhi, mid = call(
         fold_x,
         [shape((8 * CR, 128), bf16), shape((8 * CR, 128), bf16), shape((16 * CR, 128), f32)],
-        [VM] * 3, [], 16 << 20, "fold_x", cost(4),
+        [VM] * 3, [], 16 << 20, "fold_x", cost(0.1),
     )(mid, lo, hi)
     lo, hi = exchange(gzhi, gzlo, "gz")
-    force = call(fold_force_x, shape((8, 128), f32), [VM] * 3, [], 8 << 20, "fold_force", cost(0.2))(force, flo, fhi)
+    force = call(fold_force_x, shape((8, 128), f32), [VM] * 3, [], 8 << 20, "fold_force", cost(4))(force, flo, fhi)
     flo, fhi = exchange(force, force, "gz")
     gylo, gyhi, mid, force = call(
         fold_z,

time: 71.3 us -> 66 us (0.926)
  Pallas kernels: 24 us -> 20.1 us
  waiting for transfers between devices: 13.6 us -> 10.5 us
  starting transfers between devices: 27.9 us -> 29 us
    ppermute x16, waiting for transfers between devices: 13.6 us -> 10.5 us  [exchange(): return (lax.ppermute(to_up, axis, up), lax.ppermute(to_down, axis, down))]
    ppermute x16, starting transfers between devices: 27.9 us -> 29 us  [exchange(): return (lax.ppermute(to_up, axis, up), lax.ppermute(to_down, axis, down))]
    pallas_call x1, Pallas kernels: 2.94 us -> 2.02 us  [run_b2(): call(kernel_b2, shape((784, 128), bf16), [VM] * 4 + [SM], scratch, 16 <<...]
    pallas_call x1, Pallas kernels: 6.27 us -> 5.38 us  [run_b1(): call(kernel_b1, out, specs, scratch, 28 << 20, 'hidden_and_forces', cost(7))]
    pallas_call x1, Pallas kernels: 4.03 us -> 3.2 us  [run_a2(): call(kernel_a2, out, [VM] * 8, [], 20 << 20, 'mix_backward', cost(4))]
    pallas_call x1, Pallas kernels: 5.03 us -> 4.21 us  [run_a3(): call(kernel_a3, out, [VM, VM, VM, SM, SM, VM, VM], scratch, 20 << 20, 'so...]
  transfers between devices with their start and end apart: 16 -> 16, of which waited for: 6 -> 6; matrix products, arithmetic and copies ran while one was open for 2% -> 2% of each run, Pallas kernels for 32% -> 29%
where the time goes in v3:
time: 66 us; the launch traced here: 65.2 us
  starting transfers between devices  29 us (44%)
  Pallas kernels  20.1 us (30%)
  waiting for transfers between devices  10.5 us (16%)
  local copies, waits for them, and re-layouts  2.99 us (5%)
  other arithmetic  1.75 us (3%)
  between operations  0.86 us (1%)
    ppermute x16, starting transfers between devices, exchange(): return (lax.ppermute(to_up, axis, up), lax.ppermute(to_down, axis, down))  29 us
    ppermute x16, waiting for transfers between devices, exchange(): return (lax.ppermute(to_up, axis, up), lax.ppermute(to_down, axis, down))  10.5 us
    pallas_call x1, Pallas kernels, run_b1(): call(kernel_b1, out, specs, scratch, 28 << 20, 'hidden_and_forces', cost(7))  5.38 us
    pallas_call x1, Pallas kernels, run_a3(): call(kernel_a3, out, [VM, VM, VM, SM, SM, VM, VM], scratch, 20 << 20, 'so...  4.21 us
    pallas_call x1, Pallas kernels, run_a1(): call(kernel_a1, out, [VM] + [HB] * 5, scratch, 24 << 20, 'rotations', cos...  4.09 us
    pallas_call x1, Pallas kernels, run_a2(): call(kernel_a2, out, [VM] * 8, [], 20 << 20, 'mix_backward', cost(4))  3.2 us
    pallas_call x1, Pallas kernels, run_b2(): call(kernel_b2, shape((784, 128), bf16), [VM] * 4 + [SM], scratch, 16 <<...  2.02 us
  transfers between devices with their start and end apart: 16, of which 6 were waited for; matrix products, arithmetic and copies ran while one was open for 2% of the time, Pallas kernels for 29%

profile of v3, /device:TPU:32, one launch (start us, length us, event | category | flops | bytes accessed | tf_op | source)
XLA Modules:
  0.0 65.2 jit_solution(12275983725391112911)
XLA Ops:
  0.6 1.1 %fusion.4 = (bf16[2,1,2,49,2,128]{5,4,3,2,1,0:T(2,128)(2,1)S(1)}, bf16[2,1,2,49,2,128]{5,4,3,2,1,0:T(2,128)(2,1)S(1)}) fusion(bf16[2,2,2,49,2,128]{5,4,3,2,1,0:T(2,128)(2,1)} %bitcast.26), kind=kLoop, calls=%fused_computation.7 | loop fusion | bytes 401408 | tf_op jit(solution)/shard_map/slice | solution.py:658
  1.7 5.5 %collective-permute-start.1 = (bf16[2,1,2,49,2,128]{5,4,3,2,1,0:T(2,128)(2,1)S(1)}, bf16[2,1,2,49,2,128]{5,4,3,2,1,0:T(2,128)(2,1)S(1)}, u32[]{:S(2)}, u32[]{:S(2)}) collective-permute-start(bf16[2,1,2,49,2,128]{5,4,3,2,1,0:T(2,128)(2,1)S(1)} %get-tuple-element.141), channel_id=1, source_target_pairs={{8,0},{16,8},{24,16},{0,24},{9,1},{17,9},{25,17},{1,25},{10,2},{18... | collective-permute-start | bytes 301064 | tf_op jit(solution)/shard_map/ppermute | solution.py:633
  7.2 0.0 collective-permute-start
  7.2 1.0 %reshape.52 = bf16[192,235]{1,0:T(8,128)(2,1)S(1)} reshape(bf16[2,2,2,12,2,235]{5,4,3,2,1,0:T(2,128)(2,1)} %bitcast.40) | data formatting | bytes 180480 | tf_op jit(solution)/shard_map/reshape | solution.py:651
  8.2 0.0 copy-start
  8.2 0.0 copy-start.1
  8.2 0.0 copy-start.2
  8.3 4.1 %rotations.1 = (bf16[24,256,128]{2,1,0:T(8,128)(2,1)S(1)}, bf16[192,896]{1,0:T(8,128)(2,1)S(1)}, bf16[384,768]{1,0:T(8,128)(2,1)S(1)}, bf16[384,640]{1,0:T(8,128...) custom-call(bf16[192,256]{1,0:T(8,128)(2,1)S(1)} %pad.4.wt_ref, ...), custom_call_target="tpu_custom_call" | custom-call | flops 6000000000 | bytes 1048576 | tf_op jit(solution)/shard_map/rotations/pallas_call | solution.py:582
  12.4 0.0 copy-start.3
  12.4 0.0 collective-permute-done.1
  12.4 3.4 %collective-permute-done = bf16[2,1,2,49,2,128]{5,4,3,2,1,0:T(2,128)(2,1)S(1)} collective-permute-done((bf16[2,1,2,49,2,128]{5,4,3,2,1,0:T(2,128)(2,1)S(1)}, bf16[2,1,2,49,2,128]{5,4,3,2,1,0:T(2,128)(2,1)S(1)}, u32[]{:S(2)}, u32[]{:S(2)}) %collective-permute-start) | collective-permute-done | bytes 100384 | tf_op jit(solution)/shard_map/ppermute | solution.py:633
  15.8 0.6 pad_maximum_fusion
  16.4 0.3 fusion.1
  16.6 1.7 %collective-permute-start.2 = (bf16[2,4,1,49,2,128]{5,4,3,2,1,0:T(2,128)(2,1)S(1)}, bf16[2,4,1,49,2,128]{5,4,3,2,1,0:T(2,128)(2,1)S(1)}, u32[]{:S(2)}, u32[]{:S(2)}) collective-permute-start(bf16[2,4,1,49,2,128]{5,4,3,2,1,0:T(2,128)(2,1)S(1)} %get-tuple-element.89), channel_id=1, source_target_pairs={{0,1},{1,2},{2,3},{3,4},{4,5},{5,6},{6,7},{7,0},{8,9},{9,10},{10,1... | collective-permute-start | bytes 602120 | tf_op jit(solution)/shard_map/ppermute | solution.py:633
  18.3 2.6 %collective-permute-start.3 = (bf16[2,4,1,49,2,128]{5,4,3,2,1,0:T(2,128)(2,1)S(1)}, bf16[2,4,1,49,2,128]{5,4,3,2,1,0:T(2,128)(2,1)S(1)}, u32[]{:S(2)}, u32[]{:S(2)}) collective-permute-start(bf16[2,4,1,49,2,128]{5,4,3,2,1,0:T(2,128)(2,1)S(1)} %get-tuple-element.90), channel_id=1, source_target_pairs={{1,0},{2,1},{3,2},{4,3},{5,4},{6,5},{7,6},{0,7},{9,8},{10,9},{11,1... | collective-permute-start | bytes 602120 | tf_op jit(solution)/shard_map/ppermute | solution.py:633
  20.9 3.2 %mix_backward.1 = (f32[192,896]{1,0:T(8,128)S(1)}, bf16[24,256,128]{2,1,0:T(8,128)(2,1)S(1)}, bf16[24,64,256]{2,1,0:T(8,128)(2,1)S(1)}, bf16[24,2,128,128]{3,2,1,0:T(8,128)(2,1)S(1)}) custom-call(bf16[24,256,128]{2,1,0:T(8,128)(2,1)S(1)} %get-tuple-element.82.u_ref, bf16[192,896]{1,0:T(8,128)(2,1)S(1)} %get-tuple-element.83.z0_ref.g0_ref, ...), custom_call_target="tpu_custom_call" | custom-call | flops 4000000000 | bytes 1048576 | tf_op jit(solution)/shard_map/mix_backward/pallas_call | solution.py:591
  24.1 0.0 copy-start.6
  24.1 0.0 copy-start.7
  24.1 0.0 copy-start.8
  24.1 0.3 fusion
  24.4 0.6 collective-permute-done.2
  25.0 0.3 fusion.2
  25.3 0.6 pad_maximum_fusion.2
  25.9 0.6 pad_maximum_fusion.1
  26.5 0.0 collective-permute-start.4
  26.5 2.9 %collective-permute-start.5 = (bf16[1,4,4,49,2,128]{5,4,3,2,1,0:T(2,128)(2,1)S(1)}, bf16[1,4,4,49,2,128]{5,4,3,2,1,0:T(2,128)(2,1)S(1)}, u32[]{:S(2)}, u32[]{:S(2)}) collective-permute-start(bf16[1,4,4,49,2,128]{5,4,3,2,1,0:T(2,128)(2,1)S(1)} %pad_maximum_fusion.2), channel_id=1, source_target_pairs={{32,0},{64,32},{96,64},{128,96},{160,128},{192,160},{224,192},{0,2... | collective-permute-start | bytes 1204232 | tf_op jit(solution)/shard_map/ppermute | solution.py:633
  29.4 0.0 copy-start.5
  29.4 0.0 copy-start.9
  29.5 4.2 %source_gradients.1 = (bf16[1664,128]{1,0:T(8,128)(2,1)S(1)}, bf16[1664,128]{1,0:T(8,128)(2,1)S(1)}, f32[3328,128]{1,0:T(8,128)S(1)}, f32[3,192,128]{2,1,0:T(8,128)S(1)}) custom-call(bf16[24,64,256]{2,1,0:T(8,128)(2,1)S(1)} %get-tuple-element.87.v_ref, bf16[24,256,128]{2,1,0:T(8,128)(2,1)S(1)} %get-tuple-element.94.gr_ref, ...), custom_call_target="tpu_custom_call" | custom-call | flops 5000000000 | bytes 1048576 | tf_op jit(solution)/shard_map/source_gradients/pallas_call | solution.py:600
  33.7 0.0 collective-permute-start.6
  33.7 2.9 %collective-permute-start.7 = (bf16[1664,128]{1,0:T(8,128)(2,1)S(1)}, bf16[1664,128]{1,0:T(8,128)(2,1)S(1)}, u32[]{:S(2)}, u32[]{:S(2)}) collective-permute-start(bf16[1664,128]{1,0:T(8,128)(2,1)S(1)} %get-tuple-element.107), channel_id=1, source_target_pairs={{32,0},{64,32},{96,64},{128,96},{160,128},{192,160},{224,192},{0,2... | collective-permute-start | bytes 1277960 | tf_op jit(solution)/shard_map/ppermute | solution.py:633
  36.7 5.4 %hidden_and_forces.1 = (bf16[24,256,128]{2,1,0:T(8,128)(2,1)S(1)}, f32[8,128]{1,0:T(8,128)S(1)}) custom-call(bf16[784,128]{1,0:T(8,128)(2,1)S(1)} %bitcast.28, bf16[392,128]{1,0:T(8,128)(2,1)S(1)} %bitcast.33, bf16[392,128]{1,0:T(8,128)(2,1)S(1)} %bitcast.32, bf16[784,128]{1,0:T(8,128)(2,1)S(1)} %bitcast.30, bf16[784,128]{1,0:T(8,128)(2,1)S(1)} %bitcast.31, ...), custom_call_target="tpu_custom_call" | custom-call | flops 7000000000 | bytes 1048576 | tf_op jit(solution)/shard_map/hidden_and_forces/pallas_call | solution.py:613
  42.1 1.3 %collective-permute-start.11 = (f32[8,128]{1,0:T(8,128)S(1)}, f32[8,128]{1,0:T(8,128)S(1)}, u32[]{:S(2)}, u32[]{:S(2)}) collective-permute-start(f32[8,128]{1,0:T(8,128)S(1)} %get-tuple-element.113.mine_ref), channel_id=1, source_target_pairs={{32,0},{64,32},{96,64},{128,96},{160,128},{192,160},{224,192},{0,2... | collective-permute-start | bytes 12296 | tf_op jit(solution)/shard_map/ppermute | solution.py:633
  43.3 0.2 fold_x.1
  43.5 0.8 %collective-permute-start.8 = (bf16[832,128]{1,0:T(8,128)(2,1)S(1)}, bf16[832,128]{1,0:T(8,128)(2,1)S(1)}, u32[]{:S(2)}, u32[]{:S(2)}) collective-permute-start(bf16[832,128]{1,0:T(8,128)(2,1)S(1)} %get-tuple-element.111), channel_id=1, source_target_pairs={{0,1},{1,2},{2,3},{3,4},{4,5},{5,6},{6,7},{7,0},{8,9},{9,10},{10,1... | collective-permute-start | bytes 638984 | tf_op jit(solution)/shard_map/ppermute | solution.py:633
  44.3 3.4 %collective-permute-start.9 = (bf16[832,128]{1,0:T(8,128)(2,1)S(1)}, bf16[832,128]{1,0:T(8,128)(2,1)S(1)}, u32[]{:S(2)}, u32[]{:S(2)}) collective-permute-start(bf16[832,128]{1,0:T(8,128)(2,1)S(1)} %get-tuple-element.112), channel_id=1, source_target_pairs={{1,0},{2,1},{3,2},{4,3},{5,4},{6,5},{7,6},{0,7},{9,8},{10,9},{11,1... | collective-permute-start | bytes 638984 | tf_op jit(solution)/shard_map/ppermute | solution.py:633
  47.7 0.1 fold_force.1.force_ref
  47.8 3.7 %collective-permute-start.13 = (f32[8,128]{1,0:T(8,128)S(1)}, f32[8,128]{1,0:T(8,128)S(1)}, u32[]{:S(2)}, u32[]{:S(2)}) collective-permute-start(f32[8,128]{1,0:T(8,128)S(1)} %fold_force.1.force_ref), channel_id=1, source_target_pairs={{1,0},{2,1},{3,2},{4,3},{5,4},{6,5},{7,6},{0,7},{9,8},{10,9},{11,1... | collective-permute-start | bytes 12296 | tf_op jit(solution)/shard_map/ppermute | solution.py:633
  51.5 0.0 collective-permute-start.12
  51.5 1.3 %collective-permute-done.13.fhi_ref = f32[8,128]{1,0:T(8,128)S(1)} collective-permute-done((f32[8,128]{1,0:T(8,128)S(1)}, f32[8,128]{1,0:T(8,128)S(1)}, u32[]{:S(2)}, u32[]{:S(2)}) %collective-permute-start.13) | collective-permute-done | bytes 4128 | tf_op jit(solution)/shard_map/ppermute | solution.py:633
  52.8 4.4 %collective-permute-done.12.flo_ref = f32[8,128]{1,0:T(8,128)S(1)} collective-permute-done((f32[8,128]{1,0:T(8,128)S(1)}, f32[8,128]{1,0:T(8,128)S(1)}, u32[]{:S(2)}, u32[]{:S(2)}) %collective-permute-start.12) | collective-permute-done | bytes 4128 | tf_op jit(solution)/shard_map/ppermute | solution.py:633
  57.2 0.1 fold_z.1
  57.3 0.1 collective-permute-start.14
  57.4 4.1 %collective-permute-start.15 = (bf16[432,128]{1,0:T(8,128)(2,1)S(1)}, bf16[432,128]{1,0:T(8,128)(2,1)S(1)}, u32[]{:S(2)}, u32[]{:S(2)}) collective-permute-start(bf16[432,128]{1,0:T(8,128)(2,1)S(1)} %get-tuple-element.119), channel_id=1, source_target_pairs={{8,0},{16,8},{24,16},{0,24},{9,1},{17,9},{25,17},{1,25},{10,2},{18... | collective-permute-start | bytes 331784 | tf_op jit(solution)/shard_map/ppermute | solution.py:633
  61.5 2.0 %updated.1 = bf16[784,128]{1,0:T(8,128)(2,1)} custom-call(bf16[784,128]{1,0:T(8,128)(2,1)S(1)} %bitcast.29, bf16[24,64,256]{2,1,0:T(8,128)(2,1)S(1)} %get-tuple-element.87.v_ref, bf16[24,256,128]{2,1,0:T(8,128)(2,1)S(1)} %get-tuple-element.116.h_ref, f32[24,256]{1,0:T(8,128)S(1)} %get-tuple-element.117.envl_ref, s32[2,2,2]{2,1,0:T(2,128)S(1)} %copy-done.8), custom_call_target="tpu_custom_call" | custom-call | flops 2000000000 | bytes 1048576 | tf_op jit(solution)/shard_map/updated/pallas_call | solution.py:620
  63.6 0.7 %collective-permute-done.14.lo_ref = bf16[432,128]{1,0:T(8,128)(2,1)S(1)} collective-permute-done((bf16[432,128]{1,0:T(8,128)(2,1)S(1)}, bf16[432,128]{1,0:T(8,128)(2,1)S(1)}, u32[]{:S(2)}, u32[]{:S(2)}) %collective-permute-start.14) | collective-permute-done | bytes 110624 | tf_op jit(solution)/shard_map/ppermute | solution.py:633
  64.3 0.1 collective-permute-done.15.hi_ref
  64.4 0.9 %fold_y.1 = (f32[784,128]{1,0:T(8,128)}, f32[16,3]{1,0:T(8,128)}) custom-call(f32[832,128]{1,0:T(8,128)S(1)} %get-tuple-element.121.mid_ref, f32[8,128]{1,0:T(8,128)S(1)} %get-tuple-element.122.force_ref, bf16[432,128]{1,0:T(8,128)(2,1)S(1)} %collective-permute-done.14.lo_ref, bf16[432,128]{1,0:T(8,128)(2,1)S(1)} %collective-permute-done.15.hi_ref), custom_call_target="tpu_custom_call" | custom-call | flops 1000000000 | bytes 1048576 | tf_op jit(solution)/shard_map/fold_y/pallas_call | solution.py:699
  (22 shorter events, 0.1 us)
Async XLA Ops:
  1.7 10.6 %collective-permute-start.1 = (bf16[2,1,2,49,2,128]{5,4,3,2,1,0:T(2,128)(2,1)S(1)}, bf16[2,1,2,49,2,128]{5,4,3,2,1,0:T(2,128)(2,1)S(1)}, u32[]{:S(2)}, u32[]{:S(2)}) collective-permute-start(bf16[2,1,2,49,2,128]{5,4,3,2,1,0:T(2,128)(2,1)S(1)} %get-tuple-element.141), channel_id=1, source_target_pairs={{8,0},{16,8},{24,16},{0,24},{9,1},{17,9},{25,17},{1,25},{10,2},{18... | collective-permute-start | bytes 301064 | tf_op jit(solution)/shard_map/ppermute | solution.py:633
  7.2 8.6 %collective-permute-start = (bf16[2,1,2,49,2,128]{5,4,3,2,1,0:T(2,128)(2,1)S(1)}, bf16[2,1,2,49,2,128]{5,4,3,2,1,0:T(2,128)(2,1)S(1)}, u32[]{:S(2)}, u32[]{:S(2)}) collective-permute-start(bf16[2,1,2,49,2,128]{5,4,3,2,1,0:T(2,128)(2,1)S(1)} %get-tuple-element.142), channel_id=1, source_target_pairs={{0,8},{8,16},{16,24},{24,0},{1,9},{9,17},{17,25},{25,1},{2,10},{10... | collective-permute-start | bytes 301064 | tf_op jit(solution)/shard_map/ppermute | solution.py:633
  8.2 7.5 %copy-start = (bf16[2,2,2,2,49,128]{5,3,4,2,1,0:T(2,128)(2,1)S(1)}, bf16[2,2,2,2,49,128]{5,3,4,2,1,0:T(2,128)(2,1)}, u32[]{:S(2)}) copy-start(bf16[2,2,2,2,49,128]{5,3,4,2,1,0:T(2,128)(2,1)} %param.13) | copy-start | bytes 602116
  8.2 12.6 %copy-start.1 = (bf16[2,768,768]{2,1,0:T(8,128)(2,1)S(1)}, bf16[2,768,768]{2,1,0:T(8,128)(2,1)}, u32[]{:S(2)}) copy-start(bf16[2,768,768]{2,1,0:T(8,128)(2,1)} %w1v.3) | copy-start | bytes 7077892
  8.2 12.6 %copy-start.2 = (bf16[2,640,640]{2,1,0:T(8,128)(2,1)S(1)}, bf16[2,640,640]{2,1,0:T(8,128)(2,1)}, u32[]{:S(2)}) copy-start(bf16[2,640,640]{2,1,0:T(8,128)(2,1)} %w2v.3) | copy-start | bytes 4915204
  12.4 8.5 %copy-start.3 = (bf16[896,896]{1,0:T(8,128)(2,1)S(1)}, bf16[896,896]{1,0:T(8,128)(2,1)}, u32[]{:S(2)}) copy-start(bf16[896,896]{1,0:T(8,128)(2,1)} %w0v.3) | copy-start | bytes 4816900
  16.6 8.4 %collective-permute-start.2 = (bf16[2,4,1,49,2,128]{5,4,3,2,1,0:T(2,128)(2,1)S(1)}, bf16[2,4,1,49,2,128]{5,4,3,2,1,0:T(2,128)(2,1)S(1)}, u32[]{:S(2)}, u32[]{:S(2)}) collective-permute-start(bf16[2,4,1,49,2,128]{5,4,3,2,1,0:T(2,128)(2,1)S(1)} %get-tuple-element.89), channel_id=1, source_target_pairs={{0,1},{1,2},{2,3},{3,4},{4,5},{5,6},{6,7},{7,0},{8,9},{9,10},{10,1... | collective-permute-start | bytes 602120 | tf_op jit(solution)/shard_map/ppermute | solution.py:633
  18.3 6.7 %collective-permute-start.3 = (bf16[2,4,1,49,2,128]{5,4,3,2,1,0:T(2,128)(2,1)S(1)}, bf16[2,4,1,49,2,128]{5,4,3,2,1,0:T(2,128)(2,1)S(1)}, u32[]{:S(2)}, u32[]{:S(2)}) collective-permute-start(bf16[2,4,1,49,2,128]{5,4,3,2,1,0:T(2,128)(2,1)S(1)} %get-tuple-element.90), channel_id=1, source_target_pairs={{1,0},{2,1},{3,2},{4,3},{5,4},{6,5},{7,6},{0,7},{9,8},{10,9},{11,1... | collective-permute-start | bytes 602120 | tf_op jit(solution)/shard_map/ppermute | solution.py:633
  24.1 5.3 %copy-start.6 = (f32[3,2,2,2,2,12]{5,4,3,2,1,0:T(2,128)S(1)}, f32[3,2,2,2,2,12]{5,4,3,2,1,0:T(2,128)}, u32[]{:S(2)}) copy-start(f32[3,2,2,2,2,12]{5,4,3,2,1,0:T(2,128)} %param.19) | copy-start | bytes 6916
  24.1 5.3 %copy-start.7 = (s32[2,2,2,2,12]{4,3,2,1,0:T(2,128)S(1)}, s32[2,2,2,2,12]{4,3,2,1,0:T(2,128)}, u32[]{:S(2)}) copy-start(s32[2,2,2,2,12]{4,3,2,1,0:T(2,128)} %param.16) | copy-start | bytes 2308
  24.1 5.3 %copy-start.8 = (s32[2,2,2]{2,1,0:T(2,128)S(1)}, s32[2,2,2]{2,1,0:T(2,128)}, u32[]{:S(2)}) copy-start(s32[2,2,2]{2,1,0:T(2,128)} %counts_ref.3) | copy-start | bytes 100
  26.5 10.2 %collective-permute-start.4 = (bf16[1,4,4,49,2,128]{5,4,3,2,1,0:T(2,128)(2,1)S(1)}, bf16[1,4,4,49,2,128]{5,4,3,2,1,0:T(2,128)(2,1)S(1)}, u32[]{:S(2)}, u32[]{:S(2)}) collective-permute-start(bf16[1,4,4,49,2,128]{5,4,3,2,1,0:T(2,128)(2,1)S(1)} %pad_maximum_fusion.1), channel_id=1, source_target_pairs={{0,32},{32,64},{64,96},{96,128},{128,160},{160,192},{192,224},{224... | collective-permute-start | bytes 1204232 | tf_op jit(solution)/shard_map/ppermute | solution.py:633
  26.5 10.2 %collective-permute-start.5 = (bf16[1,4,4,49,2,128]{5,4,3,2,1,0:T(2,128)(2,1)S(1)}, bf16[1,4,4,49,2,128]{5,4,3,2,1,0:T(2,128)(2,1)S(1)}, u32[]{:S(2)}, u32[]{:S(2)}) collective-permute-start(bf16[1,4,4,49,2,128]{5,4,3,2,1,0:T(2,128)(2,1)S(1)} %pad_maximum_fusion.2), channel_id=1, source_target_pairs={{32,0},{64,32},{96,64},{128,96},{160,128},{192,160},{224,192},{0,2... | collective-permute-start | bytes 1204232 | tf_op jit(solution)/shard_map/ppermute | solution.py:633
  29.4 7.2 %copy-start.4 = (f32[128,896]{1,0:T(8,128)S(1)}, f32[128,896]{1,0:T(8,128)}, u32[]{:S(2)}) copy-start(f32[128,896]{1,0:T(8,128)} %rout_ref.1) | copy-start | bytes 1376260
  29.4 7.2 %copy-start.5 = (f32[256,128]{1,0:T(8,128)S(1)}, f32[256,128]{1,0:T(8,128)}, u32[]{:S(2)}) copy-start(f32[256,128]{1,0:T(8,128)} %rin_ref.1) | copy-start | bytes 393220
  29.4 7.2 %copy-start.9 = (s32[64]{0:T(128)S(1)}, s32[64]{0:T(128)}, u32[]{:S(2)}) copy-start(s32[64]{0:T(128)} %constant.5.clone.base_ref) | copy-start | bytes 772
  33.7 9.7 %collective-permute-start.6 = (bf16[1664,128]{1,0:T(8,128)(2,1)S(1)}, bf16[1664,128]{1,0:T(8,128)(2,1)S(1)}, u32[]{:S(2)}, u32[]{:S(2)}) collective-permute-start(bf16[1664,128]{1,0:T(8,128)(2,1)S(1)} %get-tuple-element.106), channel_id=1, source_target_pairs={{0,32},{32,64},{64,96},{96,128},{128,160},{160,192},{192,224},{224... | collective-permute-start | bytes 1277960 | tf_op jit(solution)/shard_map/ppermute | solution.py:633
  33.7 9.6 %collective-permute-start.7 = (bf16[1664,128]{1,0:T(8,128)(2,1)S(1)}, bf16[1664,128]{1,0:T(8,128)(2,1)S(1)}, u32[]{:S(2)}, u32[]{:S(2)}) collective-permute-start(bf16[1664,128]{1,0:T(8,128)(2,1)S(1)} %get-tuple-element.107), channel_id=1, source_target_pairs={{32,0},{64,32},{96,64},{128,96},{160,128},{192,160},{224,192},{0,2... | collective-permute-start | bytes 1277960 | tf_op jit(solution)/shard_map/ppermute | solution.py:633
  42.1 5.7 %collective-permute-start.11 = (f32[8,128]{1,0:T(8,128)S(1)}, f32[8,128]{1,0:T(8,128)S(1)}, u32[]{:S(2)}, u32[]{:S(2)}) collective-permute-start(f32[8,128]{1,0:T(8,128)S(1)} %get-tuple-element.113.mine_ref), channel_id=1, source_target_pairs={{32,0},{64,32},{96,64},{128,96},{160,128},{192,160},{224,192},{0,2... | collective-permute-start | bytes 12296 | tf_op jit(solution)/shard_map/ppermute | solution.py:633
  43.3 4.4 %collective-permute-start.10 = (f32[8,128]{1,0:T(8,128)S(1)}, f32[8,128]{1,0:T(8,128)S(1)}, u32[]{:S(2)}, u32[]{:S(2)}) collective-permute-start(f32[8,128]{1,0:T(8,128)S(1)} %get-tuple-element.113.mine_ref), channel_id=1, source_target_pairs={{0,32},{32,64},{64,96},{96,128},{128,160},{160,192},{192,224},{224... | collective-permute-start | bytes 12296 | tf_op jit(solution)/shard_map/ppermute | solution.py:633
  43.5 13.7 %collective-permute-start.8 = (bf16[832,128]{1,0:T(8,128)(2,1)S(1)}, bf16[832,128]{1,0:T(8,128)(2,1)S(1)}, u32[]{:S(2)}, u32[]{:S(2)}) collective-permute-start(bf16[832,128]{1,0:T(8,128)(2,1)S(1)} %get-tuple-element.111), channel_id=1, source_target_pairs={{0,1},{1,2},{2,3},{3,4},{4,5},{5,6},{6,7},{7,0},{8,9},{9,10},{10,1... | collective-permute-start | bytes 638984 | tf_op jit(solution)/shard_map/ppermute | solution.py:633
  44.3 12.9 %collective-permute-start.9 = (bf16[832,128]{1,0:T(8,128)(2,1)S(1)}, bf16[832,128]{1,0:T(8,128)(2,1)S(1)}, u32[]{:S(2)}, u32[]{:S(2)}) collective-permute-start(bf16[832,128]{1,0:T(8,128)(2,1)S(1)} %get-tuple-element.112), channel_id=1, source_target_pairs={{1,0},{2,1},{3,2},{4,3},{5,4},{6,5},{7,6},{0,7},{9,8},{10,9},{11,1... | collective-permute-start | bytes 638984 | tf_op jit(solution)/shard_map/ppermute | solution.py:633
  47.8 5.0 %collective-permute-start.13 = (f32[8,128]{1,0:T(8,128)S(1)}, f32[8,128]{1,0:T(8,128)S(1)}, u32[]{:S(2)}, u32[]{:S(2)}) collective-permute-start(f32[8,128]{1,0:T(8,128)S(1)} %fold_force.1.force_ref), channel_id=1, source_target_pairs={{1,0},{2,1},{3,2},{4,3},{5,4},{6,5},{7,6},{0,7},{9,8},{10,9},{11,1... | collective-permute-start | bytes 12296 | tf_op jit(solution)/shard_map/ppermute | solution.py:633
  51.5 5.7 %collective-permute-start.12 = (f32[8,128]{1,0:T(8,128)S(1)}, f32[8,128]{1,0:T(8,128)S(1)}, u32[]{:S(2)}, u32[]{:S(2)}) collective-permute-start(f32[8,128]{1,0:T(8,128)S(1)} %fold_force.1.force_ref), channel_id=1, source_target_pairs={{0,1},{1,2},{2,3},{3,4},{4,5},{5,6},{6,7},{7,0},{8,9},{9,10},{10,1... | collective-permute-start | bytes 12296 | tf_op jit(solution)/shard_map/ppermute | solution.py:633
  57.3 7.0 %collective-permute-start.14 = (bf16[432,128]{1,0:T(8,128)(2,1)S(1)}, bf16[432,128]{1,0:T(8,128)(2,1)S(1)}, u32[]{:S(2)}, u32[]{:S(2)}) collective-permute-start(bf16[432,128]{1,0:T(8,128)(2,1)S(1)} %get-tuple-element.118), channel_id=1, source_target_pairs={{0,8},{8,16},{16,24},{24,0},{1,9},{9,17},{17,25},{25,1},{2,10},{10... | collective-permute-start | bytes 331784 | tf_op jit(solution)/shard_map/ppermute | solution.py:633
  57.4 7.0 %collective-permute-start.15 = (bf16[432,128]{1,0:T(8,128)(2,1)S(1)}, bf16[432,128]{1,0:T(8,128)(2,1)S(1)}, u32[]{:S(2)}, u32[]{:S(2)}) collective-permute-start(bf16[432,128]{1,0:T(8,128)(2,1)S(1)} %get-tuple-element.119), channel_id=1, source_target_pairs={{8,0},{16,8},{24,16},{0,24},{9,1},{17,9},{25,17},{1,25},{10,2},{18... | collective-permute-start | bytes 331784 | tf_op jit(solution)/shard_map/ppermute | solution.py:633

commit v4 on v3

--- a/solution.py
+++ b/solution.py
@@ -62,7 +62,11 @@
         for py in range(4):
             for pz in range(4):
                 if px in (0, 3):
-                    at = 784 + 392 * 2 + 784 * 2 + (px == 3) * 1568 + (py * 4 + pz) * 98
+                    at = 784 + 392 * 2 + 784 * 2 + (px == 3) * 784
+                    if pz in (0, 3):
+                        at += 784 * 2 + (pz == 3) * 392 + py * 98
+                    else:
+                        at += (py * 2 + pz - 1) * 98
                 elif pz in (0, 3):
                     at = 784 + 392 * 2 + (pz == 3) * 784 + ((px - 1) * 4 + py) * 98
                 elif py in (0, 3):
@@ -335,14 +339,14 @@
 
 
 def kernel_b1(
-    own_ref, ylo_ref, yhi_ref, zlo_ref, zhi_ref, xlo_ref, xhi_ref, base_ref, src_ref,
+    own_ref, ylo_ref, yhi_ref, zlo_ref, zhi_ref, xlo_ref, xhi_ref, xzlo_ref, xzhi_ref, base_ref, src_ref,
     u4_ref, g0_ref, g1_ref, g2_ref, gi0_ref, rad_ref, dsilu_ref, wb_ref, ratio_ref, side_ref, rin_ref, rout_ref,
     w0v, w1v, w2v,
     h_ref, force_ref,
     fs_ref, x0_ref, x1_ref, x2_ref, p0_ref,
 ):
     at = 0
-    for piece in (own_ref, ylo_ref, yhi_ref, zlo_ref, zhi_ref, xlo_ref, xhi_ref):
+    for piece in (own_ref, ylo_ref, yhi_ref, zlo_ref, zhi_ref, xlo_ref, xhi_ref, xzlo_ref, xzhi_ref):
         n = piece.shape[0]
         fs_ref[at : at + n, :] = piece[...].astype(f32)
         at += n
@@ -609,7 +613,7 @@
         pltpu.VMEM((E, 896), bf16), pltpu.VMEM((2 * E, 768), bf16), pltpu.VMEM((2 * E, 640), bf16),
         pltpu.VMEM((E, 896), f32),
     ]
-    specs = [VM] * 7 + [SM, SM] + [VM] * 15
+    specs = [VM] * 9 + [SM, SM] + [VM] * 15
     return call(kernel_b1, out, specs, scratch, 28 << 20, "hidden_and_forces", cost(7))(
         *pieces, jnp.asarray(base_table()), src, *saved, rin, rout, w0, w1, w2
     )
@@ -663,16 +667,17 @@
     up, down = tall[:, :, 1:2], tall[:, :, 0:1]
     (u, z0, z1, z2, rad), up, down = tie((u, z0, z1, z2, rad), up, down)
     zlo, zhi = exchange(up, down, "gz")
+    xlo, xhi = exchange(tall[1:2], tall[0:1], "gx")
     gi0, gr, v, u4 = run_a2(u, z0, z1, z2, rad, w0, w1, w2)
     gr, zlo, zhi = tie(gr, zlo, zhi)
-    top = jnp.concatenate([zlo[1:2], tall[1:2], zhi[1:2]], axis=2)
-    low = jnp.concatenate([zlo[0:1], tall[0:1], zhi[0:1]], axis=2)
+    top = jnp.concatenate([zlo[1:2], zhi[1:2]], axis=0)
+    low = jnp.concatenate([zlo[0:1], zhi[0:1]], axis=0)
     gr, top, low = tie(gr, top, low)
-    xlo, xhi = exchange(top, low, "gx")
+    xzlo, xzhi = exchange(top, low, "gx")
     gxlo, gxhi, mid, side = run_a3(v, gr, cs, counts, src, dirs)
 
     lo, hi = exchange(gxhi, gxlo, "gx")
-    rows = [p.reshape(-1, 128) for p in (feats, ylo, yhi, zlo, zhi, xlo, xhi)]
+    rows = [p.reshape(-1, 128) for p in (feats, ylo, yhi, zlo, zhi, xlo, xhi, xzlo, xzhi)]
     h, force = run_b1(rows, src, (u4, z0, z1, z2, gi0, rad, dsilu, wb, ratio, side), rin, rout, w0, w1, w2)
     h, lo, hi = tie(h, lo, hi)
     flo, fhi = exchange(force, force, "gx")

time: 66 us -> 64.9 us (0.983)
    ppermute x16 -> x18, waiting for transfers between devices: 10.5 us -> 11 us  [exchange(): return (lax.ppermute(to_up, axis, up), lax.ppermute(to_down, axis, down))]
    ppermute x16 -> x18, starting transfers between devices: 29 us -> 28.6 us  [exchange(): return (lax.ppermute(to_up, axis, up), lax.ppermute(to_down, axis, down))]
  transfers between devices with their start and end apart: 16 -> 18, of which waited for: 6 -> 4; matrix products, arithmetic and copies ran while one was open for 2% -> 3% of each run, Pallas kernels for 29% -> 30%
where the time goes in v4:
time: 64.9 us; the launch traced here: 64.8 us
  starting transfers between devices  28.6 us (44%)
  Pallas kernels  20.1 us (31%)
  waiting for transfers between devices  11 us (17%)
  local copies, waits for them, and re-layouts  2.99 us (5%)
  other arithmetic  1.16 us (2%)
  between operations  0.91 us (1%)
    ppermute x18, starting transfers between devices, exchange(): return (lax.ppermute(to_up, axis, up), lax.ppermute(to_down, axis, down))  28.6 us
    ppermute x18, waiting for transfers between devices, exchange(): return (lax.ppermute(to_up, axis, up), lax.ppermute(to_down, axis, down))  11 us
    pallas_call x1, Pallas kernels, run_b1(): call(kernel_b1, out, specs, scratch, 28 << 20, 'hidden_and_forces', cost(7))  5.38 us
    pallas_call x1, Pallas kernels, run_a3(): call(kernel_a3, out, [VM, VM, VM, SM, SM, VM, VM], scratch, 20 << 20, 'so...  4.22 us
    pallas_call x1, Pallas kernels, run_a1(): call(kernel_a1, out, [VM] + [HB] * 5, scratch, 24 << 20, 'rotations', cos...  4.08 us
    pallas_call x1, Pallas kernels, run_a2(): call(kernel_a2, out, [VM] * 8, [], 20 << 20, 'mix_backward', cost(4))  3.19 us
    pallas_call x1, Pallas kernels, run_b2(): call(kernel_b2, shape((784, 128), bf16), [VM] * 4 + [SM], scratch, 16 <<...  2.03 us
  transfers between devices with their start and end apart: 18, of which 4 were waited for; matrix products, arithmetic and copies ran while one was open for 3% of the time, Pallas kernels for 30%

profile of v4, /device:TPU:32, one launch (start us, length us, event | category | flops | bytes accessed | tf_op | source)
XLA Modules:
  0.0 64.8 jit_solution(5528208793480617044)
XLA Ops:
  0.6 1.1 %fusion.4 = (bf16[2,1,2,49,2,128]{5,4,3,2,1,0:T(2,128)(2,1)S(1)}, bf16[2,1,2,49,2,128]{5,4,3,2,1,0:T(2,128)(2,1)S(1)}) fusion(bf16[2,2,2,49,2,128]{5,4,3,2,1,0:T(2,128)(2,1)} %bitcast.28), kind=kLoop, calls=%fused_computation.7 | loop fusion | bytes 401408 | tf_op jit(solution)/shard_map/slice | solution.py:662
  1.7 5.5 %collective-permute-start.1 = (bf16[2,1,2,49,2,128]{5,4,3,2,1,0:T(2,128)(2,1)S(1)}, bf16[2,1,2,49,2,128]{5,4,3,2,1,0:T(2,128)(2,1)S(1)}, u32[]{:S(2)}, u32[]{:S(2)}) collective-permute-start(bf16[2,1,2,49,2,128]{5,4,3,2,1,0:T(2,128)(2,1)S(1)} %get-tuple-element.141), channel_id=1, source_target_pairs={{8,0},{16,8},{24,16},{0,24},{9,1},{17,9},{25,17},{1,25},{10,2},{18... | collective-permute-start | bytes 301064 | tf_op jit(solution)/shard_map/ppermute | solution.py:637
  7.2 1.0 %reshape.58 = bf16[192,235]{1,0:T(8,128)(2,1)S(1)} reshape(bf16[2,2,2,12,2,235]{5,4,3,2,1,0:T(2,128)(2,1)} %bitcast.44) | data formatting | bytes 180480 | tf_op jit(solution)/shard_map/reshape | solution.py:655
  8.2 0.0 copy-start
  8.2 0.0 copy-start.2
  8.2 0.0 copy-start.3
  8.3 4.1 %rotations.1 = (bf16[24,256,128]{2,1,0:T(8,128)(2,1)S(1)}, bf16[192,896]{1,0:T(8,128)(2,1)S(1)}, bf16[384,768]{1,0:T(8,128)(2,1)S(1)}, bf16[384,640]{1,0:T(8,128...) custom-call(bf16[192,256]{1,0:T(8,128)(2,1)S(1)} %pad.4.wt_ref, ...), custom_call_target="tpu_custom_call" | custom-call | flops 6000000000 | bytes 1048576 | tf_op jit(solution)/shard_map/rotations/pallas_call | solution.py:586
  12.3 0.0 copy-start.1
  12.4 3.4 %collective-permute-done = bf16[2,1,2,49,2,128]{5,4,3,2,1,0:T(2,128)(2,1)S(1)} collective-permute-done((bf16[2,1,2,49,2,128]{5,4,3,2,1,0:T(2,128)(2,1)S(1)}, bf16[2,1,2,49,2,128]{5,4,3,2,1,0:T(2,128)(2,1)S(1)}, u32[]{:S(2)}, u32[]{:S(2)}) %collective-permute-start) | collective-permute-done | bytes 100384 | tf_op jit(solution)/shard_map/ppermute | solution.py:637
  15.8 0.6 pad_maximum_fusion
  16.4 0.3 fusion.1
  16.6 0.3 fusion
  16.9 1.7 %collective-permute-start.2 = (bf16[2,4,1,49,2,128]{5,4,3,2,1,0:T(2,128)(2,1)S(1)}, bf16[2,4,1,49,2,128]{5,4,3,2,1,0:T(2,128)(2,1)S(1)}, u32[]{:S(2)}, u32[]{:S(2)}) collective-permute-start(bf16[2,4,1,49,2,128]{5,4,3,2,1,0:T(2,128)(2,1)S(1)} %get-tuple-element.89), channel_id=1, source_target_pairs={{0,1},{1,2},{2,3},{3,4},{4,5},{5,6},{6,7},{7,0},{8,9},{9,10},{10,1... | collective-permute-start | bytes 602120 | tf_op jit(solution)/shard_map/ppermute | solution.py:637
  18.6 2.6 %collective-permute-start.3 = (bf16[2,4,1,49,2,128]{5,4,3,2,1,0:T(2,128)(2,1)S(1)}, bf16[2,4,1,49,2,128]{5,4,3,2,1,0:T(2,128)(2,1)S(1)}, u32[]{:S(2)}, u32[]{:S(2)}) collective-permute-start(bf16[2,4,1,49,2,128]{5,4,3,2,1,0:T(2,128)(2,1)S(1)} %get-tuple-element.90), channel_id=1, source_target_pairs={{1,0},{2,1},{3,2},{4,3},{5,4},{6,5},{7,6},{0,7},{9,8},{10,9},{11,1... | collective-permute-start | bytes 602120 | tf_op jit(solution)/shard_map/ppermute | solution.py:637
  21.1 1.1 %collective-permute-start.5 = (bf16[1,4,2,49,2,128]{5,4,3,2,1,0:T(2,128)(2,1)S(1)}, bf16[1,4,2,49,2,128]{5,4,3,2,1,0:T(2,128)(2,1)S(1)}, u32[]{:S(2)}, u32[]{:S(2)}) collective-permute-start(bf16[1,4,2,49,2,128]{5,4,3,2,1,0:T(2,128)(2,1)S(1)} %get-tuple-element.133), channel_id=1, source_target_pairs={{32,0},{64,32},{96,64},{128,96},{160,128},{192,160},{224,192},{0,2... | collective-permute-start | bytes 602120 | tf_op jit(solution)/shard_map/ppermute | solution.py:637
  22.2 3.2 %mix_backward.1 = (f32[192,896]{1,0:T(8,128)S(1)}, bf16[24,256,128]{2,1,0:T(8,128)(2,1)S(1)}, bf16[24,64,256]{2,1,0:T(8,128)(2,1)S(1)}, bf16[24,2,128,128]{3,2,1,0:T(8,128)(2,1)S(1)}) custom-call(bf16[24,256,128]{2,1,0:T(8,128)(2,1)S(1)} %get-tuple-element.82.u_ref, bf16[192,896]{1,0:T(8,128)(2,1)S(1)} %get-tuple-element.83.z0_ref.g0_ref, ...), custom_call_target="tpu_custom_call" | custom-call | flops 4000000000 | bytes 1048576 | tf_op jit(solution)/shard_map/mix_backward/pallas_call | solution.py:595
  25.4 0.0 copy-start.6
  25.5 0.0 copy-start.7
  25.5 0.0 copy-start.8
  25.5 0.0 collective-permute-done.3
  25.5 0.3 fusion.2
  25.8 0.3 pad_maximum_fusion.2
  26.1 0.3 pad_maximum_fusion.1
  26.4 0.5 collective-permute-start.6
  26.9 2.4 %collective-permute-start.7 = (bf16[2,4,1,49,2,128]{5,4,3,2,1,0:T(2,128)(2,1)S(1)}, bf16[2,4,1,49,2,128]{5,4,3,2,1,0:T(2,128)(2,1)S(1)}, u32[]{:S(2)}, u32[]{:S(2)}) collective-permute-start(bf16[2,4,1,49,2,128]{5,4,3,2,1,0:T(2,128)(2,1)S(1)} %pad_maximum_fusion.2), channel_id=1, source_target_pairs={{32,0},{64,32},{96,64},{128,96},{160,128},{192,160},{224,192},{0,2... | collective-permute-start | bytes 602120 | tf_op jit(solution)/shard_map/ppermute | solution.py:637
  29.4 0.0 copy-start.5
  29.4 0.0 copy-start.9
  29.4 4.2 %source_gradients.1 = (bf16[1664,128]{1,0:T(8,128)(2,1)S(1)}, bf16[1664,128]{1,0:T(8,128)(2,1)S(1)}, f32[3328,128]{1,0:T(8,128)S(1)}, f32[3,192,128]{2,1,0:T(8,128)S(1)}) custom-call(bf16[24,64,256]{2,1,0:T(8,128)(2,1)S(1)} %get-tuple-element.87.v_ref, bf16[24,256,128]{2,1,0:T(8,128)(2,1)S(1)} %get-tuple-element.94.gr_ref, ...), custom_call_target="tpu_custom_call" | custom-call | flops 5000000000 | bytes 1048576 | tf_op jit(solution)/shard_map/source_gradients/pallas_call | solution.py:604
  33.6 0.0 collective-permute-start.8
  33.6 2.9 %collective-permute-start.9 = (bf16[1664,128]{1,0:T(8,128)(2,1)S(1)}, bf16[1664,128]{1,0:T(8,128)(2,1)S(1)}, u32[]{:S(2)}, u32[]{:S(2)}) collective-permute-start(bf16[1664,128]{1,0:T(8,128)(2,1)S(1)} %get-tuple-element.107), channel_id=1, source_target_pairs={{32,0},{64,32},{96,64},{128,96},{160,128},{192,160},{224,192},{0,2... | collective-permute-start | bytes 1277960 | tf_op jit(solution)/shard_map/ppermute | solution.py:637
  36.6 0.0 collective-permute-done.4
  36.6 0.0 collective-permute-done.6
  36.6 5.4 %hidden_and_forces.1 = (bf16[24,256,128]{2,1,0:T(8,128)(2,1)S(1)}, f32[8,128]{1,0:T(8,128)S(1)}) custom-call(bf16[784,128]{1,0:T(8,128)(2,1)S(1)} %bitcast.30, bf16[392,128]{1,0:T(8,128)(2,1)S(1)} %bitcast.35, bf16[392,128]{1,0:T(8,128)(2,1)S(1)} %bitcast.34, bf16[784,128]{1,0:T(8,128)(2,1)S(1)} %bitcast.32, bf16[784,128]{1,0:T(8,128)(2,1)S(1)} %bitcast.33, ...), custom_call_target="tpu_custom_call" | custom-call | flops 7000000000 | bytes 1048576 | tf_op jit(solution)/shard_map/hidden_and_forces/pallas_call | solution.py:617
  42.0 0.0 collective-permute-start.13
  42.0 0.5 collective-permute-start.12
  42.5 0.2 fold_x.1
  42.7 0.6 collective-permute-start.10
  43.3 3.6 %collective-permute-start.11 = (bf16[832,128]{1,0:T(8,128)(2,1)S(1)}, bf16[832,128]{1,0:T(8,128)(2,1)S(1)}, u32[]{:S(2)}, u32[]{:S(2)}) collective-permute-start(bf16[832,128]{1,0:T(8,128)(2,1)S(1)} %get-tuple-element.112), channel_id=1, source_target_pairs={{1,0},{2,1},{3,2},{4,3},{5,4},{6,5},{7,6},{0,7},{9,8},{10,9},{11,1... | collective-permute-start | bytes 638984 | tf_op jit(solution)/shard_map/ppermute | solution.py:637
  46.9 0.1 fold_force.1.force_ref
  47.0 3.0 %collective-permute-start.15 = (f32[8,128]{1,0:T(8,128)S(1)}, f32[8,128]{1,0:T(8,128)S(1)}, u32[]{:S(2)}, u32[]{:S(2)}) collective-permute-start(f32[8,128]{1,0:T(8,128)S(1)} %fold_force.1.force_ref), channel_id=1, source_target_pairs={{1,0},{2,1},{3,2},{4,3},{5,4},{6,5},{7,6},{0,7},{9,8},{10,9},{11,1... | collective-permute-start | bytes 12296 | tf_op jit(solution)/shard_map/ppermute | solution.py:637
  50.0 1.4 %collective-permute-done.15.fhi_ref = f32[8,128]{1,0:T(8,128)S(1)} collective-permute-done((f32[8,128]{1,0:T(8,128)S(1)}, f32[8,128]{1,0:T(8,128)S(1)}, u32[]{:S(2)}, u32[]{:S(2)}) %collective-permute-start.15) | collective-permute-done | bytes 4128 | tf_op jit(solution)/shard_map/ppermute | solution.py:637
  51.4 4.3 %collective-permute-done.14.flo_ref = f32[8,128]{1,0:T(8,128)S(1)} collective-permute-done((f32[8,128]{1,0:T(8,128)S(1)}, f32[8,128]{1,0:T(8,128)S(1)}, u32[]{:S(2)}, u32[]{:S(2)}) %collective-permute-start.14) | collective-permute-done | bytes 4128 | tf_op jit(solution)/shard_map/ppermute | solution.py:637
  55.7 0.1 fold_z.1
  55.8 0.1 collective-permute-start.16
  55.9 4.1 %collective-permute-start.17 = (bf16[432,128]{1,0:T(8,128)(2,1)S(1)}, bf16[432,128]{1,0:T(8,128)(2,1)S(1)}, u32[]{:S(2)}, u32[]{:S(2)}) collective-permute-start(bf16[432,128]{1,0:T(8,128)(2,1)S(1)} %get-tuple-element.119), channel_id=1, source_target_pairs={{8,0},{16,8},{24,16},{0,24},{9,1},{17,9},{25,17},{1,25},{10,2},{18... | collective-permute-start | bytes 331784 | tf_op jit(solution)/shard_map/ppermute | solution.py:637
  60.0 2.0 %updated.1 = bf16[784,128]{1,0:T(8,128)(2,1)} custom-call(bf16[784,128]{1,0:T(8,128)(2,1)S(1)} %bitcast.31, bf16[24,64,256]{2,1,0:T(8,128)(2,1)S(1)} %get-tuple-element.87.v_ref, bf16[24,256,128]{2,1,0:T(8,128)(2,1)S(1)} %get-tuple-element.116.h_ref, f32[24,256]{1,0:T(8,128)S(1)} %get-tuple-element.117.envl_ref, s32[2,2,2]{2,1,0:T(2,128)S(1)} %copy-done.8), custom_call_target="tpu_custom_call" | custom-call | flops 2000000000 | bytes 1048576 | tf_op jit(solution)/shard_map/updated/pallas_call | solution.py:624
  62.0 1.9 %collective-permute-done.16.lo_ref = bf16[432,128]{1,0:T(8,128)(2,1)S(1)} collective-permute-done((bf16[432,128]{1,0:T(8,128)(2,1)S(1)}, bf16[432,128]{1,0:T(8,128)(2,1)S(1)}, u32[]{:S(2)}, u32[]{:S(2)}) %collective-permute-start.16) | collective-permute-done | bytes 110624 | tf_op jit(solution)/shard_map/ppermute | solution.py:637
  63.9 0.9 %fold_y.1 = (f32[784,128]{1,0:T(8,128)}, f32[16,3]{1,0:T(8,128)}) custom-call(f32[832,128]{1,0:T(8,128)S(1)} %get-tuple-element.121.mid_ref, f32[8,128]{1,0:T(8,128)S(1)} %get-tuple-element.122.force_ref, bf16[432,128]{1,0:T(8,128)(2,1)S(1)} %collective-permute-done.16.lo_ref, bf16[432,128]{1,0:T(8,128)(2,1)S(1)} %collective-permute-done.17.hi_ref), custom_call_target="tpu_custom_call" | custom-call | flops 1000000000 | bytes 1048576 | tf_op jit(solution)/shard_map/fold_y/pallas_call | solution.py:704
  (26 shorter events, 0.1 us)
Async XLA Ops:
  1.7 10.6 %collective-permute-start.1 = (bf16[2,1,2,49,2,128]{5,4,3,2,1,0:T(2,128)(2,1)S(1)}, bf16[2,1,2,49,2,128]{5,4,3,2,1,0:T(2,128)(2,1)S(1)}, u32[]{:S(2)}, u32[]{:S(2)}) collective-permute-start(bf16[2,1,2,49,2,128]{5,4,3,2,1,0:T(2,128)(2,1)S(1)} %get-tuple-element.141), channel_id=1, source_target_pairs={{8,0},{16,8},{24,16},{0,24},{9,1},{17,9},{25,17},{1,25},{10,2},{18... | collective-permute-start | bytes 301064 | tf_op jit(solution)/shard_map/ppermute | solution.py:637
  7.2 8.6 %collective-permute-start = (bf16[2,1,2,49,2,128]{5,4,3,2,1,0:T(2,128)(2,1)S(1)}, bf16[2,1,2,49,2,128]{5,4,3,2,1,0:T(2,128)(2,1)S(1)}, u32[]{:S(2)}, u32[]{:S(2)}) collective-permute-start(bf16[2,1,2,49,2,128]{5,4,3,2,1,0:T(2,128)(2,1)S(1)} %get-tuple-element.142), channel_id=1, source_target_pairs={{0,8},{8,16},{16,24},{24,0},{1,9},{9,17},{17,25},{25,1},{2,10},{10... | collective-permute-start | bytes 301064 | tf_op jit(solution)/shard_map/ppermute | solution.py:637
  8.2 7.5 %copy-start = (bf16[2,2,2,2,49,128]{5,3,4,2,1,0:T(2,128)(2,1)S(1)}, bf16[2,2,2,2,49,128]{5,3,4,2,1,0:T(2,128)(2,1)}, u32[]{:S(2)}) copy-start(bf16[2,2,2,2,49,128]{5,3,4,2,1,0:T(2,128)(2,1)} %param.13) | copy-start | bytes 602116
  8.2 14.0 %copy-start.2 = (bf16[2,640,640]{2,1,0:T(8,128)(2,1)S(1)}, bf16[2,640,640]{2,1,0:T(8,128)(2,1)}, u32[]{:S(2)}) copy-start(bf16[2,640,640]{2,1,0:T(8,128)(2,1)} %w2v.3) | copy-start | bytes 4915204
  8.2 14.0 %copy-start.3 = (bf16[896,896]{1,0:T(8,128)(2,1)S(1)}, bf16[896,896]{1,0:T(8,128)(2,1)}, u32[]{:S(2)}) copy-start(bf16[896,896]{1,0:T(8,128)(2,1)} %w0v.3) | copy-start | bytes 4816900
  12.3 9.9 %copy-start.1 = (bf16[2,768,768]{2,1,0:T(8,128)(2,1)S(1)}, bf16[2,768,768]{2,1,0:T(8,128)(2,1)}, u32[]{:S(2)}) copy-start(bf16[2,768,768]{2,1,0:T(8,128)(2,1)} %w1v.3) | copy-start | bytes 7077892
  16.9 8.5 %collective-permute-start.2 = (bf16[2,4,1,49,2,128]{5,4,3,2,1,0:T(2,128)(2,1)S(1)}, bf16[2,4,1,49,2,128]{5,4,3,2,1,0:T(2,128)(2,1)S(1)}, u32[]{:S(2)}, u32[]{:S(2)}) collective-permute-start(bf16[2,4,1,49,2,128]{5,4,3,2,1,0:T(2,128)(2,1)S(1)} %get-tuple-element.89), channel_id=1, source_target_pairs={{0,1},{1,2},{2,3},{3,4},{4,5},{5,6},{6,7},{7,0},{8,9},{9,10},{10,1... | collective-permute-start | bytes 602120 | tf_op jit(solution)/shard_map/ppermute | solution.py:637
  18.6 6.9 %collective-permute-start.3 = (bf16[2,4,1,49,2,128]{5,4,3,2,1,0:T(2,128)(2,1)S(1)}, bf16[2,4,1,49,2,128]{5,4,3,2,1,0:T(2,128)(2,1)S(1)}, u32[]{:S(2)}, u32[]{:S(2)}) collective-permute-start(bf16[2,4,1,49,2,128]{5,4,3,2,1,0:T(2,128)(2,1)S(1)} %get-tuple-element.90), channel_id=1, source_target_pairs={{1,0},{2,1},{3,2},{4,3},{5,4},{6,5},{7,6},{0,7},{9,8},{10,9},{11,1... | collective-permute-start | bytes 602120 | tf_op jit(solution)/shard_map/ppermute | solution.py:637
  21.1 12.5 %collective-permute-start.5 = (bf16[1,4,2,49,2,128]{5,4,3,2,1,0:T(2,128)(2,1)S(1)}, bf16[1,4,2,49,2,128]{5,4,3,2,1,0:T(2,128)(2,1)S(1)}, u32[]{:S(2)}, u32[]{:S(2)}) collective-permute-start(bf16[1,4,2,49,2,128]{5,4,3,2,1,0:T(2,128)(2,1)S(1)} %get-tuple-element.133), channel_id=1, source_target_pairs={{32,0},{64,32},{96,64},{128,96},{160,128},{192,160},{224,192},{0,2... | collective-permute-start | bytes 602120 | tf_op jit(solution)/shard_map/ppermute | solution.py:637
  22.2 14.4 %collective-permute-start.4 = (bf16[1,4,2,49,2,128]{5,4,3,2,1,0:T(2,128)(2,1)S(1)}, bf16[1,4,2,49,2,128]{5,4,3,2,1,0:T(2,128)(2,1)S(1)}, u32[]{:S(2)}, u32[]{:S(2)}) collective-permute-start(bf16[1,4,2,49,2,128]{5,4,3,2,1,0:T(2,128)(2,1)S(1)} %get-tuple-element.134), channel_id=1, source_target_pairs={{0,32},{32,64},{64,96},{96,128},{128,160},{160,192},{192,224},{224... | collective-permute-start | bytes 602120 | tf_op jit(solution)/shard_map/ppermute | solution.py:637
  25.4 3.9 %copy-start.6 = (f32[3,2,2,2,2,12]{5,4,3,2,1,0:T(2,128)S(1)}, f32[3,2,2,2,2,12]{5,4,3,2,1,0:T(2,128)}, u32[]{:S(2)}) copy-start(f32[3,2,2,2,2,12]{5,4,3,2,1,0:T(2,128)} %param.19) | copy-start | bytes 6916
  25.5 3.9 %copy-start.7 = (s32[2,2,2,2,12]{4,3,2,1,0:T(2,128)S(1)}, s32[2,2,2,2,12]{4,3,2,1,0:T(2,128)}, u32[]{:S(2)}) copy-start(s32[2,2,2,2,12]{4,3,2,1,0:T(2,128)} %param.16) | copy-start | bytes 2308
  25.5 3.9 %copy-start.8 = (s32[2,2,2]{2,1,0:T(2,128)S(1)}, s32[2,2,2]{2,1,0:T(2,128)}, u32[]{:S(2)}) copy-start(s32[2,2,2]{2,1,0:T(2,128)} %counts_ref.3) | copy-start | bytes 100
  26.4 10.2 %collective-permute-start.6 = (bf16[2,4,1,49,2,128]{5,4,3,2,1,0:T(2,128)(2,1)S(1)}, bf16[2,4,1,49,2,128]{5,4,3,2,1,0:T(2,128)(2,1)S(1)}, u32[]{:S(2)}, u32[]{:S(2)}) collective-permute-start(bf16[2,4,1,49,2,128]{5,4,3,2,1,0:T(2,128)(2,1)S(1)} %pad_maximum_fusion.1), channel_id=1, source_target_pairs={{0,32},{32,64},{64,96},{96,128},{128,160},{160,192},{192,224},{224... | collective-permute-start | bytes 602120 | tf_op jit(solution)/shard_map/ppermute | solution.py:637
  26.9 9.7 %collective-permute-start.7 = (bf16[2,4,1,49,2,128]{5,4,3,2,1,0:T(2,128)(2,1)S(1)}, bf16[2,4,1,49,2,128]{5,4,3,2,1,0:T(2,128)(2,1)S(1)}, u32[]{:S(2)}, u32[]{:S(2)}) collective-permute-start(bf16[2,4,1,49,2,128]{5,4,3,2,1,0:T(2,128)(2,1)S(1)} %pad_maximum_fusion.2), channel_id=1, source_target_pairs={{32,0},{64,32},{96,64},{128,96},{160,128},{192,160},{224,192},{0,2... | collective-permute-start | bytes 602120 | tf_op jit(solution)/shard_map/ppermute | solution.py:637
  29.4 7.2 %copy-start.4 = (f32[128,896]{1,0:T(8,128)S(1)}, f32[128,896]{1,0:T(8,128)}, u32[]{:S(2)}) copy-start(f32[128,896]{1,0:T(8,128)} %rout_ref.1) | copy-start | bytes 1376260
  29.4 7.2 %copy-start.5 = (f32[256,128]{1,0:T(8,128)S(1)}, f32[256,128]{1,0:T(8,128)}, u32[]{:S(2)}) copy-start(f32[256,128]{1,0:T(8,128)} %rin_ref.1) | copy-start | bytes 393220
  29.4 7.2 %copy-start.9 = (s32[64]{0:T(128)S(1)}, s32[64]{0:T(128)}, u32[]{:S(2)}) copy-start(s32[64]{0:T(128)} %constant.5.clone.base_ref) | copy-start | bytes 772
  33.6 8.9 %collective-permute-start.8 = (bf16[1664,128]{1,0:T(8,128)(2,1)S(1)}, bf16[1664,128]{1,0:T(8,128)(2,1)S(1)}, u32[]{:S(2)}, u32[]{:S(2)}) collective-permute-start(bf16[1664,128]{1,0:T(8,128)(2,1)S(1)} %get-tuple-element.106), channel_id=1, source_target_pairs={{0,32},{32,64},{64,96},{96,128},{128,160},{160,192},{192,224},{224... | collective-permute-start | bytes 1277960 | tf_op jit(solution)/shard_map/ppermute | solution.py:637
  33.6 8.9 %collective-permute-start.9 = (bf16[1664,128]{1,0:T(8,128)(2,1)S(1)}, bf16[1664,128]{1,0:T(8,128)(2,1)S(1)}, u32[]{:S(2)}, u32[]{:S(2)}) collective-permute-start(bf16[1664,128]{1,0:T(8,128)(2,1)S(1)} %get-tuple-element.107), channel_id=1, source_target_pairs={{32,0},{64,32},{96,64},{128,96},{160,128},{192,160},{224,192},{0,2... | collective-permute-start | bytes 1277960 | tf_op jit(solution)/shard_map/ppermute | solution.py:637
  42.0 4.9 %collective-permute-start.13 = (f32[8,128]{1,0:T(8,128)S(1)}, f32[8,128]{1,0:T(8,128)S(1)}, u32[]{:S(2)}, u32[]{:S(2)}) collective-permute-start(f32[8,128]{1,0:T(8,128)S(1)} %get-tuple-element.113.mine_ref), channel_id=1, source_target_pairs={{32,0},{64,32},{96,64},{128,96},{160,128},{192,160},{224,192},{0,2... | collective-permute-start | bytes 12296 | tf_op jit(solution)/shard_map/ppermute | solution.py:637
  42.0 4.9 %collective-permute-start.12 = (f32[8,128]{1,0:T(8,128)S(1)}, f32[8,128]{1,0:T(8,128)S(1)}, u32[]{:S(2)}, u32[]{:S(2)}) collective-permute-start(f32[8,128]{1,0:T(8,128)S(1)} %get-tuple-element.113.mine_ref), channel_id=1, source_target_pairs={{0,32},{32,64},{64,96},{96,128},{128,160},{160,192},{192,224},{224... | collective-permute-start | bytes 12296 | tf_op jit(solution)/shard_map/ppermute | solution.py:637
  42.7 13.0 %collective-permute-start.10 = (bf16[832,128]{1,0:T(8,128)(2,1)S(1)}, bf16[832,128]{1,0:T(8,128)(2,1)S(1)}, u32[]{:S(2)}, u32[]{:S(2)}) collective-permute-start(bf16[832,128]{1,0:T(8,128)(2,1)S(1)} %get-tuple-element.111), channel_id=1, source_target_pairs={{0,1},{1,2},{2,3},{3,4},{4,5},{5,6},{6,7},{7,0},{8,9},{9,10},{10,1... | collective-permute-start | bytes 638984 | tf_op jit(solution)/shard_map/ppermute | solution.py:637
  43.3 12.4 %collective-permute-start.11 = (bf16[832,128]{1,0:T(8,128)(2,1)S(1)}, bf16[832,128]{1,0:T(8,128)(2,1)S(1)}, u32[]{:S(2)}, u32[]{:S(2)}) collective-permute-start(bf16[832,128]{1,0:T(8,128)(2,1)S(1)} %get-tuple-element.112), channel_id=1, source_target_pairs={{1,0},{2,1},{3,2},{4,3},{5,4},{6,5},{7,6},{0,7},{9,8},{10,9},{11,1... | collective-permute-start | bytes 638984 | tf_op jit(solution)/shard_map/ppermute | solution.py:637
  47.0 4.4 %collective-permute-start.15 = (f32[8,128]{1,0:T(8,128)S(1)}, f32[8,128]{1,0:T(8,128)S(1)}, u32[]{:S(2)}, u32[]{:S(2)}) collective-permute-start(f32[8,128]{1,0:T(8,128)S(1)} %fold_force.1.force_ref), channel_id=1, source_target_pairs={{1,0},{2,1},{3,2},{4,3},{5,4},{6,5},{7,6},{0,7},{9,8},{10,9},{11,1... | collective-permute-start | bytes 12296 | tf_op jit(solution)/shard_map/ppermute | solution.py:637
  50.0 5.7 %collective-permute-start.14 = (f32[8,128]{1,0:T(8,128)S(1)}, f32[8,128]{1,0:T(8,128)S(1)}, u32[]{:S(2)}, u32[]{:S(2)}) collective-permute-start(f32[8,128]{1,0:T(8,128)S(1)} %fold_force.1.force_ref), channel_id=1, source_target_pairs={{0,1},{1,2},{2,3},{3,4},{4,5},{5,6},{6,7},{7,0},{8,9},{9,10},{10,1... | collective-permute-start | bytes 12296 | tf_op jit(solution)/shard_map/ppermute | solution.py:637
  55.8 8.1 %collective-permute-start.16 = (bf16[432,128]{1,0:T(8,128)(2,1)S(1)}, bf16[432,128]{1,0:T(8,128)(2,1)S(1)}, u32[]{:S(2)}, u32[]{:S(2)}) collective-permute-start(bf16[432,128]{1,0:T(8,128)(2,1)S(1)} %get-tuple-element.118), channel_id=1, source_target_pairs={{0,8},{8,16},{16,24},{24,0},{1,9},{9,17},{17,25},{25,1},{2,10},{10... | collective-permute-start | bytes 331784 | tf_op jit(solution)/shard_map/ppermute | solution.py:637
  55.9 8.0 %collective-permute-start.17 = (bf16[432,128]{1,0:T(8,128)(2,1)S(1)}, bf16[432,128]{1,0:T(8,128)(2,1)S(1)}, u32[]{:S(2)}, u32[]{:S(2)}) collective-permute-start(bf16[432,128]{1,0:T(8,128)(2,1)S(1)} %get-tuple-element.119), channel_id=1, source_target_pairs={{8,0},{16,8},{24,16},{0,24},{9,1},{17,9},{25,17},{1,25},{10,2},{18... | collective-permute-start | bytes 331784 | tf_op jit(solution)/shard_map/ppermute | solution.py:637

commit v5 on v4

--- a/solution.py
+++ b/solution.py
@@ -100,6 +100,13 @@
     return op(ah, bh) + (op(ah, bl) + op(al, bh))
 
 
+def dot3_narrow(a, b, nt):
+    ah, al = split2(a)
+    bh, bl = split2(b)
+    wide = dot_nt(ah, jnp.concatenate([bh, bl], axis=0)) if nt else dot(ah, jnp.concatenate([bh, bl], axis=1))
+    return wide[:, :128] + (wide[:, 128:] + (dot_nt(al, bh) if nt else dot(al, bh)))
+
+
 def edge_ids():
     e = iota((E, 128), 0)
     cell = (e * 2731) >> 16
@@ -193,7 +200,7 @@
     dist = column(dist_ref[...])
     basis, offset = basis_of(dist)
     wb_ref[...] = basis * (-offset / (sigma_width * sigma_width))
-    inner = dot3(basis, rin_ref[...])
+    inner = dot3_narrow(basis, rin_ref[...], False)
     sig = jax.nn.sigmoid(inner)
     dsilu_ref[...] = sig * (1.0 + inner * (1.0 - sig))
     copies[2].wait()
@@ -258,7 +265,18 @@
     return jnp.where(low, k0, pltpu.roll(k1, 4, 1)), jnp.where(low, pltpu.roll(k0, 4, 1), k1)
 
 
-def kernel_a2(u_ref, z0_ref, z1_ref, z2_ref, rad_ref, w0v, w1v, w2v, gi0_ref, gr_ref, v_ref, u4_ref):
+def kernel_a2(
+    u_ref, z0_ref, z1_ref, z2_ref, rad_ref, srcv_ref, dir_ref, w0v, w1v, w2v,
+    gi0_ref, gr_ref, v_ref, u4_ref, side_ref,
+):
+    cell, slot, _ = edge_ids()
+    q = jnp.broadcast_to(column(srcv_ref[...].astype(f32)), (E, 128)).astype(jnp.int32)
+    lane = iota((E, 128), 1)
+    from_slot = 2 * padded_cell(q, cell) + (q & 1)
+    to_slot = 2 * padded_cell(jnp.full((E, 128), 26, jnp.int32), cell) + slot
+    sign = jnp.where(lane == from_slot, 1.0, 0.0) - jnp.where(lane == to_slot, 1.0, 0.0)
+    for d in range(3):
+        side_ref[d] = sign * column(dir_ref[16 * d : 16 * d + 16, :])
     def turn(g, carry):
         u = u_ref[g]
         v_ref[g] = u.T[:64]
@@ -297,18 +315,9 @@
 
 
 def kernel_a3(
-    v_ref, gr_ref, cs_ref, counts_ref, src_ref, srcv_ref, dir_ref,
-    xlo_ref, xhi_ref, mid_ref, side_ref, acc_ref,
+    v_ref, gr_ref, cs_ref, counts_ref, src_ref,
+    xlo_ref, xhi_ref, mid_ref, acc_ref,
 ):
-    cell, slot, _ = edge_ids()
-    q = jnp.broadcast_to(column(srcv_ref[...].astype(f32)), (E, 128)).astype(jnp.int32)
-    lane = iota((E, 128), 1)
-    from_slot = 2 * padded_cell(q, cell) + (q & 1)
-    to_slot = 2 * padded_cell(jnp.full((E, 128), 26, jnp.int32), cell) + slot
-    sign = jnp.where(lane == from_slot, 1.0, 0.0) - jnp.where(lane == to_slot, 1.0, 0.0)
-    for d in range(3):
-        side_ref[d] = sign * column(dir_ref[16 * d : 16 * d + 16, :])
-
     acc_ref[...] = jnp.zeros(acc_ref.shape, f32)
     row_ok = iota((56, 128), 0) < 49
     for cell in range(8):
@@ -424,7 +433,7 @@
                 along = along + prod[:, cut]
                 q = first + l0 + i
                 h_ref[:, 16 * q : 16 * q + 16, :] = pair_block(hp[:, cut], hn[:, cut])
-    grad_act = dot3(gi0_ref[...] * p0_ref[...], rout_ref[...], dot_nt)
+    grad_act = dot3_narrow(gi0_ref[...] * p0_ref[...], rout_ref[...], True)
     grad_basis = dot3(grad_act * dsilu_ref[...], rin_ref[...], dot_nt)
     parts = grad_basis * wb_ref[...]
     total = along * ratio_ref[...] + parts[:, :128] + parts[:, 128:]
@@ -485,14 +494,14 @@
     return mine + jnp.where(at == 1, lo, 0.0) + jnp.where(at == 2, hi, 0.0)
 
 
-def fold_force_x(mine_ref, lo_ref, hi_ref, out_ref):
-    out_ref[...] = force_sum(mine_ref[...], lo_ref[...], hi_ref[...], 64, 5)
+def fold_force_z(mine_ref, lo_ref, hi_ref, out_ref):
+    out_ref[...] = force_sum(mine_ref[...], lo_ref[...], hi_ref[...], 4, 1)
 
 
 def fold_z(
     mid_ref, lo_ref, hi_ref, force_ref, flo_ref, fhi_ref, ylo_ref, yhi_ref, out_ref, fout_ref,
 ):
-    force = force_sum(force_ref[...], flo_ref[...], fhi_ref[...], 4, 1)
+    force = force_sum(force_ref[...], flo_ref[...], fhi_ref[...], 64, 5)
     fout_ref[...] = force
     rest = force - force.astype(bf16).astype(f32)
     for ref in (ylo_ref, yhi_ref):
@@ -588,21 +597,23 @@
     )
 
 
-def run_a2(u, z0, z1, z2, rad, w0, w1, w2):
+def run_a2(u, z0, z1, z2, rad, src, dirs, w0, w1, w2):
     out = [
         shape((E, 896), f32), shape((G, 256, 128), bf16), shape((G, 64, 256), bf16), shape((G, 2, 128, 128), bf16),
+        shape((3, E, 128), f32),
     ]
-    return call(kernel_a2, out, [VM] * 8, [], 20 << 20, "mix_backward", cost(4))(u, z0, z1, z2, rad, w0, w1, w2)
-
-
-def run_a3(v, gr, cs, counts, src, dirs):
+    return call(kernel_a2, out, [VM] * 10, [], 20 << 20, "mix_backward", cost(4))(
+        u, z0, z1, z2, rad, src, dirs, w0, w1, w2
+    )
+
+
+def run_a3(v, gr, cs, counts, src):
     out = [
         shape((16 * CR, 128), bf16), shape((16 * CR, 128), bf16), shape((32 * CR, 128), f32),
-        shape((3, E, 128), f32),
     ]
     scratch = [pltpu.VMEM((64 * CR + 16, 128), f32)]
-    return call(kernel_a3, out, [VM, VM, VM, SM, SM, VM, VM], scratch, 20 << 20, "source_gradients", cost(5))(
-        v, gr, cs, counts, src, src, dirs
+    return call(kernel_a3, out, [VM, VM, VM, SM, SM], scratch, 20 << 20, "source_gradients", cost(5))(
+        v, gr, cs, counts, src
     )
 
 
@@ -644,8 +655,8 @@
 def test_run(pieces, wt, cot, src, cnt, dist, dirs, w0, w1, w2, rin, rout):
     cnt = cnt.reshape(2, 2, 2)
     u, z0, z1, z2, rad, dsilu, wb, ratio, envl, cs = run_a1(wt, cnt, dist, rin, rout, cot)
-    gi0, gr, v, u4 = run_a2(u, z0, z1, z2, rad, w0, w1, w2)
-    gxlo, gxhi, mid, side = run_a3(v, gr, cs, cnt, src, dirs)
+    gi0, gr, v, u4, side = run_a2(u, z0, z1, z2, rad, src, dirs, w0, w1, w2)
+    gxlo, gxhi, mid = run_a3(v, gr, cs, cnt, src)
     h, force = run_b1(pieces, src, (u4, z0, z1, z2, gi0, rad, dsilu, wb, ratio, side), rin, rout, w0, w1, w2)
     return run_b2(pieces[0], v, h, envl, cnt), force, gxlo, gxhi, mid
 
@@ -668,27 +679,27 @@
     (u, z0, z1, z2, rad), up, down = tie((u, z0, z1, z2, rad), up, down)
     zlo, zhi = exchange(up, down, "gz")
     xlo, xhi = exchange(tall[1:2], tall[0:1], "gx")
-    gi0, gr, v, u4 = run_a2(u, z0, z1, z2, rad, w0, w1, w2)
+    gi0, gr, v, u4, side = run_a2(u, z0, z1, z2, rad, src, dirs, w0, w1, w2)
     gr, zlo, zhi = tie(gr, zlo, zhi)
     top = jnp.concatenate([zlo[1:2], zhi[1:2]], axis=0)
     low = jnp.concatenate([zlo[0:1], zhi[0:1]], axis=0)
     gr, top, low = tie(gr, top, low)
     xzlo, xzhi = exchange(top, low, "gx")
-    gxlo, gxhi, mid, side = run_a3(v, gr, cs, counts, src, dirs)
+    gxlo, gxhi, mid = run_a3(v, gr, cs, counts, src)
 
     lo, hi = exchange(gxhi, gxlo, "gx")
     rows = [p.reshape(-1, 128) for p in (feats, ylo, yhi, zlo, zhi, xlo, xhi, xzlo, xzhi)]
     h, force = run_b1(rows, src, (u4, z0, z1, z2, gi0, rad, dsilu, wb, ratio, side), rin, rout, w0, w1, w2)
     h, lo, hi = tie(h, lo, hi)
-    flo, fhi = exchange(force, force, "gx")
+    flo, fhi = exchange(force, force, "gz")
     gzlo, gzhi, mid = call(
         fold_x,
         [shape((8 * CR, 128), bf16), shape((8 * CR, 128), bf16), shape((16 * CR, 128), f32)],
         [VM] * 3, [], 16 << 20, "fold_x", cost(0.1),
     )(mid, lo, hi)
     lo, hi = exchange(gzhi, gzlo, "gz")
-    force = call(fold_force_x, shape((8, 128), f32), [VM] * 3, [], 8 << 20, "fold_force", cost(4))(force, flo, fhi)
-    flo, fhi = exchange(force, force, "gz")
+    force = call(fold_force_z, shape((8, 128), f32), [VM] * 3, [], 8 << 20, "fold_force", cost(4))(force, flo, fhi)
+    flo, fhi = exchange(force, force, "gx")
     gylo, gyhi, mid, force = call(
         fold_z,
         [

time: 64.9 us -> 64.4 us (level)
  waiting for transfers between devices: 11 us -> 10.3 us
    ppermute x18, waiting for transfers between devices: 11 us -> 10.3 us  [exchange(): return (lax.ppermute(to_up, axis, up), lax.ppermute(to_down, axis, down))]
  transfers between devices with their start and end apart: 18 -> 18, of which waited for: 4 -> 5; matrix products, arithmetic and copies ran while one was open for 3% -> 3% of each run, Pallas kernels for 30% -> 30%
where the time goes in v5:
time: 64.4 us; the launch traced here: 64.2 us
  starting transfers between devices  28.8 us (45%)
  Pallas kernels  20.1 us (31%)
  waiting for transfers between devices  10.3 us (16%)
  local copies, waits for them, and re-layouts  2.98 us (5%)
  other arithmetic  1.16 us (2%)
  between operations  0.91 us (1%)
    ppermute x18, starting transfers between devices, exchange(): return (lax.ppermute(to_up, axis, up), lax.ppermute(to_down, axis, down))  28.8 us
    ppermute x18, waiting for transfers between devices, exchange(): return (lax.ppermute(to_up, axis, up), lax.ppermute(to_down, axis, down))  10.3 us
    pallas_call x1, Pallas kernels, run_b1(): call(kernel_b1, out, specs, scratch, 28 << 20, 'hidden_and_forces', cost(7))  5.37 us
    pallas_call x1, Pallas kernels, run_a1(): call(kernel_a1, out, [VM] + [HB] * 5, scratch, 24 << 20, 'rotations', cos...  4.02 us
    pallas_call x1, Pallas kernels, run_a2(): call(kernel_a2, out, [VM] * 10, [], 20 << 20, 'mix_backward', cost(4))  3.81 us
    pallas_call x1, Pallas kernels, run_a3(): call(kernel_a3, out, [VM, VM, VM, SM, SM], scratch, 20 << 20, 'source_gra...  3.63 us
    pallas_call x1, Pallas kernels, run_b2(): call(kernel_b2, shape((784, 128), bf16), [VM] * 4 + [SM], scratch, 16 <<...  2.03 us
  transfers between devices with their start and end apart: 18, of which 5 were waited for; matrix products, arithmetic and copies ran while one was open for 3% of the time, Pallas kernels for 30%

profile of v5, /device:TPU:32, one launch (start us, length us, event | category | flops | bytes accessed | tf_op | source)
XLA Modules:
  0.0 64.2 jit_solution(12811517524912642253)
XLA Ops:
  0.6 1.1 %fusion.4 = (bf16[2,1,2,49,2,128]{5,4,3,2,1,0:T(2,128)(2,1)S(1)}, bf16[2,1,2,49,2,128]{5,4,3,2,1,0:T(2,128)(2,1)S(1)}) fusion(bf16[2,2,2,49,2,128]{5,4,3,2,1,0:T(2,128)(2,1)} %bitcast.28), kind=kLoop, calls=%fused_computation.7 | loop fusion | bytes 401408 | tf_op jit(solution)/shard_map/slice | solution.py:673
  1.7 5.5 %collective-permute-start.1 = (bf16[2,1,2,49,2,128]{5,4,3,2,1,0:T(2,128)(2,1)S(1)}, bf16[2,1,2,49,2,128]{5,4,3,2,1,0:T(2,128)(2,1)S(1)}, u32[]{:S(2)}, u32[]{:S(2)}) collective-permute-start(bf16[2,1,2,49,2,128]{5,4,3,2,1,0:T(2,128)(2,1)S(1)} %get-tuple-element.141), channel_id=1, source_target_pairs={{8,0},{16,8},{24,16},{0,24},{9,1},{17,9},{25,17},{1,25},{10,2},{18... | collective-permute-start | bytes 301064 | tf_op jit(solution)/shard_map/ppermute | solution.py:648
  7.2 0.0 collective-permute-start
  7.2 1.0 %reshape.58 = bf16[192,235]{1,0:T(8,128)(2,1)S(1)} reshape(bf16[2,2,2,12,2,235]{5,4,3,2,1,0:T(2,128)(2,1)} %bitcast.44) | data formatting | bytes 180480 | tf_op jit(solution)/shard_map/reshape | solution.py:666
  8.2 0.0 copy-start
  8.2 0.0 copy-start.2
  8.2 0.0 copy-start.3
  8.3 4.0 %rotations.1 = (bf16[24,256,128]{2,1,0:T(8,128)(2,1)S(1)}, bf16[192,896]{1,0:T(8,128)(2,1)S(1)}, bf16[384,768]{1,0:T(8,128)(2,1)S(1)}, bf16[384,640]{1,0:T(8,128...) custom-call(bf16[192,256]{1,0:T(8,128)(2,1)S(1)} %pad.4.wt_ref, ...), custom_call_target="tpu_custom_call" | custom-call | flops 6000000000 | bytes 1048576 | tf_op jit(solution)/shard_map/rotations/pallas_call | solution.py:595
  12.3 0.0 copy-start.1
  12.3 0.0 copy-start.6
  12.3 0.0 copy-start.7
  12.3 0.0 collective-permute-done.1
  12.3 3.4 %collective-permute-done = bf16[2,1,2,49,2,128]{5,4,3,2,1,0:T(2,128)(2,1)S(1)} collective-permute-done((bf16[2,1,2,49,2,128]{5,4,3,2,1,0:T(2,128)(2,1)S(1)}, bf16[2,1,2,49,2,128]{5,4,3,2,1,0:T(2,128)(2,1)S(1)}, u32[]{:S(2)}, u32[]{:S(2)}) %collective-permute-start) | collective-permute-done | bytes 100384 | tf_op jit(solution)/shard_map/ppermute | solution.py:648
  15.8 0.6 pad_maximum_fusion
  16.4 0.3 fusion.1
  16.6 0.3 fusion
  16.9 1.7 %collective-permute-start.2 = (bf16[2,4,1,49,2,128]{5,4,3,2,1,0:T(2,128)(2,1)S(1)}, bf16[2,4,1,49,2,128]{5,4,3,2,1,0:T(2,128)(2,1)S(1)}, u32[]{:S(2)}, u32[]{:S(2)}) collective-permute-start(bf16[2,4,1,49,2,128]{5,4,3,2,1,0:T(2,128)(2,1)S(1)} %get-tuple-element.89), channel_id=1, source_target_pairs={{0,1},{1,2},{2,3},{3,4},{4,5},{5,6},{6,7},{7,0},{8,9},{9,10},{10,1... | collective-permute-start | bytes 602120 | tf_op jit(solution)/shard_map/ppermute | solution.py:648
  18.6 2.6 %collective-permute-start.3 = (bf16[2,4,1,49,2,128]{5,4,3,2,1,0:T(2,128)(2,1)S(1)}, bf16[2,4,1,49,2,128]{5,4,3,2,1,0:T(2,128)(2,1)S(1)}, u32[]{:S(2)}, u32[]{:S(2)}) collective-permute-start(bf16[2,4,1,49,2,128]{5,4,3,2,1,0:T(2,128)(2,1)S(1)} %get-tuple-element.90), channel_id=1, source_target_pairs={{1,0},{2,1},{3,2},{4,3},{5,4},{6,5},{7,6},{0,7},{9,8},{10,9},{11,1... | collective-permute-start | bytes 602120 | tf_op jit(solution)/shard_map/ppermute | solution.py:648
  21.1 1.1 %collective-permute-start.5 = (bf16[1,4,2,49,2,128]{5,4,3,2,1,0:T(2,128)(2,1)S(1)}, bf16[1,4,2,49,2,128]{5,4,3,2,1,0:T(2,128)(2,1)S(1)}, u32[]{:S(2)}, u32[]{:S(2)}) collective-permute-start(bf16[1,4,2,49,2,128]{5,4,3,2,1,0:T(2,128)(2,1)S(1)} %get-tuple-element.133), channel_id=1, source_target_pairs={{32,0},{64,32},{96,64},{128,96},{160,128},{192,160},{224,192},{0,2... | collective-permute-start | bytes 602120 | tf_op jit(solution)/shard_map/ppermute | solution.py:648
  22.2 0.0 collective-permute-start.4
  22.3 3.8 %mix_backward.1 = (f32[192,896]{1,0:T(8,128)S(1)}, bf16[24,256,128]{2,1,0:T(8,128)(2,1)S(1)}, bf16[24,64,256]{2,1,0:T(8,128)(2,1)S(1)}, bf16[24,2,128,128]{3,2,1,0:T(8,128)(2,1)S(1)}, f32[3,192,128]{2,1,0:T(8,128)S(1)}) custom-call(bf16[24,256,128]{2,1,0:T(8,128)(2,1)S(1)} %get-tuple-element.82.u_ref, bf16[192,896]{1,0:T(8,128)(2,1)S(1)} %get-tuple-element.83.z0_ref.g0_ref, ...), custom_call_target="tpu_custom_call" | custom-call | flops 4000000000 | bytes 1048576 | tf_op jit(solution)/shard_map/mix_backward/pallas_call | solution.py:605
  26.1 0.0 copy-start.8
  26.1 0.0 collective-permute-done.3
  26.1 0.3 fusion.2
  26.4 0.3 pad_maximum_fusion.2
  26.7 0.3 pad_maximum_fusion.1
  27.0 0.5 collective-permute-start.6
  27.5 2.4 %collective-permute-start.7 = (bf16[2,4,1,49,2,128]{5,4,3,2,1,0:T(2,128)(2,1)S(1)}, bf16[2,4,1,49,2,128]{5,4,3,2,1,0:T(2,128)(2,1)S(1)}, u32[]{:S(2)}, u32[]{:S(2)}) collective-permute-start(bf16[2,4,1,49,2,128]{5,4,3,2,1,0:T(2,128)(2,1)S(1)} %pad_maximum_fusion.2), channel_id=1, source_target_pairs={{32,0},{64,32},{96,64},{128,96},{160,128},{192,160},{224,192},{0,2... | collective-permute-start | bytes 602120 | tf_op jit(solution)/shard_map/ppermute | solution.py:648
  30.0 3.6 %source_gradients.1 = (bf16[1664,128]{1,0:T(8,128)(2,1)S(1)}, bf16[1664,128]{1,0:T(8,128)(2,1)S(1)}, f32[3328,128]{1,0:T(8,128)S(1)}) custom-call(bf16[24,64,256]{2,1,0:T(8,128)(2,1)S(1)} %get-tuple-element.87.v_ref, bf16[24,256,128]{2,1,0:T(8,128)(2,1)S(1)} %get-tuple-element.94.gr_ref, f32[800,128]{1,0:T(8,128)S(1)} %get-tuple-element.95.cs_ref, ...), custom_call_target="tpu_custom_call" | custom-call | flops 5000000000 | bytes 1048576 | tf_op jit(solution)/shard_map/source_gradients/pallas_call | solution.py:615
  33.6 0.0 collective-permute-start.8
  33.6 2.9 %collective-permute-start.9 = (bf16[1664,128]{1,0:T(8,128)(2,1)S(1)}, bf16[1664,128]{1,0:T(8,128)(2,1)S(1)}, u32[]{:S(2)}, u32[]{:S(2)}) collective-permute-start(bf16[1664,128]{1,0:T(8,128)(2,1)S(1)} %get-tuple-element.107), channel_id=1, source_target_pairs={{32,0},{64,32},{96,64},{128,96},{160,128},{192,160},{224,192},{0,2... | collective-permute-start | bytes 1277960 | tf_op jit(solution)/shard_map/ppermute | solution.py:648
  36.6 0.0 collective-permute-done.4
  36.6 5.4 %hidden_and_forces.1 = (bf16[24,256,128]{2,1,0:T(8,128)(2,1)S(1)}, f32[8,128]{1,0:T(8,128)S(1)}) custom-call(bf16[784,128]{1,0:T(8,128)(2,1)S(1)} %bitcast.30, bf16[392,128]{1,0:T(8,128)(2,1)S(1)} %bitcast.35, bf16[392,128]{1,0:T(8,128)(2,1)S(1)} %bitcast.34, bf16[784,128]{1,0:T(8,128)(2,1)S(1)} %bitcast.32, bf16[784,128]{1,0:T(8,128)(2,1)S(1)} %bitcast.33, ...), custom_call_target="tpu_custom_call" | custom-call | flops 7000000000 | bytes 1048576 | tf_op jit(solution)/shard_map/hidden_and_forces/pallas_call | solution.py:628
  42.0 3.1 %collective-permute-start.13 = (f32[8,128]{1,0:T(8,128)S(1)}, f32[8,128]{1,0:T(8,128)S(1)}, u32[]{:S(2)}, u32[]{:S(2)}) collective-permute-start(f32[8,128]{1,0:T(8,128)S(1)} %get-tuple-element.113.mine_ref), channel_id=1, source_target_pairs={{1,0},{2,1},{3,2},{4,3},{5,4},{6,5},{7,6},{0,7},{9,8},{10,9},{11,1... | collective-permute-start | bytes 12296 | tf_op jit(solution)/shard_map/ppermute | solution.py:648
  45.1 0.2 fold_x.1
  45.3 0.1 collective-permute-start.10
  45.4 4.2 %collective-permute-start.11 = (bf16[832,128]{1,0:T(8,128)(2,1)S(1)}, bf16[832,128]{1,0:T(8,128)(2,1)S(1)}, u32[]{:S(2)}, u32[]{:S(2)}) collective-permute-start(bf16[832,128]{1,0:T(8,128)(2,1)S(1)} %get-tuple-element.112), channel_id=1, source_target_pairs={{1,0},{2,1},{3,2},{4,3},{5,4},{6,5},{7,6},{0,7},{9,8},{10,9},{11,1... | collective-permute-start | bytes 638984 | tf_op jit(solution)/shard_map/ppermute | solution.py:648
  49.6 1.2 %collective-permute-done.12.lo_ref = f32[8,128]{1,0:T(8,128)S(1)} collective-permute-done((f32[8,128]{1,0:T(8,128)S(1)}, f32[8,128]{1,0:T(8,128)S(1)}, u32[]{:S(2)}, u32[]{:S(2)}) %collective-permute-start.12) | collective-permute-done | bytes 4128 | tf_op jit(solution)/shard_map/ppermute | solution.py:648
  50.8 0.1 fold_force.1.force_ref
  50.9 0.5 collective-permute-start.14
  51.4 0.8 %collective-permute-done.15.fhi_ref = f32[8,128]{1,0:T(8,128)S(1)} collective-permute-done((f32[8,128]{1,0:T(8,128)S(1)}, f32[8,128]{1,0:T(8,128)S(1)}, u32[]{:S(2)}, u32[]{:S(2)}) %collective-permute-start.15) | collective-permute-done | bytes 4128 | tf_op jit(solution)/shard_map/ppermute | solution.py:648
  52.2 2.9 %collective-permute-done.14.flo_ref = f32[8,128]{1,0:T(8,128)S(1)} collective-permute-done((f32[8,128]{1,0:T(8,128)S(1)}, f32[8,128]{1,0:T(8,128)S(1)}, u32[]{:S(2)}, u32[]{:S(2)}) %collective-permute-start.14) | collective-permute-done | bytes 4128 | tf_op jit(solution)/shard_map/ppermute | solution.py:648
  55.1 0.1 fold_z.1
  55.2 0.1 collective-permute-start.16
  55.3 4.1 %collective-permute-start.17 = (bf16[432,128]{1,0:T(8,128)(2,1)S(1)}, bf16[432,128]{1,0:T(8,128)(2,1)S(1)}, u32[]{:S(2)}, u32[]{:S(2)}) collective-permute-start(bf16[432,128]{1,0:T(8,128)(2,1)S(1)} %get-tuple-element.119), channel_id=1, source_target_pairs={{8,0},{16,8},{24,16},{0,24},{9,1},{17,9},{25,17},{1,25},{10,2},{18... | collective-permute-start | bytes 331784 | tf_op jit(solution)/shard_map/ppermute | solution.py:648
  59.5 2.0 %updated.1 = bf16[784,128]{1,0:T(8,128)(2,1)} custom-call(bf16[784,128]{1,0:T(8,128)(2,1)S(1)} %bitcast.31, bf16[24,64,256]{2,1,0:T(8,128)(2,1)S(1)} %get-tuple-element.87.v_ref, bf16[24,256,128]{2,1,0:T(8,128)(2,1)S(1)} %get-tuple-element.116.h_ref, f32[24,256]{1,0:T(8,128)S(1)} %get-tuple-element.117.envl_ref, s32[2,2,2]{2,1,0:T(2,128)S(1)} %copy-done.8), custom_call_target="tpu_custom_call" | custom-call | flops 2000000000 | bytes 1048576 | tf_op jit(solution)/shard_map/updated/pallas_call | solution.py:635
  61.5 1.9 %collective-permute-done.16.lo_ref = bf16[432,128]{1,0:T(8,128)(2,1)S(1)} collective-permute-done((bf16[432,128]{1,0:T(8,128)(2,1)S(1)}, bf16[432,128]{1,0:T(8,128)(2,1)S(1)}, u32[]{:S(2)}, u32[]{:S(2)}) %collective-permute-start.16) | collective-permute-done | bytes 110624 | tf_op jit(solution)/shard_map/ppermute | solution.py:648
  63.4 0.9 %fold_y.1 = (f32[784,128]{1,0:T(8,128)}, f32[16,3]{1,0:T(8,128)}) custom-call(f32[832,128]{1,0:T(8,128)S(1)} %get-tuple-element.121.mid_ref, f32[8,128]{1,0:T(8,128)S(1)} %get-tuple-element.122.force_ref, bf16[432,128]{1,0:T(8,128)(2,1)S(1)} %collective-permute-done.16.lo_ref, bf16[432,128]{1,0:T(8,128)(2,1)S(1)} %collective-permute-done.17.hi_ref), custom_call_target="tpu_custom_call" | custom-call | flops 1000000000 | bytes 1048576 | tf_op jit(solution)/shard_map/fold_y/pallas_call | solution.py:715
  (26 shorter events, 0.1 us)
Async XLA Ops:
  1.7 10.6 %collective-permute-start.1 = (bf16[2,1,2,49,2,128]{5,4,3,2,1,0:T(2,128)(2,1)S(1)}, bf16[2,1,2,49,2,128]{5,4,3,2,1,0:T(2,128)(2,1)S(1)}, u32[]{:S(2)}, u32[]{:S(2)}) collective-permute-start(bf16[2,1,2,49,2,128]{5,4,3,2,1,0:T(2,128)(2,1)S(1)} %get-tuple-element.141), channel_id=1, source_target_pairs={{8,0},{16,8},{24,16},{0,24},{9,1},{17,9},{25,17},{1,25},{10,2},{18... | collective-permute-start | bytes 301064 | tf_op jit(solution)/shard_map/ppermute | solution.py:648
  7.2 8.6 %collective-permute-start = (bf16[2,1,2,49,2,128]{5,4,3,2,1,0:T(2,128)(2,1)S(1)}, bf16[2,1,2,49,2,128]{5,4,3,2,1,0:T(2,128)(2,1)S(1)}, u32[]{:S(2)}, u32[]{:S(2)}) collective-permute-start(bf16[2,1,2,49,2,128]{5,4,3,2,1,0:T(2,128)(2,1)S(1)} %get-tuple-element.142), channel_id=1, source_target_pairs={{0,8},{8,16},{16,24},{24,0},{1,9},{9,17},{17,25},{25,1},{2,10},{10... | collective-permute-start | bytes 301064 | tf_op jit(solution)/shard_map/ppermute | solution.py:648
  8.2 7.5 %copy-start = (bf16[2,2,2,2,49,128]{5,3,4,2,1,0:T(2,128)(2,1)S(1)}, bf16[2,2,2,2,49,128]{5,3,4,2,1,0:T(2,128)(2,1)}, u32[]{:S(2)}) copy-start(bf16[2,2,2,2,49,128]{5,3,4,2,1,0:T(2,128)(2,1)} %param.13) | copy-start | bytes 602116
  8.2 14.0 %copy-start.2 = (bf16[2,640,640]{2,1,0:T(8,128)(2,1)S(1)}, bf16[2,640,640]{2,1,0:T(8,128)(2,1)}, u32[]{:S(2)}) copy-start(bf16[2,640,640]{2,1,0:T(8,128)(2,1)} %w2v.3) | copy-start | bytes 4915204
  8.2 14.0 %copy-start.3 = (bf16[896,896]{1,0:T(8,128)(2,1)S(1)}, bf16[896,896]{1,0:T(8,128)(2,1)}, u32[]{:S(2)}) copy-start(bf16[896,896]{1,0:T(8,128)(2,1)} %w0v.3) | copy-start | bytes 4816900
  12.3 10.0 %copy-start.1 = (bf16[2,768,768]{2,1,0:T(8,128)(2,1)S(1)}, bf16[2,768,768]{2,1,0:T(8,128)(2,1)}, u32[]{:S(2)}) copy-start(bf16[2,768,768]{2,1,0:T(8,128)(2,1)} %w1v.3) | copy-start | bytes 7077892
  12.3 9.9 %copy-start.6 = (f32[3,2,2,2,2,12]{5,4,3,2,1,0:T(2,128)S(1)}, f32[3,2,2,2,2,12]{5,4,3,2,1,0:T(2,128)}, u32[]{:S(2)}) copy-start(f32[3,2,2,2,2,12]{5,4,3,2,1,0:T(2,128)} %param.19) | copy-start | bytes 6916
  12.3 9.9 %copy-start.7 = (s32[2,2,2,2,12]{4,3,2,1,0:T(2,128)S(1)}, s32[2,2,2,2,12]{4,3,2,1,0:T(2,128)}, u32[]{:S(2)}) copy-start(s32[2,2,2,2,12]{4,3,2,1,0:T(2,128)} %param.16) | copy-start | bytes 2308
  16.9 9.2 %collective-permute-start.2 = (bf16[2,4,1,49,2,128]{5,4,3,2,1,0:T(2,128)(2,1)S(1)}, bf16[2,4,1,49,2,128]{5,4,3,2,1,0:T(2,128)(2,1)S(1)}, u32[]{:S(2)}, u32[]{:S(2)}) collective-permute-start(bf16[2,4,1,49,2,128]{5,4,3,2,1,0:T(2,128)(2,1)S(1)} %get-tuple-element.89), channel_id=1, source_target_pairs={{0,1},{1,2},{2,3},{3,4},{4,5},{5,6},{6,7},{7,0},{8,9},{9,10},{10,1... | collective-permute-start | bytes 602120 | tf_op jit(solution)/shard_map/ppermute | solution.py:648
  18.6 7.5 %collective-permute-start.3 = (bf16[2,4,1,49,2,128]{5,4,3,2,1,0:T(2,128)(2,1)S(1)}, bf16[2,4,1,49,2,128]{5,4,3,2,1,0:T(2,128)(2,1)S(1)}, u32[]{:S(2)}, u32[]{:S(2)}) collective-permute-start(bf16[2,4,1,49,2,128]{5,4,3,2,1,0:T(2,128)(2,1)S(1)} %get-tuple-element.90), channel_id=1, source_target_pairs={{1,0},{2,1},{3,2},{4,3},{5,4},{6,5},{7,6},{0,7},{9,8},{10,9},{11,1... | collective-permute-start | bytes 602120 | tf_op jit(solution)/shard_map/ppermute | solution.py:648
  21.1 12.5 %collective-permute-start.5 = (bf16[1,4,2,49,2,128]{5,4,3,2,1,0:T(2,128)(2,1)S(1)}, bf16[1,4,2,49,2,128]{5,4,3,2,1,0:T(2,128)(2,1)S(1)}, u32[]{:S(2)}, u32[]{:S(2)}) collective-permute-start(bf16[1,4,2,49,2,128]{5,4,3,2,1,0:T(2,128)(2,1)S(1)} %get-tuple-element.133), channel_id=1, source_target_pairs={{32,0},{64,32},{96,64},{128,96},{160,128},{192,160},{224,192},{0,2... | collective-permute-start | bytes 602120 | tf_op jit(solution)/shard_map/ppermute | solution.py:648
  22.2 14.4 %collective-permute-start.4 = (bf16[1,4,2,49,2,128]{5,4,3,2,1,0:T(2,128)(2,1)S(1)}, bf16[1,4,2,49,2,128]{5,4,3,2,1,0:T(2,128)(2,1)S(1)}, u32[]{:S(2)}, u32[]{:S(2)}) collective-permute-start(bf16[1,4,2,49,2,128]{5,4,3,2,1,0:T(2,128)(2,1)S(1)} %get-tuple-element.134), channel_id=1, source_target_pairs={{0,32},{32,64},{64,96},{96,128},{128,160},{160,192},{192,224},{224... | collective-permute-start | bytes 602120 | tf_op jit(solution)/shard_map/ppermute | solution.py:648
  26.1 3.9 %copy-start.8 = (s32[2,2,2]{2,1,0:T(2,128)S(1)}, s32[2,2,2]{2,1,0:T(2,128)}, u32[]{:S(2)}) copy-start(s32[2,2,2]{2,1,0:T(2,128)} %counts_ref.3) | copy-start | bytes 100
  27.0 9.6 %collective-permute-start.6 = (bf16[2,4,1,49,2,128]{5,4,3,2,1,0:T(2,128)(2,1)S(1)}, bf16[2,4,1,49,2,128]{5,4,3,2,1,0:T(2,128)(2,1)S(1)}, u32[]{:S(2)}, u32[]{:S(2)}) collective-permute-start(bf16[2,4,1,49,2,128]{5,4,3,2,1,0:T(2,128)(2,1)S(1)} %pad_maximum_fusion.1), channel_id=1, source_target_pairs={{0,32},{32,64},{64,96},{96,128},{128,160},{160,192},{192,224},{224... | collective-permute-start | bytes 602120 | tf_op jit(solution)/shard_map/ppermute | solution.py:648
  27.5 9.1 %collective-permute-start.7 = (bf16[2,4,1,49,2,128]{5,4,3,2,1,0:T(2,128)(2,1)S(1)}, bf16[2,4,1,49,2,128]{5,4,3,2,1,0:T(2,128)(2,1)S(1)}, u32[]{:S(2)}, u32[]{:S(2)}) collective-permute-start(bf16[2,4,1,49,2,128]{5,4,3,2,1,0:T(2,128)(2,1)S(1)} %pad_maximum_fusion.2), channel_id=1, source_target_pairs={{32,0},{64,32},{96,64},{128,96},{160,128},{192,160},{224,192},{0,2... | collective-permute-start | bytes 602120 | tf_op jit(solution)/shard_map/ppermute | solution.py:648
  30.0 6.6 %copy-start.4 = (f32[128,896]{1,0:T(8,128)S(1)}, f32[128,896]{1,0:T(8,128)}, u32[]{:S(2)}) copy-start(f32[128,896]{1,0:T(8,128)} %rout_ref.1) | copy-start | bytes 1376260
  30.0 6.6 %copy-start.5 = (f32[256,128]{1,0:T(8,128)S(1)}, f32[256,128]{1,0:T(8,128)}, u32[]{:S(2)}) copy-start(f32[256,128]{1,0:T(8,128)} %rin_ref.1) | copy-start | bytes 393220
  30.0 6.7 %copy-start.9 = (s32[64]{0:T(128)S(1)}, s32[64]{0:T(128)}, u32[]{:S(2)}) copy-start(s32[64]{0:T(128)} %constant.5.clone.base_ref) | copy-start | bytes 772
  33.6 11.5 %collective-permute-start.8 = (bf16[1664,128]{1,0:T(8,128)(2,1)S(1)}, bf16[1664,128]{1,0:T(8,128)(2,1)S(1)}, u32[]{:S(2)}, u32[]{:S(2)}) collective-permute-start(bf16[1664,128]{1,0:T(8,128)(2,1)S(1)} %get-tuple-element.106), channel_id=1, source_target_pairs={{0,32},{32,64},{64,96},{96,128},{128,160},{160,192},{192,224},{224... | collective-permute-start | bytes 1277960 | tf_op jit(solution)/shard_map/ppermute | solution.py:648
  33.6 11.5 %collective-permute-start.9 = (bf16[1664,128]{1,0:T(8,128)(2,1)S(1)}, bf16[1664,128]{1,0:T(8,128)(2,1)S(1)}, u32[]{:S(2)}, u32[]{:S(2)}) collective-permute-start(bf16[1664,128]{1,0:T(8,128)(2,1)S(1)} %get-tuple-element.107), channel_id=1, source_target_pairs={{32,0},{64,32},{96,64},{128,96},{160,128},{192,160},{224,192},{0,2... | collective-permute-start | bytes 1277960 | tf_op jit(solution)/shard_map/ppermute | solution.py:648
  42.0 7.6 %collective-permute-start.13 = (f32[8,128]{1,0:T(8,128)S(1)}, f32[8,128]{1,0:T(8,128)S(1)}, u32[]{:S(2)}, u32[]{:S(2)}) collective-permute-start(f32[8,128]{1,0:T(8,128)S(1)} %get-tuple-element.113.mine_ref), channel_id=1, source_target_pairs={{1,0},{2,1},{3,2},{4,3},{5,4},{6,5},{7,6},{0,7},{9,8},{10,9},{11,1... | collective-permute-start | bytes 12296 | tf_op jit(solution)/shard_map/ppermute | solution.py:648
  45.1 5.7 %collective-permute-start.12 = (f32[8,128]{1,0:T(8,128)S(1)}, f32[8,128]{1,0:T(8,128)S(1)}, u32[]{:S(2)}, u32[]{:S(2)}) collective-permute-start(f32[8,128]{1,0:T(8,128)S(1)} %get-tuple-element.113.mine_ref), channel_id=1, source_target_pairs={{0,1},{1,2},{2,3},{3,4},{4,5},{5,6},{6,7},{7,0},{8,9},{9,10},{10,1... | collective-permute-start | bytes 12296 | tf_op jit(solution)/shard_map/ppermute | solution.py:648
  45.3 9.9 %collective-permute-start.10 = (bf16[832,128]{1,0:T(8,128)(2,1)S(1)}, bf16[832,128]{1,0:T(8,128)(2,1)S(1)}, u32[]{:S(2)}, u32[]{:S(2)}) collective-permute-start(bf16[832,128]{1,0:T(8,128)(2,1)S(1)} %get-tuple-element.111), channel_id=1, source_target_pairs={{0,1},{1,2},{2,3},{3,4},{4,5},{5,6},{6,7},{7,0},{8,9},{9,10},{10,1... | collective-permute-start | bytes 638984 | tf_op jit(solution)/shard_map/ppermute | solution.py:648
  45.4 9.8 %collective-permute-start.11 = (bf16[832,128]{1,0:T(8,128)(2,1)S(1)}, bf16[832,128]{1,0:T(8,128)(2,1)S(1)}, u32[]{:S(2)}, u32[]{:S(2)}) collective-permute-start(bf16[832,128]{1,0:T(8,128)(2,1)S(1)} %get-tuple-element.112), channel_id=1, source_target_pairs={{1,0},{2,1},{3,2},{4,3},{5,4},{6,5},{7,6},{0,7},{9,8},{10,9},{11,1... | collective-permute-start | bytes 638984 | tf_op jit(solution)/shard_map/ppermute | solution.py:648
  50.9 1.3 %collective-permute-start.15 = (f32[8,128]{1,0:T(8,128)S(1)}, f32[8,128]{1,0:T(8,128)S(1)}, u32[]{:S(2)}, u32[]{:S(2)}) collective-permute-start(f32[8,128]{1,0:T(8,128)S(1)} %fold_force.1.force_ref), channel_id=1, source_target_pairs={{32,0},{64,32},{96,64},{128,96},{160,128},{192,160},{224,192},{0,2... | collective-permute-start | bytes 12296 | tf_op jit(solution)/shard_map/ppermute | solution.py:648
  50.9 4.2 %collective-permute-start.14 = (f32[8,128]{1,0:T(8,128)S(1)}, f32[8,128]{1,0:T(8,128)S(1)}, u32[]{:S(2)}, u32[]{:S(2)}) collective-permute-start(f32[8,128]{1,0:T(8,128)S(1)} %fold_force.1.force_ref), channel_id=1, source_target_pairs={{0,32},{32,64},{64,96},{96,128},{128,160},{160,192},{192,224},{224... | collective-permute-start | bytes 12296 | tf_op jit(solution)/shard_map/ppermute | solution.py:648
  55.2 8.1 %collective-permute-start.16 = (bf16[432,128]{1,0:T(8,128)(2,1)S(1)}, bf16[432,128]{1,0:T(8,128)(2,1)S(1)}, u32[]{:S(2)}, u32[]{:S(2)}) collective-permute-start(bf16[432,128]{1,0:T(8,128)(2,1)S(1)} %get-tuple-element.118), channel_id=1, source_target_pairs={{0,8},{8,16},{16,24},{24,0},{1,9},{9,17},{17,25},{25,1},{2,10},{10... | collective-permute-start | bytes 331784 | tf_op jit(solution)/shard_map/ppermute | solution.py:648
  55.3 8.0 %collective-permute-start.17 = (bf16[432,128]{1,0:T(8,128)(2,1)S(1)}, bf16[432,128]{1,0:T(8,128)(2,1)S(1)}, u32[]{:S(2)}, u32[]{:S(2)}) collective-permute-start(bf16[432,128]{1,0:T(8,128)(2,1)S(1)} %get-tuple-element.119), channel_id=1, source_target_pairs={{8,0},{16,8},{24,16},{0,24},{9,1},{17,9},{25,17},{1,25},{10,2},{18... | collective-permute-start | bytes 331784 | tf_op jit(solution)/shard_map/ppermute | solution.py:648
